TPU v7x, 32 devices: a whole 2x2x4 slice. The times are simulated.
32 devices in a mesh: rep: 2 (over x), dp: 1, tensor: 16 (over z, y, core).
Axes of the slice: x: 2, y: 2, z: 4, core: 2. Of those that a mesh axis runs over, the one named last changes fastest.
Arguments:
- hidden: bfloat16 [1024, 8192], P(('rep', 'dp', 'tensor')), parts along dimension 0, may hold values from -6 to 6
- pre_gain: bfloat16 [8192], replicated, may hold values from 0.099609375 to 1.8984375
- in_x: bfloat16 [8192, 8192], P(('dp', 'tensor')), may hold values from -0.0625 to 0.0625
- in_z: bfloat16 [8192, 8192], P(('dp', 'tensor')), may hold values from -0.2 to 0.2
- conv_x: bfloat16 [8192, 4], P(('dp', 'tensor')), may hold values from -3 to 3
- conv_bc: bfloat16 [1024, 4], replicated, may hold values from -3 to 3
- bc_weight: bfloat16 [1024, 8192], P('tensor'), may hold values from -0.0625 to 0.0625
- dt_weight: bfloat16 [128, 8192], P(('dp', 'tensor')), may hold values from -0.0625 to 0.0625
- dt_bias: bfloat16 [128], P(('dp', 'tensor')), may hold values from -3 to 0.5
- decay_rate: bfloat16 [128], P(('dp', 'tensor')), may hold values from 0.0049743652 to 2
- skip: bfloat16 [128], P(('dp', 'tensor')), may hold values from 0.29882812 to 1.5
- norm_gain: bfloat16 [8192], P(('dp', 'tensor')), may hold values from 0.099609375 to 1.8984375
- out_weight: bfloat16 [8192, 8192], P(('dp', 'tensor')), may hold values from -0.0625 to 0.0625
- segment_ids: int32 [2, 512], P(('rep', 'dp')), parts along dimension 0, may hold values from 0 to 7, never falling along the last dimension, each value on 1 to 256 neighbouring positions
- destination: int32 [1024, 1], P(('rep', 'dp', 'tensor')), parts along dimension 0, may hold values from 0 to 15; in each aligned block of 32 rows (0 to 31, 32 to 63, ...) at most 2 rows name the same one
Outputs:
- layer_out: bfloat16 [1024, 8192], P(('rep', 'dp', 'tensor')), parts along dimension 0
- packed: bfloat16 [1024, 16384], P(('rep', 'dp', 'tensor')), parts along dimension 0
There are 2 independent parts, one for each index of `rep`. A program takes and returns all parts, laid end to end along the dimension named above; an argument that names none is the same for every part. Nothing has to cross between parts.
Inputs may be any that keep to these rules, and one draw needn't show every extreme that they name: `destination`: among the 32 rows of one device no trainer shard is named more than 2 times, a bound that some block reaches. `segment_ids`: each row of 512 positions holds 8 sequences numbered 0 to 7 in order, each 1 to 256 positions long.
All inputs are finite; a program needn't handle non-finite values.
Results may differ from a plain program's by a relative error of at most 0.014.
Values may be sent and summed in bfloat16 or wider, within the bound.
No kernel may reach another device: no remote copies, remote signals or barrier semaphores. Data moves between devices by JAX's collectives and lax.ppermute only.
A program may use at most 128 MiB of HBM per device.

v0:
```python
import jax
import jax.numpy as jnp
from jax import lax
from jax.sharding import PartitionSpec as P

HEAD_DIM = 64
INNER = 8192
HEADS = 128
STATE = 128
GROUPS = 4
BLOCK = 128
CAP = 2


highest = lax.Precision.HIGHEST


def dot_rows(left, right):
    return lax.dot_general(
        left, right, (((1,), (1,)), ((), ())), preferred_element_type=jnp.float32
    )


def rms_rows(values, scale):
    wide = values.astype(jnp.float32)
    meansq = jnp.mean(wide * wide, axis=-1, keepdims=True)
    return (wide * lax.rsqrt(meansq + 1e-05) * scale.astype(jnp.float32)).astype(jnp.bfloat16)


def causal_conv(signal, kernel, segment):
    length = signal.shape[0]
    taps_count = kernel.shape[1]
    result = jnp.zeros(signal.shape, jnp.float32)
    for offset in range(taps_count):
        steps_back = taps_count - 1 - offset
        shifted = jnp.pad(signal, ((steps_back, 0), (0, 0)))[:length]
        shifted_seg = jnp.pad(segment, (steps_back, 0), constant_values=-1)[:length]
        same = (shifted_seg == segment).astype(jnp.float32)
        result = result + shifted * kernel[:, offset][None, :] * same[:, None]
    return result


def state_scan(inputs, deltas, rates, keys_b, queries_c, skips, segment):
    total, heads_n, dim_p = inputs.shape
    count = total // BLOCK
    order = jnp.arange(BLOCK)

    def advance(carry, block):
        state, previous = carry
        block_x, block_dt, block_b, block_c, block_seg = block
        cumul = jnp.cumsum(-rates[None, :] * block_dt, axis=0)
        allowed = (block_seg[:, None] == block_seg[None, :]) & (order[:, None] >= order[None, :])
        gaps = cumul[:, None, :] - cumul[None, :, :]
        decays = jnp.where(
            allowed[:, :, None], jnp.exp(jnp.where(allowed[:, :, None], gaps, 0.0)), 0.0
        )
        scores = jnp.einsum("ihn,jhn->ijh", block_c, block_b, precision=highest)
        mixing = scores * decays * block_dt[None, :, :]
        output = jnp.einsum("ijh,jhp->ihp", mixing, block_x, precision=highest)
        carried = (block_seg == previous).astype(jnp.float32)
        from_state = jnp.einsum("ihn,hpn->ihp", block_c, state, precision=highest)
        output = output + (carried[:, None] * jnp.exp(cumul))[:, :, None] * from_state
        output = output + skips[None, :, None] * block_x
        final_seg = block_seg[BLOCK - 1]
        ending = (block_seg == final_seg).astype(jnp.float32)
        weights_end = jnp.exp(cumul[BLOCK - 1][None, :] - cumul) * block_dt * ending[:, None]
        keeping = (previous == final_seg).astype(jnp.float32)
        fresh = jnp.einsum("jh,jhp,jhn->hpn", weights_end, block_x, block_b, precision=highest)
        state = keeping * jnp.exp(cumul[BLOCK - 1])[:, None, None] * state + fresh
        return ((state, final_seg), output)

    blocks = (
        inputs.reshape(count, BLOCK, heads_n, dim_p),
        deltas.reshape(count, BLOCK, heads_n),
        keys_b.reshape(count, BLOCK, heads_n, -1),
        queries_c.reshape(count, BLOCK, heads_n, -1),
        segment.reshape(count, BLOCK),
    )
    start = (jnp.zeros((heads_n, dim_p, keys_b.shape[-1]), jnp.float32), jnp.array(-1, jnp.int32))
    carry_end, outputs = lax.scan(advance, start, blocks)
    return outputs.reshape(total, heads_n, dim_p)


def mixer_core(tokens, segment, params, head_ids, ssm_raw, conv_bc):
    proj_x, proj_z, taps_x, proj_dt, bias_dt, rates, skips = params
    row_total = tokens.shape[0]
    heads_here = head_ids.shape[0]
    width_bc = GROUPS * STATE
    x_raw = dot_rows(tokens, proj_x).astype(jnp.bfloat16)
    z_raw = dot_rows(tokens, proj_z).astype(jnp.bfloat16)
    dt_raw = dot_rows(tokens, proj_dt).astype(jnp.bfloat16)
    x_act = jax.nn.silu(causal_conv(x_raw.astype(jnp.float32), taps_x.astype(jnp.float32), segment))
    ssm_act = jax.nn.silu(
        causal_conv(ssm_raw.astype(jnp.float32), conv_bc.astype(jnp.float32), segment)
    )
    b_groups = ssm_act[:, :width_bc].reshape(row_total, GROUPS, STATE)
    c_groups = ssm_act[:, width_bc:].reshape(row_total, GROUPS, STATE)
    select = (head_ids[:, None] // (HEADS // GROUPS) == jnp.arange(GROUPS)[None, :]).astype(
        jnp.float32
    )
    b_heads = jnp.einsum("tgn,hg->thn", b_groups, select, precision=highest)
    c_heads = jnp.einsum("tgn,hg->thn", c_groups, select, precision=highest)
    delta = jax.nn.softplus(dt_raw.astype(jnp.float32) + bias_dt.astype(jnp.float32)[None, :])
    scanned = state_scan(
        x_act.reshape(row_total, heads_here, HEAD_DIM),
        delta,
        rates.astype(jnp.float32),
        b_heads,
        c_heads,
        skips.astype(jnp.float32),
        segment,
    )
    return scanned.reshape(row_total, -1) * jax.nn.silu(z_raw.astype(jnp.float32))


def on_device(
    hidden,
    pre_gain,
    in_x,
    in_z,
    conv_x,
    conv_bc,
    bc_weight,
    dt_weight,
    dt_bias,
    decay_rate,
    skip,
    norm_gain,
    out_weight,
    segment_ids,
    destination,
):
    tensor_count = lax.axis_size("tensor")
    group_count = lax.axis_size("dp")
    shard_count = tensor_count * group_count
    tensor_pos = lax.axis_index("tensor")
    heads_each = in_x.shape[0] // HEAD_DIM
    target = destination[:, 0]
    onehot = (target[:, None] == jnp.arange(shard_count, dtype=jnp.int32)[None, :]).astype(
        jnp.int32
    )
    ranks = jnp.sum((jnp.cumsum(onehot, axis=0) - onehot) * onehot, axis=1)
    slot_ids = target * CAP + ranks
    normed = rms_rows(hidden, pre_gain)
    tokens = lax.all_gather(normed, "tensor", axis=0, tiled=True)
    segment = segment_ids.reshape(-1)
    gathered = (
        lax.all_gather(in_x, "dp", axis=0, tiled=True),
        lax.all_gather(in_z, "dp", axis=0, tiled=True),
        lax.all_gather(conv_x, "dp", axis=0, tiled=True),
        lax.all_gather(dt_weight, "dp", axis=0, tiled=True),
        lax.all_gather(dt_bias, "dp", axis=0, tiled=True),
        lax.all_gather(decay_rate, "dp", axis=0, tiled=True),
        lax.all_gather(skip, "dp", axis=0, tiled=True),
        lax.all_gather(norm_gain, "dp", axis=0, tiled=True),
        lax.all_gather(out_weight, "dp", axis=0, tiled=True),
    )
    params = gathered[:7]
    gain_here = gathered[7]
    proj_out = gathered[8]
    head_ids = jnp.concatenate(
        [
            (member * tensor_count + tensor_pos) * heads_each + jnp.arange(heads_each)
            for member in range(group_count)
        ]
    )
    ssm_part = dot_rows(tokens, bc_weight).astype(jnp.bfloat16)
    ssm_raw = lax.all_gather(ssm_part, "tensor", axis=1, tiled=True)
    gated = mixer_core(tokens, segment, params, head_ids, ssm_raw, conv_bc)
    row_total = gated.shape[0]
    heads_here = head_ids.shape[0]
    group_sel = (head_ids[:, None] // (HEADS // GROUPS) == jnp.arange(GROUPS)[None, :]).astype(
        jnp.float32
    )
    by_head = gated.reshape(row_total, heads_here, HEAD_DIM)
    head_sq = jnp.sum(by_head * by_head, axis=2)
    partial_sq = jnp.dot(head_sq, group_sel, precision=highest)
    total_sq = lax.psum(partial_sq, "tensor")
    head_total = jnp.dot(total_sq, group_sel.T, precision=highest)
    head_scale = lax.rsqrt(head_total / (INNER // GROUPS) + 1e-05)
    scaled = (by_head * head_scale[:, :, None]).reshape(row_total, -1)
    inner = (scaled * gain_here.astype(jnp.float32)[None, :]).astype(jnp.bfloat16)
    mixer = lax.psum_scatter(
        jnp.dot(inner, proj_out, preferred_element_type=jnp.float32),
        "tensor",
        scatter_dimension=0,
        tiled=True,
    )
    layer_out = (hidden.astype(jnp.float32) + mixer).astype(jnp.bfloat16)
    joined = jnp.concatenate([hidden, layer_out], axis=1)
    filled = jnp.zeros((shard_count * CAP, joined.shape[1]), jnp.bfloat16).at[slot_ids].set(joined)
    received = lax.all_to_all(
        filled.reshape(shard_count, CAP, joined.shape[1]),
        ("dp", "tensor"),
        split_axis=0,
        concat_axis=0,
        tiled=True,
    )
    packed = received.reshape(shard_count * CAP, -1)
    return (layer_out, packed)


def solution(mesh):
    return jax.shard_map(
        on_device,
        mesh=mesh,
        in_specs=(
            P(("rep", "dp", "tensor"), None),
            P(),
            P(("dp", "tensor"), None),
            P(("dp", "tensor"), None),
            P(("dp", "tensor"), None),
            P(),
            P("tensor", None),
            P(("dp", "tensor"), None),
            P(("dp", "tensor")),
            P(("dp", "tensor")),
            P(("dp", "tensor")),
            P(("dp", "tensor")),
            P(("dp", "tensor"), None),
            P(("rep", "dp"), None),
            P(("rep", "dp", "tensor"), None),
        ),
        out_specs=(P(("rep", "dp", "tensor"), None), P(("rep", "dp", "tensor"), None)),
        check_vma=False,
    )
```

profile of v0, /device:TPU:0, one launch (start us, length us, event | category | flops | bytes accessed | tf_op | source)
XLA Modules:
  0.0 455.1 jit_solution(12654728499599176260)
XLA Ops:
  9.4 2.0 fusion.50
  11.7 77.4 %all-gather.3.cloned.1.call-done = bf16[512,8192]{1,0:T(8,128)(2,1)} async-done(((bf16[32,8192]{1,0:T(8,128)(2,1)}), bf16[512,8192]{1,0:T(8,128)(2,1)}) %all-gather.3.cloned.1.call-update) | async-done | bytes 8388624 | tf_op jit(solution)/shard_map/all_gather | solution.py:145
  89.2 6.7 %convolution_convert_fusion.2 = bf16[512,64]{0,1:T(8,128)(2,1)} fusion(bf16[512,8192]{1,0:T(8,128)(2,1)} %all-gather.3.cloned.1.call-done, bf16[64,8192]{1,0:T(8,128)(2,1)S(1)} %copy-done), kind=kOutput, calls=%fused_computation.62 | convolution fusion | flops 536903680 | bytes 9502720 | tf_op jit(solution)/shard_map/dot_general | solution.py:19
  96.1 9.5 %fusion.30 = f32[512,512]{1,0:T(8,128)S(1)} fusion(bf16[512,8192]{1,0:T(8,128)(2,1)} %all-gather.3.cloned.1.call-done, bf16[512,8192]{1,0:T(8,128)(2,1)} %param.19), kind=kOutput, calls=%fused_computation.61 | convolution fusion | flops 4295491584 | bytes 17825792 | tf_op jit(solution)/shard_map/dot_general | solution.py:19
  107.4 5.7 %fusion.59 = f32[4,128,8]{1,2,0:T(8,128)S(1)} fusion(bf16[512,8192]{1,0:T(8,128)(2,1)} %all-gather.3.cloned.1.call-done, bf16[8,8192]{1,0:T(8,128)(2,1)} %param.24, f32[8]{0:T(128)S(1)} %convert_element_type.120), kind=kOutput, calls=%fused_computation.100 | convolution fusion | flops 67145728 | bytes 8536096 | tf_op jit(solution)/shard_map/dot_general | solution.py:19
  113.1 19.1 %all-gather.5.cloned.1.call-done = bf16[512,1024]{0,1:T(8,128)(2,1)} async-done(((bf16[512,64]{0,1:T(8,128)(2,1)}), bf16[512,1024]{0,1:T(8,128)(2,1)}) %all-gather.5.cloned.1.call-update) | async-done | bytes 1048592 | tf_op jit(solution)/shard_map/all_gather | solution.py:168
  132.2 1.5 convert_element_type.128
  133.7 2.6 divide_multiply_fusion
  138.0 1.6 copy.56
  139.6 2.7 fusion.71
  142.2 2.6 fusion.69
  144.9 34.5 %while.17 = (s32[]{:T(128)}, f32[8,64,128]{2,1,0:T(8,128)S(1)}, s32[]{:T(128)}, f32[4,128,8,64]{1,3,2,0:T(8,128)}, s32[4,128]{1,0:T(4,128)S(1)}, /*index=5*/f32[...) while((s32[]{:T(128)}, f32[8,64,128]{2,1,0:T(8,128)S(1)}, ...), condition=%wide.region_3.4_spmd.clone, body=%wide.region_1.3_spmd.clone.sunk | while | flops 504746496 | bytes 7739794 | solution.py:80
  150.3 1.3 fusion.112
  159.0 1.3 fusion.112
  167.6 1.3 fusion.112
  176.2 1.3 fusion.112
  179.4 1.9 copy.70
  181.8 11.2 %fusion.81 = (f32[512,512]{1,0:T(8,128)S(1)}, f32[512,512]{1,0:T(8,128)S(1)}) fusion(f32[512,512]{1,0:T(8,128)S(1)} %reshape.231, bf16[512,8192]{1,0:T(8,128)(2,1)} %all-gather.3.cloned.1.call-done, bf16[512,8192]{1,0:T(8,128)(2,1)} %param.20), kind=kOutput, calls=%fused_computation.134 | convolution fusion | flops 4297064448 | bytes 19922944 | tf_op jit(solution)/shard_map/dot_general | solution.py:19
  193.7 32.1 %psum.7 = f32[512,4]{0,1:T(4,128)S(1)} all-reduce(f32[512,4]{0,1:T(4,128)S(1)} %fusion.64), channel_id=1, replica_groups=mesh['rep'=2,'dp'=1,'tensor'=16] {'tensor'}, use_global_device_ids=true, to_apply=%region_5.6 | all-reduce | flops 2048 | bytes 16384 | tf_op jit(solution)/shard_map/psum | solution.py:178
  226.4 11.5 %fusion.56 = f32[512,8192]{1,0:T(8,128)} fusion(bf16[512,8192]{1,0:T(8,128)(2,1)} %param.29, f32[512,512]{1,0:T(8,128)S(1)} %get-tuple-element.254, f32[512,512]{1,0:T(8,128)S(1)} %copy.65, f32[512]{0:T(512)S(1)} %convert_element_type.133), kind=kOutput, calls=%fused_computation.96 | convolution fusion | flops 4295753728 | bytes 27265024 | tf_op jit(solution)/shard_map/dot_general | solution.py:184
  238.9 175.0 %reduce-scatter.2.cloned.1.call-done = f32[32,8192]{1,0:T(8,128)} async-done(((f32[512,8192]{1,0:T(8,128)}), f32[32,8192]{1,0:T(8,128)}) %reduce-scatter.2.cloned.1.call-update) | async-done | bytes 1048592 | tf_op jit(solution)/shard_map/reduce_scatter | solution.py:183
  413.9 1.3 fusion.51
  416.0 2.3 scatter_custom_fusion
  419.0 28.4 %all_to_all.5 = bf16[16,2,16384]{2,1,0:T(2,128)(2,1)S(1)} all-to-all(bf16[16,2,16384]{2,1,0:T(2,128)(2,1)S(1)} %reshape.219), channel_id=1, replica_groups=mesh['rep'=2,'dp'=1,'tensor'=16] {'dp','tensor'}, dimensions={0} | all-to-all | bytes 2097152 | tf_op jit(solution)/shard_map/all_to_all | solution.py:192
  (137 shorter events, 35.8 us)
Async XLA Ops:
  7.2 82.0 %copy-start = (bf16[64,8192]{1,0:T(8,128)(2,1)S(1)}, bf16[64,8192]{1,0:T(8,128)(2,1)}, u32[]{:S(2)}) copy-start(bf16[64,8192]{1,0:T(8,128)(2,1)} %param.23) | copy-start | bytes 3145732
  7.2 4.3 copy-start.9
  7.2 4.3 copy-start.10
  7.2 4.3 copy-start.8
  7.2 4.4 copy-start.11
  7.2 4.4 copy-start.6
  7.2 4.5 copy-start.5
  7.2 4.5 copy-start.4
  7.3 81.9 %all-gather.3.cloned.1.call-start = ((), (), s32[]{:S(2)}) async-start(), calls=%async_computation.2 | async-start | bytes 8912896 | tf_op jit(solution)/shard_map/all_gather | solution.py:145
  11.4 120.8 %all-gather.5.cloned.1.call-start = ((), (), s32[]{:S(2)}) async-start(), calls=%async_computation.3 | async-start | bytes 1114112 | tf_op jit(solution)/shard_map/all_gather | solution.py:168
  95.9 318.0 %reduce-scatter.2.cloned.1.call-start = ((), (), s32[]{:S(2)}) async-start(), calls=%async_computation.4 | async-start | bytes 17825792 | tf_op jit(solution)/shard_map/reduce_scatter | solution.py:183
  237.9 0.7 copy-start.7
  237.9 176.0 %copy-start.2 = (bf16[32,8192]{1,0:T(8,128)(2,1)S(1)}, bf16[32,8192]{1,0:T(8,128)(2,1)}, u32[]{:S(2)}) copy-start(bf16[32,8192]{1,0:T(8,128)(2,1)} %param.17) | copy-start | bytes 1572868
  415.2 0.8 copy-start.3
  418.2 30.3 %copy-start.1 = (bf16[64,8192]{1,0:T(8,128)(2,1)S(1)}, bf16[64,8192]{1,0:T(8,128)(2,1)}, u32[]{:S(2)}) copy-start(bf16[64,8192]{1,0:T(8,128)(2,1)} %param.23) | copy-start | bytes 3145732
Sparse Core Ops, SparseCore 0:
  11.5 77.5 all-gather.2
  96.0 36.1 all-gather.4
  238.1 175.7 reduce-scatter.1
where the time goes:
time: 456 us; the launch traced here: 455 us
  waiting for transfers between devices  272 us (60%)
  matrix products  67.8 us (15%)
  blocking collectives  60.5 us (13%)
  local copies, waits for them, and re-layouts  19.2 us (4%)
  other arithmetic  16.9 us (4%)
  between operations  14.1 us (3%)
  loops' own time  4.83 us (1%)
    reduce_scatter x1, waiting for transfers between devices, on_device(): lax.psum_scatter(jnp.dot(inner, proj_out, preferred_element_type=jnp.floa...  175 us
    all_gather x1, waiting for transfers between devices, on_device(): tokens = lax.all_gather(normed, 'tensor', axis=0, tiled=True)  77.4 us
    dot_general x4, matrix products, dot_rows(): lax.dot_general(left, right, (((1,), (1,)), ((), ())), preferred_element_...  33.1 us
    psum x1, blocking collectives, on_device(): total_sq = lax.psum(partial_sq, 'tensor')  32.1 us
    all_to_all x1, blocking collectives, on_device(): lax.all_to_all(filled.reshape(shard_count, CAP, joined.shape[1]), ('dp',...  28.4 us
    all_gather x1, waiting for transfers between devices, on_device(): ssm_raw = lax.all_gather(ssm_part, 'tensor', axis=1, tiled=True)  19.1 us
    dot_general x1, matrix products, on_device(): jnp.dot(inner, proj_out, preferred_element_type=jnp.float32)  11.5 us
  transfers between devices with their start and end apart: 3, of which 3 were waited for; matrix products, arithmetic and copies ran while one was open for 4% of the time, Pallas kernels for 0%

commit v1 on v0

--- a/solution.py
+++ b/solution.py
@@ -1,6 +1,10 @@
+import functools
+
 import jax
 import jax.numpy as jnp
 from jax import lax
+from jax.experimental import pallas as pl
+from jax.experimental.pallas import tpu as pltpu
 from jax.sharding import PartitionSpec as P
 
 HEAD_DIM = 64
@@ -200,9 +204,516 @@
     return (layer_out, packed)
 
 
+PLANE = 4
+VMEM_LIMIT = 56 * 1024 * 1024
+NEG = -1e30
+
+
+def vmem():
+    return pl.BlockSpec(memory_space=pltpu.VMEM)
+
+
+def smem():
+    return pl.BlockSpec(memory_space=pltpu.SMEM)
+
+
+def dot_nt(left, right, precision=None):
+    return lax.dot_general(
+        left, right, (((1,), (1,)), ((), ())), precision=precision, preferred_element_type=jnp.float32
+    )
+
+
+def norm_kernel(spot_ref, b0, b1, b2, b3, gain_ref, small_ref, normed_ref, bc_ref, dt_ref):
+    rows, width = b0.shape[0], gain_ref.shape[1]
+    step = 1024
+    for index, block in enumerate((b0, b1, b2, b3)):
+        start = pl.multiple_of((spot_ref[0] ^ index) * rows, rows)
+        total = jnp.zeros((rows, 128), jnp.float32)
+        for col in range(0, width, step):
+            wide = block[:, col : col + step].astype(jnp.float32)
+            square = wide * wide
+            for lane in range(0, step, 128):
+                total = total + square[:, lane : lane + 128]
+        scale = lax.rsqrt(jnp.sum(total, axis=1, keepdims=True) / width + 1e-05)
+        for col in range(0, width, step):
+            wide = block[:, col : col + step].astype(jnp.float32)
+            normed_ref[pl.ds(start, rows), col : col + step] = (
+                wide * scale * gain_ref[:, col : col + step].astype(jnp.float32)
+            ).astype(jnp.bfloat16)
+    result = dot_nt(normed_ref[...], small_ref[...]).astype(jnp.bfloat16)
+    half = bc_ref.shape[1]
+    bc_ref[...] = result[:, :half]
+    dt_ref[...] = result[:, half:].astype(jnp.float32)
+
+
+def norm_plane(spot, blocks, gain, small):
+    rows, width = blocks[0].shape[0] * PLANE, gain.shape[1]
+    return pl.pallas_call(
+        norm_kernel,
+        out_shape=(
+            jax.ShapeDtypeStruct((rows, width), jnp.bfloat16),
+            jax.ShapeDtypeStruct((rows, small.shape[0] - 128), jnp.bfloat16),
+            jax.ShapeDtypeStruct((rows, 128), jnp.float32),
+        ),
+        in_specs=[smem()] + [vmem()] * 6,
+        out_specs=(vmem(), vmem(), vmem()),
+        compiler_params=pltpu.CompilerParams(vmem_limit_bytes=VMEM_LIMIT),
+        cost_estimate=pl.CostEstimate(
+            flops=2 * rows * width * small.shape[0], bytes_accessed=8 << 20, transcendentals=0
+        ),
+        name="norm_plane",
+    )(spot, *blocks, gain, small)
+
+
+def project_kernel(normed_ref, wx_ref, wz_ref, x_ref, z_ref):
+    x_ref[...] = dot_nt(normed_ref[...], wx_ref[...]).astype(jnp.bfloat16)
+    z_ref[...] = dot_nt(normed_ref[...], wz_ref[...]).astype(jnp.bfloat16)
+
+
+def project_plane(normed, in_x, in_z):
+    rows, width = normed.shape
+    cols = in_x.shape[0]
+    tile = 128
+    return pl.pallas_call(
+        project_kernel,
+        grid=(cols // tile,),
+        out_shape=(jax.ShapeDtypeStruct((rows, cols), jnp.bfloat16),) * 2,
+        in_specs=[
+            pl.BlockSpec((rows, width), lambda i: (0, 0)),
+            pl.BlockSpec((tile, width), lambda i: (i, 0)),
+            pl.BlockSpec((tile, width), lambda i: (i, 0)),
+        ],
+        out_specs=(pl.BlockSpec((rows, tile), lambda i: (0, i)),) * 2,
+        compiler_params=pltpu.CompilerParams(vmem_limit_bytes=VMEM_LIMIT),
+        cost_estimate=pl.CostEstimate(
+            flops=4 * rows * width * cols, bytes_accessed=20 << 20, transcendentals=0
+        ),
+        name="project_plane",
+    )(normed, in_x, in_z)
+
+
+def silu(value):
+    return value / (1.0 + jnp.exp(-value))
+
+
+def scan_kernel(
+    spot_ref,
+    *refs,
+    heads,
+    planes,
+):
+    xs, zs, dts = refs[:planes], refs[planes : 2 * planes], refs[2 * planes : 3 * planes]
+    refs = refs[3 * planes :]
+    early, late = refs[:4], refs[4:8]
+    (taps_x, taps_bc, masks, bias, marks, keep, head_rows, expand, skip_ref, gain_ref) = refs[8:18]
+    gated_ref, square_ref = refs[18:20]
+    x_all, z_all, dt_all, bc_all = refs[20:]
+    z_pos, spot = spot_ref[0], spot_ref[1]
+    rows = xs[0].shape[0]
+    chans = xs[0].shape[1]
+    highest_ = lax.Precision.HIGHEST
+    bit0, bit1 = (spot & 1) == 1, (spot & 2) == 2
+    x_all[0:8, :] = jnp.zeros((8, chans), jnp.float32)
+    bc_all[0:8, :] = jnp.zeros((8, 2 * STATE), jnp.float32)
+    for s in range(planes):
+        at = pl.multiple_of(lax.rem(z_pos - s + planes, planes) * rows, rows)
+        x_all[pl.ds(at + 8, rows), :] = xs[s][...].astype(jnp.float32)
+        z_all[pl.ds(at, rows), :] = zs[s][...]
+        dt_all[pl.ds(at, rows), :] = dts[s][...]
+        if s < planes - 1:
+            got = [ref[s * rows : (s + 1) * rows, :].astype(jnp.float32) for ref in early]
+        else:
+            got = [ref[...].astype(jnp.float32) for ref in late]
+        a0, a1 = jnp.where(bit0, got[1], got[0]), jnp.where(bit0, got[0], got[1])
+        a2, a3 = jnp.where(bit0, got[3], got[2]), jnp.where(bit0, got[2], got[3])
+        p0, p2 = jnp.where(bit1, a2, a0), jnp.where(bit1, a0, a2)
+        p1, p3 = jnp.where(bit1, a3, a1), jnp.where(bit1, a1, a3)
+        for chip, first, pair in ((z_pos, 0, (p0, p1)), (z_pos + GROUPS, STATE, (p2, p3))):
+            row = lax.rem(lax.div(chip, PLANE // 2) - s + planes, planes) * rows
+            row = pl.multiple_of(row, rows)
+            bc_all[pl.ds(row + 8, rows), first : first + STATE] = jnp.concatenate(pair, axis=1)
+    order_i = lax.broadcasted_iota(jnp.int32, (rows, rows), 0)
+    order_j = lax.broadcasted_iota(jnp.int32, (rows, rows), 1)
+    tri = (order_i >= order_j).astype(jnp.float32)
+    lane = lax.broadcasted_iota(jnp.int32, (rows, 128), 1)
+    real = lane < heads
+    low = lane < HEAD_DIM
+    bias_dt, rates = head_rows[0:1, :], head_rows[1:2, :]
+    lanes_x, lanes_bc = chans // 128, 2 * STATE // 128
+
+    def conv(source, taps, base, count):
+        last = taps.shape[0] - 1
+        total = source[base + 8 : base + 8 + rows, :] * taps[last : last + 1, :]
+        for back in range(1, last + 1):
+            same = jnp.concatenate([masks[back - 1, base : base + rows, :]] * count, axis=1)
+            total = total + (
+                source[base + 8 - back : base + 8 - back + rows, :]
+                * taps[last - back : last - back + 1, :]
+                * same
+            )
+        return silu(total)
+
+    state = jnp.zeros((STATE, chans), jnp.float32)
+    for p in range(planes):
+        base = p * rows
+        span = slice(base, base + rows)
+        x_act = conv(x_all, taps_x, base, lanes_x)
+        bc_act = conv(bc_all, taps_bc, base, lanes_bc).astype(jnp.bfloat16)
+        keys, queries = bc_act[:, :STATE], bc_act[:, STATE:]
+        raw = dt_all[span, :] + bias_dt
+        delta = jnp.maximum(raw, 0.0) + jnp.log1p(jnp.exp(-jnp.abs(raw)))
+        delta = jnp.where(real, delta, 0.0)
+        cum = jnp.dot(tri, -rates * delta, precision=highest_, preferred_element_type=jnp.float32)
+        cum_t = cum.T
+        last = cum[rows - 1 : rows, :]
+        carried = jnp.where(real, jnp.exp(cum) * marks[0, span, :], 0.0)
+        ending = jnp.where(real, jnp.exp(last - cum) * marks[1, span, :] * delta, 0.0)
+        decay_end = jnp.where(real[0:8], jnp.exp(jnp.broadcast_to(last, (8, 128))) * keep[p : p + 1, :], 0.0)
+        spread = jnp.dot(
+            jnp.concatenate([delta, carried, ending, decay_end], axis=0),
+            expand[...],
+            precision=highest_,
+            preferred_element_type=jnp.float32,
+        )
+        delta_x = (spread[:rows] * x_act).astype(jnp.bfloat16)
+        end_x = (spread[2 * rows : 3 * rows] * x_act).astype(jnp.bfloat16)
+        scores = dot_nt(queries, keys)
+        from_state = jnp.dot(queries, state.astype(jnp.bfloat16), preferred_element_type=jnp.float32)
+        block_bias = bias[span, :]
+        outs = []
+        for pair in range(heads // 2):
+            both = delta_x[:, pair * 128 : (pair + 1) * 128]
+            part = []
+            for h in (2 * pair, 2 * pair + 1):
+                gap = cum[:, h : h + 1] - cum_t[h : h + 1, :]
+                mixing = (jnp.exp(gap + block_bias) * scores).astype(jnp.bfloat16)
+                part.append(jnp.dot(mixing, both, preferred_element_type=jnp.float32))
+            outs.append(jnp.where(low, part[0], part[1]))
+        y = jnp.concatenate(outs, axis=1)
+        y = y + spread[rows : 2 * rows] * from_state + skip_ref[...] * x_act
+        gated = y * silu(z_all[span, :].astype(jnp.float32))
+        square_ref[p : p + 1, :] = dot_nt(
+            jnp.ones((8, chans), jnp.float32), gated * gated, precision=highest_
+        )[0:1, :]
+        gated_ref[span, :] = (gated * gain_ref[...]).astype(jnp.bfloat16)
+        if p + 1 < planes:
+            fresh = lax.dot_general(
+                keys, end_x, (((0,), (0,)), ((), ())), preferred_element_type=jnp.float32
+            )
+            state = spread[3 * rows : 3 * rows + 1] * state + fresh
+
+
+def scan_all(spots, xs, zs, dts, early, late, consts, heads):
+    planes = len(xs)
+    rows, chans = xs[0].shape
+    return pl.pallas_call(
+        functools.partial(scan_kernel, heads=heads, planes=planes),
+        out_shape=(
+            jax.ShapeDtypeStruct((planes * rows, chans), jnp.bfloat16),
+            jax.ShapeDtypeStruct((8, rows), jnp.float32),
+        ),
+        in_specs=[smem()] + [vmem()] * (3 * planes + 8 + len(consts)),
+        out_specs=(vmem(), vmem()),
+        scratch_shapes=[
+            pltpu.VMEM((planes * rows + 8, chans), jnp.float32),
+            pltpu.VMEM((planes * rows, chans), jnp.bfloat16),
+            pltpu.VMEM((planes * rows, 128), jnp.float32),
+            pltpu.VMEM((planes * rows + 8, 2 * STATE), jnp.float32),
+        ],
+        compiler_params=pltpu.CompilerParams(vmem_limit_bytes=VMEM_LIMIT),
+        cost_estimate=pl.CostEstimate(flops=1 << 30, bytes_accessed=8 << 20, transcendentals=0),
+        name="scan_all",
+    )(spots, *xs, *zs, *dts, *early, *late, *consts)
+
+
+def away_kernel(at_ref, gated_ref, weight_ref, away_ref):
+    rows = away_ref.shape[0] // 2
+    left = jnp.concatenate(
+        [gated_ref[pl.ds(pl.multiple_of(at_ref[i], rows), rows), :] for i in range(2)], axis=0
+    )
+    away_ref[...] = jnp.dot(left, weight_ref[...], preferred_element_type=jnp.float32).astype(
+        jnp.bfloat16
+    )
+
+
+def home_kernel(at_ref, gated_ref, weight_ref, got_ref, send_ref, keep_ref):
+    rows = send_ref.shape[0]
+    left = jnp.concatenate(
+        [gated_ref[pl.ds(pl.multiple_of(at_ref[i], rows), rows), :] for i in range(2)], axis=0
+    )
+    total = jnp.dot(left, weight_ref[...], preferred_element_type=jnp.float32)
+    total = total + got_ref[...].astype(jnp.float32)
+    send_ref[...] = total[:rows].astype(jnp.bfloat16)
+    keep_ref[...] = total[rows:]
+
+
+def out_part(at, gated, weight, got, rows):
+    chans, width = weight.shape
+    tile = 2048
+    column = lambda i: (0, i)
+    specs = [
+        smem(),
+        pl.BlockSpec(gated.shape, lambda i: (0, 0)),
+        pl.BlockSpec((chans, tile), column),
+    ]
+    common = dict(
+        grid=(width // tile,),
+        compiler_params=pltpu.CompilerParams(vmem_limit_bytes=VMEM_LIMIT),
+        cost_estimate=pl.CostEstimate(
+            flops=4 * rows * width * chans, bytes_accessed=10 << 20, transcendentals=0
+        ),
+    )
+    if got is None:
+        return pl.pallas_call(
+            away_kernel,
+            out_shape=jax.ShapeDtypeStruct((2 * rows, width), jnp.bfloat16),
+            in_specs=specs,
+            out_specs=pl.BlockSpec((2 * rows, tile), column),
+            name="out_away",
+            **common,
+        )(at, gated, weight)
+    return pl.pallas_call(
+        home_kernel,
+        out_shape=(
+            jax.ShapeDtypeStruct((rows, width), jnp.bfloat16),
+            jax.ShapeDtypeStruct((rows, width), jnp.float32),
+        ),
+        in_specs=specs + [pl.BlockSpec((2 * rows, tile), column)],
+        out_specs=(pl.BlockSpec((rows, tile), column),) * 2,
+        name="out_home",
+        **common,
+    )(at, gated, weight, got)
+
+
+def pick_kernel(select_ref, *refs):
+    rows = jnp.concatenate([ref[...] for ref in refs[:-1]], axis=0)
+    refs[-1][...] = jnp.dot(
+        select_ref[...], rows, preferred_element_type=jnp.float32
+    ).astype(jnp.bfloat16)
+
+
+def pick_rows(select, blocks, width):
+    tile = 1024
+    rows = blocks[0].shape[0]
+    return pl.pallas_call(
+        pick_kernel,
+        grid=(width // tile,),
+        out_shape=jax.ShapeDtypeStruct((select.shape[0], width), jnp.bfloat16),
+        in_specs=[pl.BlockSpec(select.shape, lambda i: (0, 0))]
+        + [pl.BlockSpec((rows, tile), lambda i: (0, i))] * len(blocks),
+        out_specs=pl.BlockSpec((select.shape[0], tile), lambda i: (0, i)),
+        compiler_params=pltpu.CompilerParams(vmem_limit_bytes=VMEM_LIMIT),
+        cost_estimate=pl.CostEstimate(
+            flops=2 * select.shape[0] * select.shape[1] * width,
+            bytes_accessed=9 << 20,
+            transcendentals=0,
+        ),
+        name="pick_rows",
+    )(select, *blocks)
+
+
+def scan_constants(
+    segment_ids, conv_x, conv_bc, dt_bias, decay_rate, skip, norm_gain, z_pos, planes
+):
+    f32 = jnp.float32
+    heads = dt_bias.shape[0]
+    segment = segment_ids.reshape(-1)
+    total_rows = segment.shape[0]
+    plane_rows = total_rows // planes
+    position = jnp.arange(total_rows)
+    masks = jnp.stack(
+        [
+            jnp.broadcast_to(
+                ((jnp.roll(segment, back) == segment) & (position >= back)).astype(f32)[:, None],
+                (total_rows, 128),
+            )
+            for back in range(1, conv_x.shape[1])
+        ]
+    )
+    by_plane = segment.reshape(planes, plane_rows)
+    inner_order = jnp.arange(plane_rows)
+    allowed = (by_plane[:, :, None] == by_plane[:, None, :]) & (
+        inner_order[:, None] >= inner_order[None, :]
+    )
+    bias = jnp.where(allowed, 0.0, NEG).astype(f32).reshape(total_rows, plane_rows)
+    final = by_plane[:, -1]
+    previous = jnp.concatenate([jnp.full((1,), -1, final.dtype), final[:-1]])
+    marks = jnp.stack(
+        [
+            jnp.broadcast_to(value.astype(f32).reshape(-1, 1), (total_rows, 128))
+            for value in (by_plane == previous[:, None], by_plane == final[:, None])
+        ]
+    )
+    keep = jnp.broadcast_to((previous == final).astype(f32)[:, None], (planes, 128))
+    keep = jnp.pad(keep, ((0, 8 - planes), (0, 0)))
+    head_rows = jnp.pad(
+        jnp.stack([dt_bias.astype(f32), decay_rate.astype(f32)]), ((0, 6), (0, 128 - heads))
+    )
+    expand = (jnp.arange(128)[:, None] == jnp.arange(heads * HEAD_DIM)[None, :] // HEAD_DIM).astype(f32)
+    skip_row = jnp.repeat(skip.astype(f32), HEAD_DIM)[None, :]
+    out_gain = norm_gain.astype(f32)[None, :]
+    taps_x = conv_x.astype(f32).T
+    width_bc = GROUPS * STATE
+    taps_bc = jnp.concatenate(
+        [
+            lax.dynamic_slice_in_dim(conv_bc, z_pos * STATE + start, STATE, axis=0)
+            for start in (0, width_bc)
+        ],
+        axis=0,
+    ).astype(f32).T
+    return (taps_x, taps_bc, masks, bias, marks, keep, head_rows, expand, skip_row, out_gain)
+
+
+def on_device_planes(
+    hidden,
+    pre_gain,
+    in_x,
+    in_z,
+    conv_x,
+    conv_bc,
+    bc_weight,
+    dt_weight,
+    dt_bias,
+    decay_rate,
+    skip,
+    norm_gain,
+    out_weight,
+    segment_ids,
+    destination,
+):
+    count = lax.axis_size("tensor")
+    planes = count // PLANE
+    me = lax.axis_index("tensor")
+    z_pos, spot = me // PLANE, me % PLANE
+    rows, width = hidden.shape
+    plane_rows = rows * PLANE
+    heads = dt_weight.shape[0]
+    every = range(count)
+    ring = [(t, (t + PLANE) % count) for t in every]
+    over_y = [(t, t ^ 2) for t in every]
+    over_core = [(t, t ^ 1) for t in every]
+
+    def permute(value, pairs):
+        return lax.ppermute(value, "tensor", pairs)
+
+    f32 = jnp.float32
+    small = jnp.concatenate(
+        [bc_weight, jnp.zeros((0, width), bc_weight.dtype)]
+        + [dt_weight, jnp.zeros((128 - heads, width), dt_weight.dtype)],
+        axis=0,
+    )
+    gain_row = pre_gain[None, :]
+    consts = scan_constants(
+        segment_ids, conv_x, conv_bc, dt_bias, decay_rate, skip, norm_gain, z_pos, planes
+    )
+    spot_only = spot.astype(jnp.int32)[None]
+    spots = jnp.stack([z_pos, spot]).astype(jnp.int32)
+
+    target = destination[:, 0]
+    own = jnp.concatenate(
+        [hidden, jnp.broadcast_to(destination.astype(jnp.bfloat16), (rows, 128))], axis=1
+    )
+    straight, crossed = [own], []
+    straight_core, crossed_core = [], []
+    for step in range(planes):
+        moved = [permute(straight[step], over_y), permute(straight[step], over_core)]
+        if step + 1 < planes:
+            moved.append(permute(straight[step], ring))
+        if step:
+            moved.append(permute(crossed[step - 1], over_core))
+        moved = list(lax.optimization_barrier(tuple(moved)))
+        crossed.append(moved[0])
+        straight_core.append(moved[1])
+        if step + 1 < planes:
+            straight.append(moved[2])
+        if step:
+            crossed_core.append(moved[-1])
+    crossed_core.append(permute(crossed[-1], over_core))
+
+    def exchange(piece):
+        result = []
+        for turn in range(PLANE):
+            pairs = []
+            for t in every:
+                chip, side = t // 2, t % 2
+                have = (chip // GROUPS) * 2 + side
+                pairs.append((t, (chip % GROUPS) * PLANE + (have ^ turn)))
+            result.append(permute(piece, pairs))
+        return result
+
+    normed, pieces, dts = [], [], []
+    for step in range(planes):
+        blocks = [straight[step], straight_core[step], crossed[step], crossed_core[step]]
+        n, b, d = norm_plane(spot_only, blocks, gain_row, small)
+        normed.append(n)
+        pieces.append(b)
+        dts.append(d)
+    early = exchange(jnp.concatenate(pieces[:-1], axis=0))
+    late = exchange(pieces[-1])
+    xs, zs = [], []
+    for step in range(planes):
+        x, z = project_plane(normed[step], in_x, in_z)
+        xs.append(x)
+        zs.append(z)
+    gated, squares = scan_all(spots, xs, zs, dts, early, late, consts, heads)
+
+    squares = squares + permute(squares, over_core)
+    squares = squares + permute(squares, over_y)
+    scale = lax.rsqrt(squares[:planes].reshape(-1) / (INNER // GROUPS) + 1e-05)
+
+    travelling = None
+    for step in range(planes):
+        plane = (z_pos - 1 - step) % planes
+        side, level = spot % 2, spot // 2
+
+        def rows_at(level_, side_):
+            return ((plane * 2 + level_) * 2 + side_) * rows
+
+        away_at = jnp.stack([rows_at(1 - level, 1 - side), rows_at(level, 1 - side)]).astype(jnp.int32)
+        home_at = jnp.stack([rows_at(1 - level, side), rows_at(level, side)]).astype(jnp.int32)
+        away = out_part(away_at, gated, out_weight, None, rows)
+        got = permute(away, over_core)
+        send, hold = out_part(home_at, gated, out_weight, got, rows)
+        got_y = permute(send, over_y)
+        mine = lax.dynamic_slice_in_dim(scale, rows_at(level, side), rows)[:, None]
+        total = (hold + got_y.astype(f32)) * mine
+        if travelling is not None:
+            total = total + travelling.astype(f32)
+        if step + 1 < planes:
+            travelling = permute(total.astype(jnp.bfloat16), ring)
+    layer_out = (hidden.astype(f32) + total).astype(jnp.bfloat16)
+
+    blocks, sources = [], []
+    for step in range(planes):
+        for index, block in enumerate(
+            (straight[step], straight_core[step], crossed[step], crossed_core[step])
+        ):
+            blocks.append(block)
+            sources.append(((z_pos - step) % planes) * PLANE + (spot ^ index))
+    sources = jnp.stack(sources)
+    targets = jnp.stack([block[:, width] for block in blocks]).astype(jnp.int32)
+    match = (targets == me).astype(jnp.int32)
+    ranks = jnp.cumsum(match, axis=1) - match
+    slots = jnp.where(match == 1, sources[:, None] * CAP + ranks, -1).reshape(-1)
+    select = (slots[None, :] == jnp.arange(count * CAP)[:, None]).astype(jnp.bfloat16)
+    picked = pick_rows(select, blocks, width)
+
+    onehot = (target[:, None] == jnp.arange(count, dtype=jnp.int32)[None, :]).astype(jnp.int32)
+    own_ranks = jnp.sum((jnp.cumsum(onehot, axis=0) - onehot) * onehot, axis=1)
+    own_slots = target * CAP + own_ranks
+    place = (own_slots[None, :] == jnp.arange(count * CAP)[:, None]).astype(jnp.bfloat16)
+    filled = jnp.dot(place, layer_out, preferred_element_type=f32).astype(jnp.bfloat16)
+    received = lax.all_to_all(
+        filled.reshape(count, CAP, width), "tensor", split_axis=0, concat_axis=0, tiled=True
+    )
+    packed = jnp.concatenate([picked, received.reshape(count * CAP, width)], axis=1)
+    return (layer_out, packed)
+
+
 def solution(mesh):
+    planar = mesh.shape["dp"] == 1 and mesh.shape["tensor"] == PLANE * GROUPS
     return jax.shard_map(
-        on_device,
+        on_device_planes if planar else on_device,
         mesh=mesh,
         in_specs=(
             P(("rep", "dp", "tensor"), None),

time: 456 us -> 264 us (0.58)
  waiting for transfers between devices: 272 us -> 57.3 us
  Pallas kernels: 0 us -> 125 us
  matrix products: 67.8 us -> 0.28 us
  blocking collectives: 60.5 us -> 0 us
  starting transfers between devices: 0.3 us -> 33.2 us
  between operations: 14.1 us -> 1.14 us
  other arithmetic: 16.9 us -> 22 us
  loops' own time: 4.83 us -> 0 us
    reduce_scatter x1 -> x0, waiting for transfers between devices: 175 us -> none  [on_device(): lax.psum_scatter(jnp.dot(inner, proj_out, preferred_element_type=jnp.floa...]
    pallas_call x0 -> x18, Pallas kernels: none -> 125 us  [the longest x4 39 us: project_plane(): pl.pallas_call(project_kernel, grid=(cols // tile,), out_shape=(jax.Shape...]
    all_gather x2 -> x0, waiting for transfers between devices: 96.5 us -> none  [the longest x1 77.4 us: on_device(): tokens = lax.all_gather(normed, 'tensor', axis=0, tiled=True)]
    dot_general x25 -> x1, matrix products: 67.8 us -> 0.28 us  [on_device_planes(): jnp.dot(place, layer_out, preferred_element_type=f32).astype(jnp.bfloat16)]
    ppermute x0 -> x36, waiting for transfers between devices: none -> 53.9 us  [permute(): return lax.ppermute(value, 'tensor', pairs)]
    psum x1 -> x0, blocking collectives: 32.1 us -> none  [on_device(): total_sq = lax.psum(partial_sq, 'tensor')]
    ppermute x0 -> x36, starting transfers between devices: none -> 29.6 us  [permute(): return lax.ppermute(value, 'tensor', pairs)]
    all_to_all x1 -> x0, blocking collectives: 28.4 us -> none  [on_device(): lax.all_to_all(filled.reshape(shard_count, CAP, joined.shape[1]), ('dp',...]
  transfers between devices with their start and end apart: 3 -> 37, of which waited for: 3 -> 12; matrix products, arithmetic and copies ran while one was open for 4% -> 13% of each run, Pallas kernels for 0% -> 42%
where the time goes in v1:
time: 264 us; the launch traced here: 262 us
  Pallas kernels  125 us (47%)
  waiting for transfers between devices  57.3 us (22%)
  starting transfers between devices  33.2 us (13%)
  local copies, waits for them, and re-layouts  22.9 us (9%)
  other arithmetic  22 us (8%)
    ppermute x36, waiting for transfers between devices, permute(): return lax.ppermute(value, 'tensor', pairs)  53.9 us
    pallas_call x4, Pallas kernels, project_plane(): pl.pallas_call(project_kernel, grid=(cols // tile,), out_shape=(jax.Shape...  39 us
    ppermute x36, starting transfers between devices, permute(): return lax.ppermute(value, 'tensor', pairs)  29.6 us
    pallas_call x4, Pallas kernels, out_part(): pl.pallas_call(home_kernel, out_shape=(jax.ShapeDtypeStruct((rows, width)...  24.7 us
    pallas_call x4, Pallas kernels, out_part(): pl.pallas_call(away_kernel, out_shape=jax.ShapeDtypeStruct((2 * rows, wid...  23.7 us
    pallas_call x4, Pallas kernels, norm_plane(): pl.pallas_call(norm_kernel, out_shape=(jax.ShapeDtypeStruct((rows, width)...  21.5 us
    pallas_call x1, Pallas kernels, scan_all(): pl.pallas_call(functools.partial(scan_kernel, heads=heads, planes=planes)...  8.93 us
    slice x9, local copies, waits for them, and re-layouts, on_device_planes(): targets = jnp.stack([block[:, width] for block in blocks]).astype(jnp.int32)  7.45 us
  transfers between devices with their start and end apart: 37, of which 12 were waited for; matrix products, arithmetic and copies ran while one was open for 13% of the time, Pallas kernels for 42%

profile of v1, /device:TPU:0, one launch (start us, length us, event | category | flops | bytes accessed | tf_op | source)
XLA Modules:
  0.0 262.0 jit_solution(15085185468392755945)
XLA Ops:
  17.6 4.3 %collective-permute-done.2.b0.refs_4_ = bf16[32,8320]{1,0:T(8,128)(2,1)S(1)} collective-permute-done((bf16[32,8320]{1,0:T(8,128)(2,1)S(1)}, bf16[32,8320]{1,0:T(8,128)(2,1)S(1)}, u32[]{:S(2)}, u32[]{:S(2)}) %collective-permute-start.2) | collective-permute-done | bytes 532512 | tf_op jit(solution)/shard_map/ppermute | solution.py:597
  25.1 10.6 %collective-permute-done.3.b2.refs_6_ = bf16[32,8320]{1,0:T(8,128)(2,1)S(1)} collective-permute-done((bf16[32,8320]{1,0:T(8,128)(2,1)S(1)}, bf16[32,8320]{1,0:T(8,128)(2,1)S(1)}, u32[]{:S(2)}, u32[]{:S(2)}) %collective-permute-start.3) | collective-permute-done | bytes 532512 | tf_op jit(solution)/shard_map/ppermute | solution.py:597
  42.7 9.8 %collective-permute-done.7.b2.refs_10_ = bf16[32,8320]{1,0:T(8,128)(2,1)S(1)} collective-permute-done((bf16[32,8320]{1,0:T(8,128)(2,1)S(1)}, bf16[32,8320]{1,0:T(8,128)(2,1)S(1)}, u32[]{:S(2)}, u32[]{:S(2)}) %collective-permute-start.7) | collective-permute-done | bytes 532512 | tf_op jit(solution)/shard_map/ppermute | solution.py:597
  61.2 5.4 %norm_plane.4 = (bf16[128,8192]{1,0:T(8,128)(2,1)}, bf16[128,64]{1,0:T(8,128)(2,1)}, f32[128,128]{1,0:T(8,128)}) custom-call(s32[1]{0:T(128)} %bitcast.3.spot_ref, bf16[32,8320]{1,0:T(8,128)(2,1)} %copy-done, bf16[32,8320]{1,0:T(8,128)(2,1)} %copy-done.2, bf16[32,8320]{1,0:T(8,128)(2,1)} %copy-done.1, bf16[32,8320]{1,0:T(8,128)(2,1)} %copy-done.7, ...), custom_call_target="tpu_custom_call" | custom-call | flops 402653184 | bytes 8388608 | tf_op jit(solution)/shard_map/norm_plane/pallas_call | solution.py:251
  67.3 9.8 %project_plane.4 = (bf16[128,512]{1,0:T(8,128)(2,1)}, bf16[128,512]{1,0:T(8,128)(2,1)}) custom-call(bf16[128,8192]{1,0:T(8,128)(2,1)} %get-tuple-element.50.normed_ref, bf16[512,8192]{1,0:T(8,128)(2,1)} %wx_ref.7, bf16[512,8192]{1,0:T(8,128)(2,1)} %wz_ref.7), custom_call_target="tpu_custom_call" | custom-call | flops 2147483648 | bytes 20971520 | tf_op jit(solution)/shard_map/project_plane/pallas_call | solution.py:277
  77.1 5.4 %norm_plane.5 = (bf16[128,8192]{1,0:T(8,128)(2,1)}, bf16[128,64]{1,0:T(8,128)(2,1)}, f32[128,128]{1,0:T(8,128)}) custom-call(s32[1]{0:T(128)} %bitcast.3.spot_ref, bf16[32,8320]{1,0:T(8,128)(2,1)} %copy-done.3, bf16[32,8320]{1,0:T(8,128)(2,1)} %copy-done.5, bf16[32,8320]{1,0:T(8,128)(2,1)} %copy-done.4, bf16[32,8320]{1,0:T(8,128)(2,1)} %copy-done.10, ...), custom_call_target="tpu_custom_call" | custom-call | flops 402653184 | bytes 8388608 | tf_op jit(solution)/shard_map/norm_plane/pallas_call | solution.py:251
  83.4 9.8 %project_plane.5 = (bf16[128,512]{1,0:T(8,128)(2,1)}, bf16[128,512]{1,0:T(8,128)(2,1)}) custom-call(bf16[128,8192]{1,0:T(8,128)(2,1)} %get-tuple-element.56.normed_ref, bf16[512,8192]{1,0:T(8,128)(2,1)} %wx_ref.7, bf16[512,8192]{1,0:T(8,128)(2,1)} %wz_ref.7), custom_call_target="tpu_custom_call" | custom-call | flops 2147483648 | bytes 20971520 | tf_op jit(solution)/shard_map/project_plane/pallas_call | solution.py:277
  93.2 5.4 %norm_plane.6 = (bf16[128,8192]{1,0:T(8,128)(2,1)}, bf16[128,64]{1,0:T(8,128)(2,1)}, f32[128,128]{1,0:T(8,128)}) custom-call(s32[1]{0:T(128)} %bitcast.3.spot_ref, bf16[32,8320]{1,0:T(8,128)(2,1)} %copy-done.6, bf16[32,8320]{1,0:T(8,128)(2,1)} %copy-done.9, bf16[32,8320]{1,0:T(8,128)(2,1)} %copy-done.8, ...), custom_call_target="tpu_custom_call" | custom-call | flops 402653184 | bytes 8388608 | tf_op jit(solution)/shard_map/norm_plane/pallas_call | solution.py:251
  103.1 9.8 %project_plane.6 = (bf16[128,512]{1,0:T(8,128)(2,1)}, bf16[128,512]{1,0:T(8,128)(2,1)}) custom-call(bf16[128,8192]{1,0:T(8,128)(2,1)} %get-tuple-element.62.normed_ref, bf16[512,8192]{1,0:T(8,128)(2,1)} %wx_ref.7, bf16[512,8192]{1,0:T(8,128)(2,1)} %wz_ref.7), custom_call_target="tpu_custom_call" | custom-call | flops 2147483648 | bytes 20971520 | tf_op jit(solution)/shard_map/project_plane/pallas_call | solution.py:277
  113.7 5.4 %norm_plane.7 = (bf16[128,8192]{1,0:T(8,128)(2,1)}, bf16[128,64]{1,0:T(8,128)(2,1)}, f32[128,128]{1,0:T(8,128)}) custom-call(s32[1]{0:T(128)} %bitcast.3.spot_ref, bf16[32,8320]{1,0:T(8,128)(2,1)} %collective-permute-done.9.b0.refs_12_, bf16[32,8320]{1,0:T(8,128)(2,1)} %collective-permute-done.12.b1.refs_13_, ...), custom_call_target="tpu_custom_call" | custom-call | flops 402653184 | bytes 8388608 | tf_op jit(solution)/shard_map/norm_plane/pallas_call | solution.py:251
  120.6 6.9 %collective-permute-start.21 = (bf16[128,64]{1,0:T(8,128)(2,1)}, bf16[128,64]{1,0:T(8,128)(2,1)S(1)}, u32[]{:S(2)}, u32[]{:S(2)}) collective-permute-start(bf16[128,64]{1,0:T(8,128)(2,1)} %get-tuple-element.79), channel_id=1, source_target_pairs={{0,2},{1,3},{2,6},{3,7},{4,10},{5,11},{6,14},{7,15},{8,0},{9,1},{1... | collective-permute-start | bytes 49160 | tf_op jit(solution)/shard_map/ppermute | solution.py:597
  128.7 9.7 %project_plane.7 = (bf16[128,512]{1,0:T(8,128)(2,1)}, bf16[128,512]{1,0:T(8,128)(2,1)}) custom-call(bf16[128,8192]{1,0:T(8,128)(2,1)} %get-tuple-element.66.normed_ref, bf16[512,8192]{1,0:T(8,128)(2,1)} %wx_ref.7, bf16[512,8192]{1,0:T(8,128)(2,1)} %wz_ref.7), custom_call_target="tpu_custom_call" | custom-call | flops 2147483648 | bytes 20971520 | tf_op jit(solution)/shard_map/project_plane/pallas_call | solution.py:277
  139.3 8.9 %scan_all.1 = (bf16[512,512]{1,0:T(8,128)(2,1)}, f32[8,128]{1,0:T(8,128)}) custom-call(s32[2]{0:T(128)} %pad_add_fusion.1.spot_ref, bf16[128,512]{1,0:T(8,128)(2,1)} %get-tuple-element.51.refs_0_, bf16[128,512]{1,0:T(8,128)(2,1)} %get-tuple-element.57.refs_1_, bf16[128,512]{1,0:T(8,128)(2,1)} %get-tuple-element.63.refs_2_, ...), custom_call_target="tpu_custom_call" | custom-call | flops 1073741824 | bytes 8388608 | tf_op jit(solution)/shard_map/scan_all/pallas_call | solution.py:409
  148.2 5.9 %out_away.7 = bf16[64,8192]{1,0:T(8,128)(2,1)} custom-call(s32[2]{0:T(128)} %pad_add_fusion.9.at_ref, bf16[512,512]{1,0:T(8,128)(2,1)} %get-tuple-element.80.gated_ref, bf16[512,8192]{1,0:T(8,128)(2,1)} %weight_ref.15), custom_call_target="tpu_custom_call" | custom-call | flops 536870912 | bytes 10485760 | tf_op jit(solution)/shard_map/out_away/pallas_call | solution.py:467
  154.8 5.9 %out_away.6 = bf16[64,8192]{1,0:T(8,128)(2,1)} custom-call(s32[2]{0:T(128)} %pad_add_fusion.7.at_ref, bf16[512,512]{1,0:T(8,128)(2,1)} %get-tuple-element.80.gated_ref, bf16[512,8192]{1,0:T(8,128)(2,1)} %weight_ref.15), custom_call_target="tpu_custom_call" | custom-call | flops 536870912 | bytes 10485760 | tf_op jit(solution)/shard_map/out_away/pallas_call | solution.py:467
  164.6 6.2 %out_home.7 = (bf16[32,8192]{1,0:T(8,128)(2,1)}, f32[32,8192]{1,0:T(8,128)}) custom-call(s32[2]{0:T(128)} %pad_add_fusion.8.at_ref, bf16[512,512]{1,0:T(8,128)(2,1)} %get-tuple-element.80.gated_ref, bf16[512,8192]{1,0:T(8,128)(2,1)} %weight_ref.15, bf16[64,8192]{1,0:T(8,128)(2,1)} %copy-done.15), custom_call_target="tpu_custom_call" | custom-call | flops 536870912 | bytes 10485760 | tf_op jit(solution)/shard_map/out_home/pallas_call | solution.py:475
  173.6 5.9 %out_away.5 = bf16[64,8192]{1,0:T(8,128)(2,1)} custom-call(s32[2]{0:T(128)} %pad_add_fusion.5.at_ref, bf16[512,512]{1,0:T(8,128)(2,1)} %get-tuple-element.80.gated_ref, bf16[512,8192]{1,0:T(8,128)(2,1)} %weight_ref.15), custom_call_target="tpu_custom_call" | custom-call | flops 536870912 | bytes 10485760 | tf_op jit(solution)/shard_map/out_away/pallas_call | solution.py:467
  179.5 5.8 %collective-permute-done.26 = f32[8,128]{1,0:T(8,128)S(1)} collective-permute-done((f32[8,128]{1,0:T(8,128)S(1)}, f32[8,128]{1,0:T(8,128)S(1)}, u32[]{:S(2)}, u32[]{:S(2)}) %collective-permute-start.26) | collective-permute-done | bytes 4128 | tf_op jit(solution)/shard_map/ppermute | solution.py:597
  186.4 6.2 %out_home.6 = (bf16[32,8192]{1,0:T(8,128)(2,1)}, f32[32,8192]{1,0:T(8,128)}) custom-call(s32[2]{0:T(128)} %pad_add_fusion.6.at_ref, bf16[512,512]{1,0:T(8,128)(2,1)} %get-tuple-element.80.gated_ref, bf16[512,8192]{1,0:T(8,128)(2,1)} %weight_ref.15, bf16[64,8192]{1,0:T(8,128)(2,1)} %copy-done.14), custom_call_target="tpu_custom_call" | custom-call | flops 536870912 | bytes 10485760 | tf_op jit(solution)/shard_map/out_home/pallas_call | solution.py:475
  193.7 5.9 %out_away.4 = bf16[64,8192]{1,0:T(8,128)(2,1)} custom-call(s32[2]{0:T(128)} %pad_add_fusion.3.at_ref, bf16[512,512]{1,0:T(8,128)(2,1)} %get-tuple-element.80.gated_ref, bf16[512,8192]{1,0:T(8,128)(2,1)} %weight_ref.15), custom_call_target="tpu_custom_call" | custom-call | flops 536870912 | bytes 10485760 | tf_op jit(solution)/shard_map/out_away/pallas_call | solution.py:467
  200.6 6.2 %out_home.5 = (bf16[32,8192]{1,0:T(8,128)(2,1)}, f32[32,8192]{1,0:T(8,128)}) custom-call(s32[2]{0:T(128)} %pad_add_fusion.4.at_ref, bf16[512,512]{1,0:T(8,128)(2,1)} %get-tuple-element.80.gated_ref, bf16[512,8192]{1,0:T(8,128)(2,1)} %weight_ref.15, bf16[64,8192]{1,0:T(8,128)(2,1)} %copy-done.16), custom_call_target="tpu_custom_call" | custom-call | flops 536870912 | bytes 10485760 | tf_op jit(solution)/shard_map/out_home/pallas_call | solution.py:475
  213.0 6.2 %out_home.4 = (bf16[32,8192]{1,0:T(8,128)(2,1)}, f32[32,8192]{1,0:T(8,128)}) custom-call(s32[2]{0:T(128)} %pad_add_fusion.at_ref, bf16[512,512]{1,0:T(8,128)(2,1)} %get-tuple-element.80.gated_ref, bf16[512,8192]{1,0:T(8,128)(2,1)} %weight_ref.15, bf16[64,8192]{1,0:T(8,128)(2,1)} %copy-done.17), custom_call_target="tpu_custom_call" | custom-call | flops 536870912 | bytes 10485760 | tf_op jit(solution)/shard_map/out_home/pallas_call | solution.py:475
  233.1 6.9 %collective-permute-done.35 = bf16[32,8192]{1,0:T(8,128)(2,1)S(1)} collective-permute-done((bf16[32,8192]{1,0:T(8,128)(2,1)S(1)}, bf16[32,8192]{1,0:T(8,128)(2,1)S(1)}, u32[]{:S(2)}, u32[]{:S(2)}) %collective-permute-start.35) | collective-permute-done | bytes 524320 | tf_op jit(solution)/shard_map/ppermute | solution.py:597
  248.9 7.4 %pick_rows.1 = bf16[32,8192]{1,0:T(8,128)(2,1)} custom-call(bf16[32,512]{1,0:T(8,128)(2,1)} %fusion.3.select_ref, bf16[32,8320]{1,0:T(8,128)(2,1)} %copy-done, bf16[32,8320]{1,0:T(8,128)(2,1)} %copy-done.2, bf16[32,8320]{1,0:T(8,128)(2,1)} %copy-done.1, bf16[32,8320]{1,0:T(8,128)(2,1)} %copy-done.7, bf16[32,8320]{1,0:T(8,128)(2,1)} %copy-done.3, ...), custom_call_target="tpu_custom_call" | custom-call | flops 268435456 | bytes 9437184 | tf_op jit(solution)/shard_map/pick_rows/pallas_call | solution.py:498
  (227 shorter events, 91.3 us)
Async XLA Ops:
  2.5 15.1 %collective-permute-start = (bf16[32,8320]{1,0:T(8,128)(2,1)S(1)}, bf16[32,8320]{1,0:T(8,128)(2,1)S(1)}, u32[]{:S(2)}, u32[]{:S(2)}) collective-permute-start(bf16[32,8320]{1,0:T(8,128)(2,1)S(1)} %pad_maximum_fusion.2.b0.refs_0_), channel_id=1, source_target_pairs={{0,2},{1,3},{2,0},{3,1},{4,6},{5,7},{6,4},{7,5},{8,10},{9,11},{10,... | collective-permute-start | bytes 1597448 | tf_op jit(solution)/shard_map/ppermute | solution.py:597
  5.5 16.4 %collective-permute-start.2 = (bf16[32,8320]{1,0:T(8,128)(2,1)S(1)}, bf16[32,8320]{1,0:T(8,128)(2,1)S(1)}, u32[]{:S(2)}, u32[]{:S(2)}) collective-permute-start(bf16[32,8320]{1,0:T(8,128)(2,1)S(1)} %pad_maximum_fusion.2.b0.refs_0_), channel_id=1, source_target_pairs={{0,4},{1,5},{2,6},{3,7},{4,8},{5,9},{6,10},{7,11},{8,12},{9,13},{1... | collective-permute-start | bytes 1597448 | tf_op jit(solution)/shard_map/ppermute | solution.py:597
  22.4 16.3 %collective-permute-start.5 = (bf16[32,8320]{1,0:T(8,128)(2,1)S(1)}, bf16[32,8320]{1,0:T(8,128)(2,1)S(1)}, u32[]{:S(2)}, u32[]{:S(2)}) collective-permute-start(bf16[32,8320]{1,0:T(8,128)(2,1)S(1)} %collective-permute-done.2.b0.refs_4_), channel_id=1, source_target_pairs={{0,4},{1,5},{2,6},{3,7},{4,8},{5,9},{6,10},{7,11},{8,12},{9,13},{1... | collective-permute-start | bytes 1597448 | tf_op jit(solution)/shard_map/ppermute | solution.py:597
  22.4 16.3 %collective-permute-start.6 = (bf16[32,8320]{1,0:T(8,128)(2,1)S(1)}, bf16[32,8320]{1,0:T(8,128)(2,1)S(1)}, u32[]{:S(2)}, u32[]{:S(2)}) collective-permute-start(bf16[32,8320]{1,0:T(8,128)(2,1)S(1)} %collective-permute-done.b2.refs_2_), channel_id=1, source_target_pairs={{0,1},{1,0},{2,3},{3,2},{4,5},{5,4},{6,7},{7,6},{8,9},{9,8},{10,11... | collective-permute-start | bytes 1597448 | tf_op jit(solution)/shard_map/ppermute | solution.py:597
  40.3 16.4 %collective-permute-start.9 = (bf16[32,8320]{1,0:T(8,128)(2,1)S(1)}, bf16[32,8320]{1,0:T(8,128)(2,1)}, u32[]{:S(2)}, u32[]{:S(2)}) collective-permute-start(bf16[32,8320]{1,0:T(8,128)(2,1)S(1)} %collective-permute-done.5.b0.refs_8_), channel_id=1, source_target_pairs={{0,4},{1,5},{2,6},{3,7},{4,8},{5,9},{6,10},{7,11},{8,12},{9,13},{1... | collective-permute-start | bytes 1597448 | tf_op jit(solution)/shard_map/ppermute | solution.py:597
  40.3 16.4 %collective-permute-start.10 = (bf16[32,8320]{1,0:T(8,128)(2,1)S(1)}, bf16[32,8320]{1,0:T(8,128)(2,1)S(1)}, u32[]{:S(2)}, u32[]{:S(2)}) collective-permute-start(bf16[32,8320]{1,0:T(8,128)(2,1)S(1)} %collective-permute-done.3.b2.refs_6_), channel_id=1, source_target_pairs={{0,1},{1,0},{2,3},{3,2},{4,5},{5,4},{6,7},{7,6},{8,9},{9,8},{10,11... | collective-permute-start | bytes 1597448 | tf_op jit(solution)/shard_map/ppermute | solution.py:597
  56.7 26.5 %collective-permute-start.11 = (bf16[32,8320]{1,0:T(8,128)(2,1)}, bf16[32,8320]{1,0:T(8,128)(2,1)}, u32[]{:S(2)}, u32[]{:S(2)}) collective-permute-start(bf16[32,8320]{1,0:T(8,128)(2,1)} %collective-permute-done.9.b0.refs_12_), channel_id=1, source_target_pairs={{0,2},{1,3},{2,0},{3,1},{4,6},{5,7},{6,4},{7,5},{8,10},{9,11},{10,... | collective-permute-start | bytes 1597448 | tf_op jit(solution)/shard_map/ppermute | solution.py:597
  57.3 25.9 %collective-permute-start.12 = (bf16[32,8320]{1,0:T(8,128)(2,1)}, bf16[32,8320]{1,0:T(8,128)(2,1)}, u32[]{:S(2)}, u32[]{:S(2)}) collective-permute-start(bf16[32,8320]{1,0:T(8,128)(2,1)} %collective-permute-done.9.b0.refs_12_), channel_id=1, source_target_pairs={{0,1},{1,0},{2,3},{3,2},{4,5},{5,4},{6,7},{7,6},{8,9},{9,8},{10,11... | collective-permute-start | bytes 1597448 | tf_op jit(solution)/shard_map/ppermute | solution.py:597
  57.3 25.9 %collective-permute-start.13 = (bf16[32,8320]{1,0:T(8,128)(2,1)S(1)}, bf16[32,8320]{1,0:T(8,128)(2,1)}, u32[]{:S(2)}, u32[]{:S(2)}) collective-permute-start(bf16[32,8320]{1,0:T(8,128)(2,1)S(1)} %collective-permute-done.7.b2.refs_10_), channel_id=1, source_target_pairs={{0,1},{1,0},{2,3},{3,2},{4,5},{5,4},{6,7},{7,6},{8,9},{9,8},{10,11... | collective-permute-start | bytes 1597448 | tf_op jit(solution)/shard_map/ppermute | solution.py:597
  83.2 29.6 %collective-permute-start.14 = (bf16[32,8320]{1,0:T(8,128)(2,1)}, bf16[32,8320]{1,0:T(8,128)(2,1)S(1)}, u32[]{:S(2)}, u32[]{:S(2)}) collective-permute-start(bf16[32,8320]{1,0:T(8,128)(2,1)} %collective-permute-done.11.b2.refs_14_), channel_id=1, source_target_pairs={{0,1},{1,0},{2,3},{3,2},{4,5},{5,4},{6,7},{7,6},{8,9},{9,8},{10,11... | collective-permute-start | bytes 1597448 | tf_op jit(solution)/shard_map/ppermute | solution.py:597
  99.3 21.1 %collective-permute-start.15 = (bf16[384,64]{1,0:T(8,128)(2,1)S(1)}, bf16[384,64]{1,0:T(8,128)(2,1)S(1)}, u32[]{:S(2)}, u32[]{:S(2)}) collective-permute-start(bf16[384,64]{1,0:T(8,128)(2,1)S(1)} %constant_dynamic-update-slice_fusion), channel_id=1, source_target_pairs={{0,0},{1,1},{2,4},{3,5},{4,8},{5,9},{6,12},{7,13},{8,2},{9,3},{10,... | collective-permute-start | bytes 147464 | tf_op jit(solution)/shard_map/ppermute | solution.py:597
  100.0 20.6 %collective-permute-start.16 = (bf16[384,64]{1,0:T(8,128)(2,1)S(1)}, bf16[384,64]{1,0:T(8,128)(2,1)S(1)}, u32[]{:S(2)}, u32[]{:S(2)}) collective-permute-start(bf16[384,64]{1,0:T(8,128)(2,1)S(1)} %constant_dynamic-update-slice_fusion), channel_id=1, source_target_pairs={{0,1},{1,0},{2,5},{3,4},{4,9},{5,8},{6,13},{7,12},{8,3},{9,2},{10,... | collective-permute-start | bytes 147464 | tf_op jit(solution)/shard_map/ppermute | solution.py:597
  100.4 27.1 %collective-permute-start.17 = (bf16[384,64]{1,0:T(8,128)(2,1)S(1)}, bf16[384,64]{1,0:T(8,128)(2,1)S(1)}, u32[]{:S(2)}, u32[]{:S(2)}) collective-permute-start(bf16[384,64]{1,0:T(8,128)(2,1)S(1)} %constant_dynamic-update-slice_fusion), channel_id=1, source_target_pairs={{0,2},{1,3},{2,6},{3,7},{4,10},{5,11},{6,14},{7,15},{8,0},{9,1},{1... | collective-permute-start | bytes 147464 | tf_op jit(solution)/shard_map/ppermute | solution.py:597
  102.9 35.6 %collective-permute-start.18 = (bf16[384,64]{1,0:T(8,128)(2,1)S(1)}, bf16[384,64]{1,0:T(8,128)(2,1)S(1)}, u32[]{:S(2)}, u32[]{:S(2)}) collective-permute-start(bf16[384,64]{1,0:T(8,128)(2,1)S(1)} %constant_dynamic-update-slice_fusion), channel_id=1, source_target_pairs={{0,3},{1,2},{2,7},{3,6},{4,11},{5,10},{6,15},{7,14},{8,1},{9,0},{1... | collective-permute-start | bytes 147464 | tf_op jit(solution)/shard_map/ppermute | solution.py:597
  119.0 19.5 %collective-permute-start.19 = (bf16[128,64]{1,0:T(8,128)(2,1)}, bf16[128,64]{1,0:T(8,128)(2,1)S(1)}, u32[]{:S(2)}, u32[]{:S(2)}) collective-permute-start(bf16[128,64]{1,0:T(8,128)(2,1)} %get-tuple-element.79), channel_id=1, source_target_pairs={{0,0},{1,1},{2,4},{3,5},{4,8},{5,9},{6,12},{7,13},{8,2},{9,3},{10,... | collective-permute-start | bytes 49160 | tf_op jit(solution)/shard_map/ppermute | solution.py:597
  120.4 18.1 %collective-permute-start.20 = (bf16[128,64]{1,0:T(8,128)(2,1)}, bf16[128,64]{1,0:T(8,128)(2,1)S(1)}, u32[]{:S(2)}, u32[]{:S(2)}) collective-permute-start(bf16[128,64]{1,0:T(8,128)(2,1)} %get-tuple-element.79), channel_id=1, source_target_pairs={{0,1},{1,0},{2,5},{3,4},{4,9},{5,8},{6,13},{7,12},{8,3},{9,2},{10,... | collective-permute-start | bytes 49160 | tf_op jit(solution)/shard_map/ppermute | solution.py:597
  120.6 17.9 %collective-permute-start.21 = (bf16[128,64]{1,0:T(8,128)(2,1)}, bf16[128,64]{1,0:T(8,128)(2,1)S(1)}, u32[]{:S(2)}, u32[]{:S(2)}) collective-permute-start(bf16[128,64]{1,0:T(8,128)(2,1)} %get-tuple-element.79), channel_id=1, source_target_pairs={{0,2},{1,3},{2,6},{3,7},{4,10},{5,11},{6,14},{7,15},{8,0},{9,1},{1... | collective-permute-start | bytes 49160 | tf_op jit(solution)/shard_map/ppermute | solution.py:597
  160.7 24.7 %collective-permute-start.29 = (bf16[64,8192]{1,0:T(8,128)(2,1)}, bf16[64,8192]{1,0:T(8,128)(2,1)S(1)}, u32[]{:S(2)}, u32[]{:S(2)}) collective-permute-start(bf16[64,8192]{1,0:T(8,128)(2,1)} %out_away.6), channel_id=1, source_target_pairs={{0,1},{1,0},{2,3},{3,2},{4,5},{5,4},{6,7},{7,6},{8,9},{9,8},{10,11... | collective-permute-start | bytes 3145736 | tf_op jit(solution)/shard_map/ppermute | solution.py:597
  170.8 22.2 %collective-permute-start.32 = (bf16[32,8192]{1,0:T(8,128)(2,1)}, bf16[32,8192]{1,0:T(8,128)(2,1)S(1)}, u32[]{:S(2)}, u32[]{:S(2)}) collective-permute-start(bf16[32,8192]{1,0:T(8,128)(2,1)} %get-tuple-element.89), channel_id=1, source_target_pairs={{0,2},{1,3},{2,0},{3,1},{4,6},{5,7},{6,4},{7,5},{8,10},{9,11},{10,... | collective-permute-start | bytes 1572872 | tf_op jit(solution)/shard_map/ppermute | solution.py:597
  179.5 20.1 %collective-permute-start.27 = (bf16[64,8192]{1,0:T(8,128)(2,1)}, bf16[64,8192]{1,0:T(8,128)(2,1)S(1)}, u32[]{:S(2)}, u32[]{:S(2)}) collective-permute-start(bf16[64,8192]{1,0:T(8,128)(2,1)} %out_away.5), channel_id=1, source_target_pairs={{0,1},{1,0},{2,3},{3,2},{4,5},{5,4},{6,7},{7,6},{8,9},{9,8},{10,11... | collective-permute-start | bytes 3145736 | tf_op jit(solution)/shard_map/ppermute | solution.py:597
  192.6 15.5 %collective-permute-start.30 = (bf16[32,8192]{1,0:T(8,128)(2,1)}, bf16[32,8192]{1,0:T(8,128)(2,1)S(1)}, u32[]{:S(2)}, u32[]{:S(2)}) collective-permute-start(bf16[32,8192]{1,0:T(8,128)(2,1)} %get-tuple-element.87), channel_id=1, source_target_pairs={{0,2},{1,3},{2,0},{3,1},{4,6},{5,7},{6,4},{7,5},{8,10},{9,11},{10,... | collective-permute-start | bytes 1572872 | tf_op jit(solution)/shard_map/ppermute | solution.py:597
  208.4 16.1 %collective-permute-start.34 = (bf16[32,8192]{1,0:T(8,128)(2,1)S(1)}, bf16[32,8192]{1,0:T(8,128)(2,1)S(1)}, u32[]{:S(2)}, u32[]{:S(2)}) collective-permute-start(bf16[32,8192]{1,0:T(8,128)(2,1)S(1)} %add_convert_fusion.2), channel_id=1, source_target_pairs={{0,4},{1,5},{2,6},{3,7},{4,8},{5,9},{6,10},{7,11},{8,12},{9,13},{1... | collective-permute-start | bytes 1572872 | tf_op jit(solution)/shard_map/ppermute | solution.py:597
  224.7 15.3 %collective-permute-start.35 = (bf16[32,8192]{1,0:T(8,128)(2,1)S(1)}, bf16[32,8192]{1,0:T(8,128)(2,1)S(1)}, u32[]{:S(2)}, u32[]{:S(2)}) collective-permute-start(bf16[32,8192]{1,0:T(8,128)(2,1)S(1)} %add_convert_fusion.1), channel_id=1, source_target_pairs={{0,4},{1,5},{2,6},{3,7},{4,8},{5,9},{6,10},{7,11},{8,12},{9,13},{1... | collective-permute-start | bytes 1572872 | tf_op jit(solution)/shard_map/ppermute | solution.py:597
  241.8 18.0 %all-to-all-start = ((bf16[16,2,8192]{2,1,0:T(2,128)(2,1)}), bf16[16,2,8192]{2,1,0:T(2,128)(2,1)S(1)}, u32[]{:S(2)}, u32[]{:S(2)}) async-start(bf16[16,2,8192]{2,1,0:T(2,128)(2,1)} %reshape.277), calls=%async_computation | async-start | bytes 1048576 | tf_op jit(solution)/shard_map/all_to_all | solution.py:706
  (50 other events, 806.5 us)

commit v2 on v0

--- a/solution.py
+++ b/solution.py
@@ -1,6 +1,10 @@
+import functools
+
 import jax
 import jax.numpy as jnp
 from jax import lax
+from jax.experimental import pallas as pl
+from jax.experimental.pallas import tpu as pltpu
 from jax.sharding import PartitionSpec as P
 
 HEAD_DIM = 64
@@ -200,9 +204,633 @@
     return (layer_out, packed)
 
 
+PLANE = 4
+VMEM_LIMIT = 16 * 1024 * 1024
+WEIGHT_LIMIT = 28 * 1024 * 1024
+NEG = -1e30
+
+
+def vmem():
+    return pl.BlockSpec(memory_space=pltpu.VMEM)
+
+
+def smem():
+    return pl.BlockSpec(memory_space=pltpu.SMEM)
+
+
+def near(value):
+    return pltpu.with_memory_space_constraint(value, pltpu.VMEM)
+
+
+def far(value):
+    return pltpu.with_memory_space_constraint(value, pltpu.MemorySpace.HBM)
+
+
+def dot_nt(left, right, precision=None):
+    return lax.dot_general(
+        left, right, (((1,), (1,)), ((), ())), precision=precision, preferred_element_type=jnp.float32
+    )
+
+
+def norm_kernel(spot_ref, *refs, pieces):
+    gain_ref, small_ref, normed_ref, bc_ref, dt_ref = refs[sum(pieces) :]
+    width = gain_ref.shape[1]
+    step = 1024
+    taken = 0
+    rows = sum(ref.shape[0] for ref in refs[: pieces[0]])
+    for index, parts in enumerate(pieces):
+        below = 0
+        for ref in refs[taken : taken + parts]:
+            high = ref.shape[0]
+            start = pl.multiple_of((spot_ref[1] ^ index) * rows + below, high)
+            total = jnp.zeros((high, 128), jnp.float32)
+            for col in range(0, width, step):
+                wide = ref[:, col : col + step].astype(jnp.float32)
+                square = wide * wide
+                for lane in range(0, step, 128):
+                    total = total + square[:, lane : lane + 128]
+            scale = lax.rsqrt(jnp.sum(total, axis=1, keepdims=True) / width + 1e-05)
+            for col in range(0, width, step):
+                wide = ref[:, col : col + step].astype(jnp.float32)
+                normed_ref[pl.ds(start, high), col : col + step] = (
+                    wide * scale * gain_ref[:, col : col + step].astype(jnp.float32)
+                ).astype(jnp.bfloat16)
+            below += high
+        taken += parts
+    result = dot_nt(normed_ref[...], small_ref[...]).astype(jnp.bfloat16)
+    half = bc_ref.shape[1]
+    bc_ref[...] = result[:, :half]
+    dt_ref[...] = result[:, half:].astype(jnp.float32)
+
+
+def norm_plane(spots, blocks, gain, small):
+    rows, width = blocks[0][0].shape[0] * PLANE, gain.shape[1]
+    flat = [near(part) for block in blocks for part in block]
+    return pl.pallas_call(
+        functools.partial(norm_kernel, pieces=tuple(len(block) for block in blocks)),
+        out_shape=(
+            jax.ShapeDtypeStruct((rows, width), jnp.bfloat16),
+            jax.ShapeDtypeStruct((rows, small.shape[0] - 128), jnp.bfloat16),
+            jax.ShapeDtypeStruct((rows, 128), jnp.float32),
+        ),
+        in_specs=[smem()] + [vmem()] * (len(flat) + 2),
+        out_specs=(vmem(), vmem(), vmem()),
+        compiler_params=pltpu.CompilerParams(vmem_limit_bytes=VMEM_LIMIT),
+        cost_estimate=pl.CostEstimate(
+            flops=1 << 31, bytes_accessed=6 << 20, transcendentals=0
+        ),
+        name="norm_plane",
+    )(spots, *flat, near(gain), near(small))
+
+
+def flow(sources, held, sems, ahead):
+    copies = [
+        pltpu.make_async_copy(source, held.at[i], sems.at[i]) for i, source in enumerate(sources)
+    ]
+    for copy in copies[:ahead]:
+        copy.start()
+
+    def take(i):
+        copies[i].wait()
+        if i + ahead < len(copies):
+            copies[i + ahead].start()
+
+    return take
+
+
+def project_kernel(*refs, planes):
+    normed, (wx_ref, wz_ref) = refs[:planes], refs[planes : planes + 2]
+    outs, (left, held, sems) = refs[planes + 2 : -3], refs[-3:]
+    tile = held.shape[1]
+    count = wx_ref.shape[0] // tile
+    take = flow(
+        [ref.at[pl.ds(i * tile, tile)] for ref in (wx_ref, wz_ref) for i in range(count)], held, sems, 3
+    )
+    rows = normed[0].shape[0]
+    for index, ref in enumerate(normed):
+        left[index * rows : (index + 1) * rows, :] = ref[...]
+    for i in range(0, 2 * count, 2):
+        take(i)
+        take(i + 1)
+        weight = jnp.concatenate([held[i], held[i + 1]], axis=0)
+        result = dot_nt(left[...], weight).astype(jnp.bfloat16)
+        col = i % count * tile
+        for index in range(planes):
+            outs[2 * index + i // count][:, col : col + 2 * tile] = result[
+                index * rows : (index + 1) * rows
+            ]
+
+
+def project_planes(normed, in_x, in_z):
+    rows, width = normed[0].shape
+    cols = in_x.shape[0]
+    tile = 128
+    pieces = 2 * cols // tile
+    count = len(normed)
+    far_space = pl.BlockSpec(memory_space=pltpu.MemorySpace.HBM)
+    outs = pl.pallas_call(
+        functools.partial(project_kernel, planes=count),
+        out_shape=(jax.ShapeDtypeStruct((rows, cols), jnp.bfloat16),) * (2 * count),
+        in_specs=[vmem()] * count + [far_space, far_space],
+        out_specs=(vmem(),) * (2 * count),
+        scratch_shapes=[
+            pltpu.VMEM((count * rows, width), jnp.bfloat16),
+            pltpu.VMEM((pieces, tile, width), jnp.bfloat16),
+            pltpu.SemaphoreType.DMA((pieces,)),
+        ],
+        compiler_params=pltpu.CompilerParams(vmem_limit_bytes=WEIGHT_LIMIT),
+        cost_estimate=pl.CostEstimate(
+            flops=6 << 30, bytes_accessed=16 << 20, transcendentals=0
+        ),
+        name="project_planes",
+    )(*[near(value) for value in normed], far(in_x), far(in_z))
+    return outs[0::2], outs[1::2]
+
+
+def silu(value):
+    return value / (1.0 + jnp.exp(-value))
+
+
+def scan_kernel(
+    spot_ref,
+    *refs,
+    heads,
+    planes,
+):
+    xs, zs, dts = refs[:planes], refs[planes : 2 * planes], refs[2 * planes : 3 * planes]
+    refs = refs[3 * planes :]
+    early, late = refs[:2], refs[2:4]
+    (taps_x, taps_bc, masks, bias, marks, keep, head_rows, gain_ref) = refs[4:12]
+    gated_ref, square_ref = refs[12:14]
+    x_all, z_all, dt_all, bc_all = refs[14:]
+    z_pos, spot = spot_ref[0], spot_ref[1]
+    rows = xs[0].shape[0]
+    chans = xs[0].shape[1]
+    highest_ = lax.Precision.HIGHEST
+    upper = spot >= 2
+    ahead = early[0].shape[0] // rows
+    x_all[0:8, :] = jnp.zeros((8, chans), jnp.float32)
+    bc_all[0:8, :] = jnp.zeros((8, 2 * STATE), jnp.float32)
+    for s in range(planes):
+        at = pl.multiple_of(lax.rem(z_pos - s + planes, planes) * rows, rows)
+        x_all[pl.ds(at + 8, rows), :] = xs[s][...].astype(jnp.float32)
+        z_all[pl.ds(at, rows), :] = zs[s][...]
+        dt_all[pl.ds(at, rows), :] = dts[s][...]
+        part = early if s < ahead else late
+        first = (s if s < ahead else s - ahead) * rows
+        one, two = [ref[first : first + rows, :].astype(jnp.float32) for ref in part]
+        for chip, left, value in (
+            (z_pos, 0, jnp.where(upper, two, one)),
+            (z_pos + GROUPS, STATE, jnp.where(upper, one, two)),
+        ):
+            row = lax.rem(lax.div(chip, PLANE // 2) - s + planes, planes) * rows
+            row = pl.multiple_of(row, rows)
+            bc_all[pl.ds(row + 8, rows), left : left + STATE] = value
+    order_i = lax.broadcasted_iota(jnp.int32, (rows, rows), 0)
+    order_j = lax.broadcasted_iota(jnp.int32, (rows, rows), 1)
+    tri = (order_i >= order_j).astype(jnp.float32)
+    lane = lax.broadcasted_iota(jnp.int32, (rows, 128), 1)
+    real = lane < heads
+    low = lane < HEAD_DIM
+    bias_dt, rates = head_rows[0:1, :], head_rows[1:2, :]
+    expand = (
+        lax.broadcasted_iota(jnp.int32, (128, chans), 0)
+        == lax.broadcasted_iota(jnp.int32, (128, chans), 1) // HEAD_DIM
+    ).astype(jnp.float32)
+    pick_row = lax.broadcasted_iota(jnp.int32, (8, 128), 0)
+    lanes_x, lanes_bc = chans // 128, 2 * STATE // 128
+
+    def conv(source, taps, base, count):
+        last = taps.shape[0] - 1
+        total = source[base + 8 : base + 8 + rows, :] * taps[last : last + 1, :]
+        for back in range(1, last + 1):
+            same = jnp.concatenate([masks[back - 1, base : base + rows, :]] * count, axis=1)
+            total = total + (
+                source[base + 8 - back : base + 8 - back + rows, :]
+                * taps[last - back : last - back + 1, :]
+                * same
+            )
+        return silu(total)
+
+    state = jnp.zeros((STATE, chans), jnp.float32)
+    for p in range(planes):
+        base = p * rows
+        span = slice(base, base + rows)
+        x_act = conv(x_all, taps_x, base, lanes_x)
+        bc_act = conv(bc_all, taps_bc, base, lanes_bc).astype(jnp.bfloat16)
+        keys, queries = bc_act[:, :STATE], bc_act[:, STATE:]
+        raw = dt_all[span, :] + bias_dt
+        delta = jnp.maximum(raw, 0.0) + jnp.log1p(jnp.exp(-jnp.abs(raw)))
+        delta = jnp.where(real, delta, 0.0)
+        cum = jnp.dot(tri, -rates * delta, precision=highest_, preferred_element_type=jnp.float32)
+        cum_t = cum.T
+        last = cum[rows - 1 : rows, :]
+        carried = jnp.where(real, jnp.exp(cum) * marks[0, span, :], 0.0)
+        ending = jnp.where(real, jnp.exp(last - cum) * marks[1, span, :] * delta, 0.0)
+        decay_end = jnp.where(pick_row == 0, jnp.exp(last) * keep[p : p + 1, :], head_rows[2:3, :])
+        decay_end = jnp.where(real[0:8], decay_end, 0.0)
+        spread = jnp.dot(
+            jnp.concatenate([delta, carried, ending, decay_end], axis=0),
+            expand,
+            precision=highest_,
+            preferred_element_type=jnp.float32,
+        )
+        delta_x = (spread[:rows] * x_act).astype(jnp.bfloat16)
+        end_x = (spread[2 * rows : 3 * rows] * x_act).astype(jnp.bfloat16)
+        scores = dot_nt(queries, keys)
+        from_state = jnp.dot(queries, state.astype(jnp.bfloat16), preferred_element_type=jnp.float32)
+        block_bias = bias[span, :]
+        outs = []
+        for pair in range(heads // 2):
+            both = delta_x[:, pair * 128 : (pair + 1) * 128]
+            part = []
+            for h in (2 * pair, 2 * pair + 1):
+                gap = cum[:, h : h + 1] - cum_t[h : h + 1, :]
+                mixing = (jnp.exp(gap + block_bias) * scores).astype(jnp.bfloat16)
+                part.append(jnp.dot(mixing, both, preferred_element_type=jnp.float32))
+            outs.append(jnp.where(low, part[0], part[1]))
+        y = jnp.concatenate(outs, axis=1)
+        y = y + spread[rows : 2 * rows] * from_state + spread[3 * rows + 1 : 3 * rows + 2] * x_act
+        gated = y * silu(z_all[span, :].astype(jnp.float32))
+        square_ref[p : p + 1, :] = dot_nt(
+            jnp.ones((8, chans), jnp.float32), gated * gated, precision=highest_
+        )[0:1, :]
+        gated_ref[span, :] = (gated * gain_ref[...].astype(jnp.float32)).astype(jnp.bfloat16)
+        if p + 1 < planes:
+            fresh = lax.dot_general(
+                keys, end_x, (((0,), (0,)), ((), ())), preferred_element_type=jnp.float32
+            )
+            state = spread[3 * rows : 3 * rows + 1] * state + fresh
+
+
+def scan_all(spots, xs, zs, dts, early, late, consts, heads):
+    planes = len(xs)
+    rows, chans = xs[0].shape
+    return pl.pallas_call(
+        functools.partial(scan_kernel, heads=heads, planes=planes),
+        out_shape=(
+            jax.ShapeDtypeStruct((planes * rows, chans), jnp.bfloat16),
+            jax.ShapeDtypeStruct((8, rows), jnp.float32),
+        ),
+        in_specs=[smem()] + [vmem()] * (3 * planes + 4 + len(consts)),
+        out_specs=(vmem(), vmem()),
+        scratch_shapes=[
+            pltpu.VMEM((planes * rows + 8, chans), jnp.float32),
+            pltpu.VMEM((planes * rows, chans), jnp.bfloat16),
+            pltpu.VMEM((planes * rows, 128), jnp.float32),
+            pltpu.VMEM((planes * rows + 8, 2 * STATE), jnp.float32),
+        ],
+        compiler_params=pltpu.CompilerParams(vmem_limit_bytes=VMEM_LIMIT),
+        cost_estimate=pl.CostEstimate(flops=1 << 30, bytes_accessed=8 << 20, transcendentals=0),
+        name="scan_all",
+    )(spots, *[near(v) for v in (*xs, *zs, *dts, *early, *late, *consts)])
+
+
+def out_kernel(spots, gated_ref, weight_ref, *refs, planes, first):
+    outs, (held, sems) = refs[:-2], refs[-2:]
+    tile = held.shape[2]
+    take = flow(
+        [weight_ref.at[:, pl.ds(first + i * tile, tile)] for i in range(held.shape[0])], held, sems, 3
+    )
+    rows = gated_ref.shape[0] // planes // PLANE
+    level, side = lax.div(spots[1], 2), lax.rem(spots[1], 2)
+    parts = []
+    for at_side in (1 - side, side):
+        for step in range(planes):
+            plane = lax.rem(spots[0] - 1 - step + planes, planes)
+            for at_level in (1 - level, level):
+                at = pl.multiple_of(((plane * 2 + at_level) * 2 + at_side) * rows, rows)
+                parts.append(gated_ref[pl.ds(at, rows), :])
+    left = jnp.concatenate(parts, axis=0)
+    for i in range(held.shape[0]):
+        take(i)
+        result = jnp.dot(left, held[i], preferred_element_type=jnp.float32).astype(jnp.bfloat16)
+        at = 0
+        for out in outs:
+            out[:, i * tile : (i + 1) * tile] = result[at : at + out.shape[0]]
+            at += out.shape[0]
+
+
+def out_part(spots, gated, weight, planes, first, width):
+    chans = weight.shape[0]
+    rows = gated.shape[0] // planes // PLANE
+    tile = 1024
+    shapes = [2 * rows] * planes + [rows] * (2 * planes)
+    outs = pl.pallas_call(
+        functools.partial(out_kernel, planes=planes, first=first),
+        out_shape=tuple(jax.ShapeDtypeStruct((high, width), jnp.bfloat16) for high in shapes),
+        in_specs=[smem(), vmem(), pl.BlockSpec(memory_space=pltpu.MemorySpace.HBM)],
+        out_specs=(vmem(),) * len(shapes),
+        scratch_shapes=[
+            pltpu.VMEM((width // tile, chans, tile), jnp.bfloat16),
+            pltpu.SemaphoreType.DMA((width // tile,)),
+        ],
+        compiler_params=pltpu.CompilerParams(vmem_limit_bytes=VMEM_LIMIT),
+        cost_estimate=pl.CostEstimate(flops=3 << 30, bytes_accessed=8 << 20, transcendentals=0),
+        name="out_part",
+    )(spots, near(gated), far(weight))
+    return outs[:planes], outs[planes::2], outs[planes + 1 :: 2]
+
+
+def pick_kernel(spots, *refs, pieces, step, planes, chained):
+    parts, out_ref = refs[: sum(pieces)], refs[-1]
+    width = out_ref.shape[1]
+    code = jnp.concatenate([ref[:, width:] for ref in parts], axis=0).astype(jnp.float32)
+    total = code.shape[0]
+    rows = total // PLANE
+    me = spots[0] * PLANE + spots[1]
+    match = code == me.astype(jnp.float32)
+    row = lax.broadcasted_iota(jnp.int32, (total, total), 0)
+    col = lax.broadcasted_iota(jnp.int32, (total, total), 1)
+    before = (row > col) & (row // rows == col // rows)
+    rank = jnp.dot(
+        before.astype(jnp.bfloat16), match.astype(jnp.bfloat16), preferred_element_type=jnp.float32
+    )
+    plane = lax.rem(spots[0] - step + planes, planes)
+    slot = ((plane * PLANE + (spots[1] ^ (row // rows))) * CAP).astype(jnp.float32) + rank
+    select = (match & (slot == col.astype(jnp.float32))).astype(jnp.float32)
+    select = select.T[: out_ref.shape[0]].astype(jnp.bfloat16)
+    tile = 1024
+    for at in range(0, width, tile):
+        raw = jnp.concatenate([ref[:, at : at + tile] for ref in parts], axis=0)
+        result = jnp.dot(select, raw, preferred_element_type=jnp.float32)
+        if chained:
+            result = result + refs[-2][:, at : at + tile].astype(jnp.float32)
+        out_ref[:, at : at + tile] = result.astype(jnp.bfloat16)
+
+
+def pick_plane(spots, blocks, earlier, slots, width, step, planes):
+    flat = [near(part) for block in blocks for part in block]
+    chain = [] if earlier is None else [near(earlier)]
+    return pl.pallas_call(
+        functools.partial(
+            pick_kernel,
+            pieces=tuple(len(block) for block in blocks),
+            step=step,
+            planes=planes,
+            chained=bool(chain),
+        ),
+        out_shape=jax.ShapeDtypeStruct((slots, width), jnp.bfloat16),
+        in_specs=[smem()] + [vmem()] * (len(flat) + len(chain)),
+        out_specs=vmem(),
+        compiler_params=pltpu.CompilerParams(vmem_limit_bytes=VMEM_LIMIT),
+        cost_estimate=pl.CostEstimate(flops=1 << 30, bytes_accessed=3 << 20, transcendentals=0),
+        name="pick_plane",
+    )(spots, *flat, *chain)
+
+
+def marks_kernel(col_ref, row_ref, masks_ref, bias_ref, marks_ref, keep_ref, padded, *, planes):
+    total = col_ref.shape[0]
+    rows = total // planes
+    col = col_ref[...]
+    padded[0:8, :] = jnp.full((8, 128), -1.0, jnp.float32)
+    padded[8:, :] = col
+    for back in range(1, masks_ref.shape[0] + 1):
+        masks_ref[back - 1] = (padded[8 - back : 8 - back + total, :] == col).astype(jnp.float32)
+    order = lax.broadcasted_iota(jnp.int32, (rows, rows), 0) >= lax.broadcasted_iota(
+        jnp.int32, (rows, rows), 1
+    )
+    keep_ref[...] = jnp.zeros(keep_ref.shape, jnp.float32)
+    for p in range(planes):
+        span = slice(p * rows, (p + 1) * rows)
+        block = col[span]
+        bias_ref[span, :] = jnp.where((block == row_ref[p : p + 1, :]) & order, 0.0, NEG)
+        previous = padded[p * rows + 7 : p * rows + 8, :]
+        final = block[rows - 1 : rows]
+        marks_ref[0, span, :] = (block == previous).astype(jnp.float32)
+        marks_ref[1, span, :] = (block == final).astype(jnp.float32)
+        keep_ref[p : p + 1, :] = (previous == final).astype(jnp.float32)
+
+
+def scan_constants(
+    segment_ids, conv_x, conv_bc, dt_bias, decay_rate, skip, norm_gain, z_pos, planes
+):
+    f32 = jnp.float32
+    heads = dt_bias.shape[0]
+    segment = segment_ids.reshape(-1).astype(f32)
+    total = segment.shape[0]
+    rows = total // planes
+    column = jnp.broadcast_to(segment[:, None], (total, 128))
+    lines = jnp.pad(segment.reshape(planes, rows), ((0, 8 - planes), (0, 0)))
+    back = conv_x.shape[1] - 1
+    masks, bias, marks, keep = pl.pallas_call(
+        functools.partial(marks_kernel, planes=planes),
+        out_shape=(
+            jax.ShapeDtypeStruct((back, total, 128), f32),
+            jax.ShapeDtypeStruct((total, rows), f32),
+            jax.ShapeDtypeStruct((2, total, 128), f32),
+            jax.ShapeDtypeStruct((8, 128), f32),
+        ),
+        in_specs=[vmem(), vmem()],
+        out_specs=(vmem(),) * 4,
+        scratch_shapes=[pltpu.VMEM((total + 8, 128), f32)],
+        compiler_params=pltpu.CompilerParams(vmem_limit_bytes=VMEM_LIMIT),
+        cost_estimate=pl.CostEstimate(flops=1 << 20, bytes_accessed=2 << 20, transcendentals=0),
+        name="scan_marks",
+    )(column, lines)
+    head_rows = jnp.pad(
+        jnp.stack([dt_bias, decay_rate, skip]).astype(f32), ((0, 5), (0, 128 - heads))
+    )
+    width_bc = GROUPS * STATE
+    taps_bc = jnp.concatenate(
+        [
+            lax.dynamic_slice_in_dim(conv_bc, z_pos * STATE + start, STATE, axis=0)
+            for start in (0, width_bc)
+        ],
+        axis=0,
+    )
+    return (
+        conv_x.astype(f32).T,
+        taps_bc.astype(f32).T,
+        masks,
+        bias,
+        marks,
+        keep,
+        head_rows,
+        norm_gain[None, :],
+    )
+
+
+def on_device_planes(
+    hidden,
+    pre_gain,
+    in_x,
+    in_z,
+    conv_x,
+    conv_bc,
+    bc_weight,
+    dt_weight,
+    dt_bias,
+    decay_rate,
+    skip,
+    norm_gain,
+    out_weight,
+    segment_ids,
+    destination,
+):
+    count = lax.axis_size("tensor")
+    planes = count // PLANE
+    me = lax.axis_index("tensor")
+    z_pos, spot = me // PLANE, me % PLANE
+    rows, width = hidden.shape
+    heads = dt_weight.shape[0]
+    every = range(count)
+    ring = [(t, (t + PLANE) % count) for t in every]
+    over_y = [(t, t ^ 2) for t in every]
+    over_core = [(t, t ^ 1) for t in every]
+
+    def permute(value, pairs):
+        return lax.ppermute(value, "tensor", pairs)
+
+    f32 = jnp.float32
+    small = jnp.concatenate(
+        [bc_weight, dt_weight, jnp.zeros((128 - heads, width), dt_weight.dtype)], axis=0
+    )
+    gain_row = pre_gain[None, :]
+    spots = jnp.stack([z_pos, spot]).astype(jnp.int32)
+
+    own = jnp.concatenate(
+        [hidden, jnp.broadcast_to(destination.astype(jnp.bfloat16), (rows, 128))], axis=1
+    )
+    half = rows // 2
+    straight, crossed = [[own]], []
+    straight_core, crossed_core = [], []
+    results = []
+    early = picked = None
+    spec = (segment_ids, conv_x, conv_bc, dt_bias, decay_rate, skip, norm_gain)
+
+    def exchange(piece):
+        other = permute(piece, over_core)
+        own_first = jnp.concatenate([piece, other], axis=1)
+        both = jnp.where(me % 2 == 0, own_first, jnp.concatenate([other, piece], axis=1))
+        result = []
+        for turn in range(2):
+            pairs = []
+            for t in every:
+                chip, side = t // 2, t % 2
+                kind, plane = chip // GROUPS, chip % GROUPS
+                pairs.append((t, plane * PLANE + (kind ^ turn) * 2 + side))
+            result.append(permute(both, pairs))
+        return result
+
+    def over(parts, pairs):
+        return [permute(part, pairs) for part in parts]
+
+    def blocks_of(step):
+        return [straight[step], straight_core[step], crossed[step], crossed_core[step]]
+
+    def compute(step):
+        return norm_plane(spots, blocks_of(step), gain_row, small)
+
+    def pick(step, earlier):
+        return pick_plane(spots, blocks_of(step), earlier, count * CAP, width, step, planes)
+
+    def own_slots(dest):
+        target = dest[:, 0]
+        onehot = (target[:, None] == jnp.arange(count, dtype=jnp.int32)[None, :]).astype(jnp.int32)
+        ranks = jnp.sum((jnp.cumsum(onehot, axis=0) - onehot) * onehot, axis=1)
+        slots = target * CAP + ranks
+        return (slots[None, :] == jnp.arange(count * CAP)[:, None]).astype(jnp.bfloat16)
+
+    for step in range(planes):
+        last = step + 1 == planes
+        group = [over(straight[step], over_core)]
+        if last:
+            group.append(
+                [permute(straight[step][0][:half], over_y), permute(crossed[step - 1][0][half:], ring)]
+            )
+        else:
+            group.append(over(straight[step], over_y))
+            group.append(over(straight[step], ring))
+        if step:
+            crossed_core.append(over(crossed[step - 1], over_core))
+        extra = {}
+        if step == 0:
+            extra["spec"] = (spec, destination)
+        else:
+            extra["result"] = compute(step - 1)
+            picked = pick(step - 1, picked)
+        if step == 1:
+            extra["consts"] = scan_constants(*spec, z_pos, planes)
+            extra["place"] = own_slots(own_dest)
+        if step == 2:
+            extra["first"] = project_planes([results[0][0], extra["result"][0]], in_x, in_z)
+        if last:
+            extra["early"] = exchange(
+                jnp.concatenate([result[1] for result in results[:2]], axis=0)
+            )
+        group, extra, picked = lax.optimization_barrier((group, extra, picked))
+        straight_core.append(group[0])
+        crossed.append(group[1])
+        if not last:
+            straight.append(group[2])
+        if step:
+            results.append(extra["result"])
+        else:
+            spec, own_dest = extra["spec"]
+        if step == 1:
+            consts, place = extra["consts"], extra["place"]
+        if step == 2:
+            first = extra["first"]
+        if last:
+            early = extra["early"]
+    crossed_core.append(over(crossed[-1], over_core))
+    results.append(compute(planes - 1))
+
+    normed, pieces, dts = zip(*results)
+    late = exchange(jnp.concatenate(pieces[2:], axis=0))
+    second = project_planes(normed[2:], in_x, in_z)
+    xs, zs = [first[i] + second[i] for i in range(2)]
+    gated, squares = scan_all(spots, xs, zs, dts, early, late, consts, heads)
+
+    squares = squares + permute(squares, over_core)
+    squares = squares + permute(squares, over_y)
+    scale = lax.rsqrt(squares[:planes].reshape(-1) / (INNER // GROUPS) + 1e-05)
+
+    parts = 2
+    part = width // parts
+    mine = [
+        lax.dynamic_slice_in_dim(scale, ((z_pos - 1 - step) % planes * PLANE + spot) * rows, rows)[:, None]
+        for step in range(planes)
+    ]
+    kept, got_y = [], []
+    for index in range(parts):
+        away, send, keep = out_part(spots, gated, out_weight, planes, index * part, part)
+        got = over(away, over_core)
+        send = [
+            (send[step].astype(f32) + got[step][:rows].astype(f32)).astype(jnp.bfloat16)
+            for step in range(planes)
+        ]
+        kept.append([(keep[step], got[step][rows:]) for step in range(planes)])
+        got_y.append(over(send, over_y))
+    travelling = [None] * parts
+    totals = [None] * parts
+    for step in range(planes):
+        for index in range(parts):
+            low, high = kept[index][step]
+            total = low.astype(f32) + high.astype(f32)
+            total = (total + got_y[index][step].astype(f32)) * mine[step]
+            if step:
+                total = total + travelling[index].astype(f32)
+            if step + 1 < planes:
+                travelling[index] = permute(total.astype(jnp.bfloat16), ring)
+            totals[index] = total
+        if step == 0:
+            picked, travelling[0] = lax.optimization_barrier((pick(planes - 1, picked), travelling[0]))
+    layer_out = (hidden.astype(f32) + jnp.concatenate(totals, axis=1)).astype(jnp.bfloat16)
+
+    filled = jnp.dot(place, layer_out, preferred_element_type=f32).astype(jnp.bfloat16)
+    received = lax.all_to_all(
+        filled.reshape(count, CAP, width), "tensor", split_axis=0, concat_axis=0, tiled=True
+    )
+    packed = jnp.concatenate([picked, received.reshape(count * CAP, width)], axis=1)
+    return (layer_out, packed)
+
+
 def solution(mesh):
+    planar = mesh.shape["dp"] == 1 and mesh.shape["tensor"] == PLANE * GROUPS
     return jax.shard_map(
-        on_device,
+        on_device_planes if planar else on_device,
         mesh=mesh,
         in_specs=(
             P(("rep", "dp", "tensor"), None),

time: 456 us -> 222 us (0.49)
  waiting for transfers between devices: 272 us -> 75.5 us
  matrix products: 67.8 us -> 0.27 us
  Pallas kernels: 0 us -> 63.2 us
  blocking collectives: 60.5 us -> 17.3 us
  starting transfers between devices: 0.3 us -> 36 us
  between operations: 14.1 us -> 1.76 us
  other arithmetic: 16.9 us -> 8.65 us
  loops' own time: 4.83 us -> 0 us
    reduce_scatter x1 -> x0, waiting for transfers between devices: 175 us -> none  [on_device(): lax.psum_scatter(jnp.dot(inner, proj_out, preferred_element_type=jnp.floa...]
    all_gather x2 -> x0, waiting for transfers between devices: 96.5 us -> none  [the longest x1 77.4 us: on_device(): tokens = lax.all_gather(normed, 'tensor', axis=0, tiled=True)]
    ppermute x0 -> x47, waiting for transfers between devices: none -> 75.5 us  [permute(): return lax.ppermute(value, 'tensor', pairs)]
    dot_general x25 -> x1, matrix products: 67.8 us -> 0.27 us  [on_device_planes(): jnp.dot(place, layer_out, preferred_element_type=f32).astype(jnp.bfloat16)]
    pallas_call x0 -> x14, Pallas kernels: none -> 63.2 us  [the longest x2 23.4 us: project_planes(): pl.pallas_call(functools.partial(project_kernel, planes=count), out_shape...]
    ppermute x0 -> x47, starting transfers between devices: none -> 36 us  [permute(): return lax.ppermute(value, 'tensor', pairs)]
    psum x1 -> x0, blocking collectives: 32.1 us -> none  [on_device(): total_sq = lax.psum(partial_sq, 'tensor')]
    all_to_all x1, blocking collectives: 28.4 us -> 17.3 us  [on_device_planes(): lax.all_to_all(filled.reshape(count, CAP, width), 'tensor', split_axis=0,...]
  transfers between devices with their start and end apart: 3 -> 47, of which waited for: 3 -> 18; matrix products, arithmetic and copies ran while one was open for 4% -> 4% of each run, Pallas kernels for 0% -> 24%
where the time goes in v2:
time: 222 us; the launch traced here: 218 us
  waiting for transfers between devices  75.5 us (34%)
  Pallas kernels  63.2 us (28%)
  starting transfers between devices  36 us (16%)
  blocking collectives  17.3 us (8%)
  local copies, waits for them, and re-layouts  15.2 us (7%)
  other arithmetic  8.65 us (4%)
    ppermute x47, waiting for transfers between devices, permute(): return lax.ppermute(value, 'tensor', pairs)  75.5 us
    ppermute x47, starting transfers between devices, permute(): return lax.ppermute(value, 'tensor', pairs)  36 us
    pallas_call x2, Pallas kernels, project_planes(): pl.pallas_call(functools.partial(project_kernel, planes=count), out_shape...  23.4 us
    all_to_all x1, blocking collectives, on_device_planes(): lax.all_to_all(filled.reshape(count, CAP, width), 'tensor', split_axis=0,...  17.3 us
    pallas_call x4, Pallas kernels, norm_plane(): pl.pallas_call(functools.partial(norm_kernel, pieces=tuple((len(block) fo...  14.9 us
    unnamed x86, local copies, waits for them, and re-layouts  11 us
    pallas_call x2, Pallas kernels, out_part(): pl.pallas_call(functools.partial(out_kernel, planes=planes, first=first),...  9.36 us
    pallas_call x4, Pallas kernels, pick_plane(): pl.pallas_call(functools.partial(pick_kernel, pieces=tuple((len(block) fo...  9.01 us
  transfers between devices with their start and end apart: 47, of which 18 were waited for; matrix products, arithmetic and copies ran while one was open for 4% of the time, Pallas kernels for 24%

profile of v2, /device:TPU:0, one launch (start us, length us, event | category | flops | bytes accessed | tf_op | source)
XLA Modules:
  0.0 217.9 jit_solution(6706259899441832350)
XLA Ops:
  9.8 9.6 %collective-permute-done.1.refs_2_ = bf16[32,8320]{1,0:T(8,128)(2,1)} collective-permute-done((bf16[32,8320]{1,0:T(8,128)(2,1)}, bf16[32,8320]{1,0:T(8,128)(2,1)}, u32[]{:S(2)}, u32[]{:S(2)}) %collective-permute-start.1) | collective-permute-done | bytes 532512 | tf_op jit(solution)/shard_map/ppermute | solution.py:683
  19.4 3.4 %collective-permute-done.2.refs_0_ = bf16[32,8320]{1,0:T(8,128)(2,1)} collective-permute-done((bf16[32,8320]{1,0:T(8,128)(2,1)}, bf16[32,8320]{1,0:T(8,128)(2,1)}, u32[]{:S(2)}, u32[]{:S(2)}) %collective-permute-start.2) | collective-permute-done | bytes 532512 | tf_op jit(solution)/shard_map/ppermute | solution.py:683
  29.5 3.8 %norm_plane.4 = (bf16[128,8192]{1,0:T(8,128)(2,1)S(1)}, bf16[128,64]{1,0:T(8,128)(2,1)S(1)}, f32[128,128]{1,0:T(8,128)S(1)}) custom-call(s32[2]{0:T(128)S(1)} %pad_add_fusion.spot_ref.spots, bf16[32,8320]{1,0:T(8,128)(2,1)} %pad_maximum_fusion.1.refs_0_, bf16[32,8320]{1,0:T(8,128)(2,1)} %collective-permute-done.refs_1_, ...), custom_call_target="tpu_custom_call" | custom-call | flops 2147483648 | bytes 6291456 | tf_op jit(solution)/shard_map/norm_plane/pallas_call | solution.py:269
  33.3 4.2 %collective-permute-done.4.refs_2_ = bf16[32,8320]{1,0:T(8,128)(2,1)} collective-permute-done((bf16[32,8320]{1,0:T(8,128)(2,1)}, bf16[32,8320]{1,0:T(8,128)(2,1)}, u32[]{:S(2)}, u32[]{:S(2)}) %collective-permute-start.4) | collective-permute-done | bytes 532512 | tf_op jit(solution)/shard_map/ppermute | solution.py:683
  42.2 3.6 %norm_plane.5 = (bf16[128,8192]{1,0:T(8,128)(2,1)S(1)}, bf16[128,64]{1,0:T(8,128)(2,1)S(1)}, f32[128,128]{1,0:T(8,128)S(1)}) custom-call(s32[2]{0:T(128)S(1)} %pad_add_fusion.spot_ref.spots, bf16[32,8320]{1,0:T(8,128)(2,1)} %collective-permute-done.2.refs_0_, bf16[32,8320]{1,0:T(8,128)(2,1)} %collective-permute-done.3.refs_1_, ...), custom_call_target="tpu_custom_call" | custom-call | flops 2147483648 | bytes 6291456 | tf_op jit(solution)/shard_map/norm_plane/pallas_call | solution.py:269
  48.7 11.7 %project_planes.2 = (bf16[128,512]{1,0:T(8,128)(2,1)S(1)}, bf16[128,512]{1,0:T(8,128)(2,1)S(1)}, bf16[128,512]{1,0:T(8,128)(2,1)S(1)}, bf16[128,512]{1,0:T(8,128)(2,1)S(1)}) custom-call(bf16[128,8192]{1,0:T(8,128)(2,1)S(1)} %get-tuple-element.119.refs_0_, bf16[128,8192]{1,0:T(8,128)(2,1)S(1)} %get-tuple-element.122.refs_1_, bf16[512,8192]{1,0:T(8,128)(2,1)} %refs_2_.3, ...), custom_call_target="tpu_custom_call" | custom-call | flops 6442450944 | bytes 16777216 | tf_op jit(solution)/shard_map/project_planes/pallas_call | solution.py:331
  70.5 3.2 %collective-permute-start.16 = (bf16[256,128]{1,0:T(8,128)(2,1)S(1)}, bf16[256,128]{1,0:T(8,128)(2,1)S(1)}, u32[]{:S(2)}, u32[]{:S(2)}) collective-permute-start(bf16[256,128]{1,0:T(8,128)(2,1)S(1)} %maximum_select_fusion), channel_id=1, source_target_pairs={{0,2},{1,3},{2,6},{3,7},{4,10},{5,11},{6,14},{7,15},{8,0},{9,1},{1... | collective-permute-start | bytes 196616 | tf_op jit(solution)/shard_map/ppermute | solution.py:683
  74.7 3.7 %norm_plane.6 = (bf16[128,8192]{1,0:T(8,128)(2,1)S(1)}, bf16[128,64]{1,0:T(8,128)(2,1)S(1)}, f32[128,128]{1,0:T(8,128)S(1)}) custom-call(s32[2]{0:T(128)S(1)} %pad_add_fusion.spot_ref.spots, bf16[32,8320]{1,0:T(8,128)(2,1)} %collective-permute-done.5.refs_0_, bf16[32,8320]{1,0:T(8,128)(2,1)S(1)} %copy-done.3, ...), custom_call_target="tpu_custom_call" | custom-call | flops 2147483648 | bytes 6291456 | tf_op jit(solution)/shard_map/norm_plane/pallas_call | solution.py:269
  79.1 2.8 %pick_plane.6.refs_6_ = bf16[32,8192]{1,0:T(8,128)(2,1)S(1)} custom-call(s32[2]{0:T(128)S(1)} %pad_add_fusion.spot_ref.spots, bf16[32,8320]{1,0:T(8,128)(2,1)} %collective-permute-done.5.refs_0_, bf16[32,8320]{1,0:T(8,128)(2,1)S(1)} %copy-done.3, bf16[32,8320]{1,0:T(8,128)(2,1)} %collective-permute-done.8.refs_2_, ...), custom_call_target="tpu_custom_call" | custom-call | flops 1073741824 | bytes 3145728 | tf_op jit(solution)/shard_map/pick_plane/pallas_call | solution.py:565
  86.3 3.7 %norm_plane.7 = (bf16[128,8192]{1,0:T(8,128)(2,1)S(1)}, bf16[128,64]{1,0:T(8,128)(2,1)S(1)}, f32[128,128]{1,0:T(8,128)S(1)}) custom-call(s32[2]{0:T(128)S(1)} %pad_add_fusion.spot_ref.spots, bf16[32,8320]{1,0:T(8,128)(2,1)} %collective-permute-done.9.refs_0_, bf16[32,8320]{1,0:T(8,128)(2,1)} %collective-permute-done.11.refs_1_, ...), custom_call_target="tpu_custom_call" | custom-call | flops 2147483648 | bytes 6291456 | tf_op jit(solution)/shard_map/norm_plane/pallas_call | solution.py:269
  90.3 11.7 %project_planes.3 = (bf16[128,512]{1,0:T(8,128)(2,1)S(1)}, bf16[128,512]{1,0:T(8,128)(2,1)S(1)}, bf16[128,512]{1,0:T(8,128)(2,1)S(1)}, bf16[128,512]{1,0:T(8,128)(2,1)S(1)}) custom-call(bf16[128,8192]{1,0:T(8,128)(2,1)S(1)} %copy-done.17, bf16[128,8192]{1,0:T(8,128)(2,1)S(1)} %get-tuple-element.145.refs_1_, bf16[512,8192]{1,0:T(8,128)(2,1)} %refs_2_.3, ...), custom_call_target="tpu_custom_call" | custom-call | flops 6442450944 | bytes 16777216 | tf_op jit(solution)/shard_map/project_planes/pallas_call | solution.py:331
  103.1 6.4 %collective-permute-start.22 = (bf16[256,128]{1,0:T(8,128)(2,1)S(1)}, bf16[256,128]{1,0:T(8,128)(2,1)S(1)}, u32[]{:S(2)}, u32[]{:S(2)}) collective-permute-start(bf16[256,128]{1,0:T(8,128)(2,1)S(1)} %maximum_select_fusion.1), channel_id=1, source_target_pairs={{0,2},{1,3},{2,6},{3,7},{4,10},{5,11},{6,14},{7,15},{8,0},{9,1},{1... | collective-permute-start | bytes 196616 | tf_op jit(solution)/shard_map/ppermute | solution.py:683
  111.5 2.9 %collective-permute-done.22.refs_15_ = bf16[256,128]{1,0:T(8,128)(2,1)S(1)} collective-permute-done((bf16[256,128]{1,0:T(8,128)(2,1)S(1)}, bf16[256,128]{1,0:T(8,128)(2,1)S(1)}, u32[]{:S(2)}, u32[]{:S(2)}) %collective-permute-start.22) | collective-permute-done | bytes 65568 | tf_op jit(solution)/shard_map/ppermute | solution.py:683
  114.5 6.4 %scan_all.1 = (bf16[512,512]{1,0:T(8,128)(2,1)S(1)}, f32[8,128]{1,0:T(8,128)S(1)}) custom-call(s32[2]{0:T(128)S(1)} %pad_add_fusion.spot_ref.spots, bf16[128,512]{1,0:T(8,128)(2,1)S(1)} %copy-done.19, bf16[128,512]{1,0:T(8,128)(2,1)S(1)} %copy-done.23, bf16[128,512]{1,0:T(8,128)(2,1)S(1)} %get-tuple-element.146.refs_2_, ...), custom_call_target="tpu_custom_call" | custom-call | flops 1073741824 | bytes 8388608 | tf_op jit(solution)/shard_map/scan_all/pallas_call | solution.py:469
  121.0 4.7 %out_part.3 = (bf16[64,4096]{1,0:T(8,128)(2,1)S(1)}, bf16[64,4096]{1,0:T(8,128)(2,1)S(1)}, bf16[64,4096]{1,0:T(8,128)(2,1)S(1)}, bf16[64,4096]{1,0:T(8,128)(2,1)...) custom-call(s32[2]{0:T(128)S(1)} %pad_add_fusion.spot_ref.spots, ...), custom_call_target="tpu_custom_call" | custom-call | flops 3221225472 | bytes 8388608 | tf_op jit(solution)/shard_map/out_part/pallas_call | solution.py:519
  126.9 4.7 %out_part.2 = (bf16[64,4096]{1,0:T(8,128)(2,1)S(1)}, bf16[64,4096]{1,0:T(8,128)(2,1)S(1)}, bf16[64,4096]{1,0:T(8,128)(2,1)S(1)}, bf16[64,4096]{1,0:T(8,128)(2,1)...) custom-call(s32[2]{0:T(128)S(1)} %pad_add_fusion.spot_ref.spots, ...), custom_call_target="tpu_custom_call" | custom-call | flops 3221225472 | bytes 8388608 | tf_op jit(solution)/shard_map/out_part/pallas_call | solution.py:519
  141.0 11.0 %collective-permute-done.43 = bf16[32,4096]{1,0:T(8,128)(2,1)S(1)} collective-permute-done((bf16[32,4096]{1,0:T(8,128)(2,1)S(1)}, bf16[32,4096]{1,0:T(8,128)(2,1)S(1)}, u32[]{:S(2)}, u32[]{:S(2)}) %collective-permute-start.43) | collective-permute-done | bytes 262176 | tf_op jit(solution)/shard_map/ppermute | solution.py:683
  153.4 4.3 %collective-permute-done.32 = bf16[32,4096]{1,0:T(8,128)(2,1)S(1)} collective-permute-done((bf16[32,4096]{1,0:T(8,128)(2,1)S(1)}, bf16[32,4096]{1,0:T(8,128)(2,1)S(1)}, u32[]{:S(2)}, u32[]{:S(2)}) %collective-permute-start.32) | collective-permute-done | bytes 262176 | tf_op jit(solution)/shard_map/ppermute | solution.py:683
  160.1 9.0 %collective-permute-done.33 = bf16[32,4096]{1,0:T(8,128)(2,1)S(1)} collective-permute-done((bf16[32,4096]{1,0:T(8,128)(2,1)S(1)}, bf16[32,4096]{1,0:T(8,128)(2,1)S(1)}, u32[]{:S(2)}, u32[]{:S(2)}) %collective-permute-start.33) | collective-permute-done | bytes 262176 | tf_op jit(solution)/shard_map/ppermute | solution.py:683
  173.0 10.6 %collective-permute-done.39 = bf16[32,4096]{1,0:T(8,128)(2,1)S(1)} collective-permute-done((bf16[32,4096]{1,0:T(8,128)(2,1)S(1)}, bf16[32,4096]{1,0:T(8,128)(2,1)S(1)}, u32[]{:S(2)}, u32[]{:S(2)}) %collective-permute-start.39) | collective-permute-done | bytes 262176 | tf_op jit(solution)/shard_map/ppermute | solution.py:683
  186.8 3.1 %collective-permute-done.24 = bf16[32,4096]{1,0:T(8,128)(2,1)S(1)} collective-permute-done((bf16[32,4096]{1,0:T(8,128)(2,1)S(1)}, bf16[32,4096]{1,0:T(8,128)(2,1)S(1)}, u32[]{:S(2)}, u32[]{:S(2)}) %collective-permute-start.24) | collective-permute-done | bytes 262176 | tf_op jit(solution)/shard_map/ppermute | solution.py:683
  189.9 5.4 %collective-permute-done.35 = bf16[32,4096]{1,0:T(8,128)(2,1)S(1)} collective-permute-done((bf16[32,4096]{1,0:T(8,128)(2,1)S(1)}, bf16[32,4096]{1,0:T(8,128)(2,1)S(1)}, u32[]{:S(2)}, u32[]{:S(2)}) %collective-permute-start.35) | collective-permute-done | bytes 262176 | tf_op jit(solution)/shard_map/ppermute | solution.py:683
  195.3 2.8 %collective-permute-done.46 = bf16[32,4096]{1,0:T(8,128)(2,1)S(1)} collective-permute-done((bf16[32,4096]{1,0:T(8,128)(2,1)S(1)}, bf16[32,4096]{1,0:T(8,128)(2,1)S(1)}, u32[]{:S(2)}, u32[]{:S(2)}) %collective-permute-start.46) | collective-permute-done | bytes 262176 | tf_op jit(solution)/shard_map/ppermute | solution.py:683
  199.1 17.3 %all_to_all.5 = bf16[16,2,8192]{2,1,0:T(2,128)(2,1)S(1)} all-to-all(bf16[16,2,8192]{2,1,0:T(2,128)(2,1)S(1)} %reshape.38), channel_id=1, replica_groups=mesh['rep'=2,'dp'=1,'tensor'=16] {'tensor'}, dimensions={0} | all-to-all | bytes 1048576 | tf_op jit(solution)/shard_map/all_to_all | solution.py:823
  (219 shorter events, 66.3 us)
Async XLA Ops:
  3.8 15.6 %collective-permute-start.1 = (bf16[32,8320]{1,0:T(8,128)(2,1)}, bf16[32,8320]{1,0:T(8,128)(2,1)}, u32[]{:S(2)}, u32[]{:S(2)}) collective-permute-start(bf16[32,8320]{1,0:T(8,128)(2,1)} %pad_maximum_fusion.1.refs_0_), channel_id=1, source_target_pairs={{0,2},{1,3},{2,0},{3,1},{4,6},{5,7},{6,4},{7,5},{8,10},{9,11},{10,... | collective-permute-start | bytes 1597448 | tf_op jit(solution)/shard_map/ppermute | solution.py:683
  6.3 16.4 %collective-permute-start.2 = (bf16[32,8320]{1,0:T(8,128)(2,1)}, bf16[32,8320]{1,0:T(8,128)(2,1)}, u32[]{:S(2)}, u32[]{:S(2)}) collective-permute-start(bf16[32,8320]{1,0:T(8,128)(2,1)} %pad_maximum_fusion.1.refs_0_), channel_id=1, source_target_pairs={{0,4},{1,5},{2,6},{3,7},{4,8},{5,9},{6,10},{7,11},{8,12},{9,13},{1... | collective-permute-start | bytes 1597448 | tf_op jit(solution)/shard_map/ppermute | solution.py:683
  22.8 14.8 %collective-permute-start.4 = (bf16[32,8320]{1,0:T(8,128)(2,1)}, bf16[32,8320]{1,0:T(8,128)(2,1)}, u32[]{:S(2)}, u32[]{:S(2)}) collective-permute-start(bf16[32,8320]{1,0:T(8,128)(2,1)} %collective-permute-done.2.refs_0_), channel_id=1, source_target_pairs={{0,2},{1,3},{2,0},{3,1},{4,6},{5,7},{6,4},{7,5},{8,10},{9,11},{10,... | collective-permute-start | bytes 1597448 | tf_op jit(solution)/shard_map/ppermute | solution.py:683
  23.3 16.3 %collective-permute-start.5 = (bf16[32,8320]{1,0:T(8,128)(2,1)}, bf16[32,8320]{1,0:T(8,128)(2,1)}, u32[]{:S(2)}, u32[]{:S(2)}) collective-permute-start(bf16[32,8320]{1,0:T(8,128)(2,1)} %collective-permute-done.2.refs_0_), channel_id=1, source_target_pairs={{0,4},{1,5},{2,6},{3,7},{4,8},{5,9},{6,10},{7,11},{8,12},{9,13},{1... | collective-permute-start | bytes 1597448 | tf_op jit(solution)/shard_map/ppermute | solution.py:683
  39.6 23.3 %collective-permute-start.7 = (bf16[32,8320]{1,0:T(8,128)(2,1)}, bf16[32,8320]{1,0:T(8,128)(2,1)S(1)}, u32[]{:S(2)}, u32[]{:S(2)}) collective-permute-start(bf16[32,8320]{1,0:T(8,128)(2,1)} %collective-permute-done.5.refs_0_), channel_id=1, source_target_pairs={{0,1},{1,0},{2,3},{3,2},{4,5},{5,4},{6,7},{7,6},{8,9},{9,8},{10,11... | collective-permute-start | bytes 1597448 | tf_op jit(solution)/shard_map/ppermute | solution.py:683
  40.1 23.6 %collective-permute-start.8 = (bf16[32,8320]{1,0:T(8,128)(2,1)}, bf16[32,8320]{1,0:T(8,128)(2,1)}, u32[]{:S(2)}, u32[]{:S(2)}) collective-permute-start(bf16[32,8320]{1,0:T(8,128)(2,1)} %collective-permute-done.5.refs_0_), channel_id=1, source_target_pairs={{0,2},{1,3},{2,0},{3,1},{4,6},{5,7},{6,4},{7,5},{8,10},{9,11},{10,... | collective-permute-start | bytes 1597448 | tf_op jit(solution)/shard_map/ppermute | solution.py:683
  41.6 22.1 %collective-permute-start.9 = (bf16[32,8320]{1,0:T(8,128)(2,1)}, bf16[32,8320]{1,0:T(8,128)(2,1)}, u32[]{:S(2)}, u32[]{:S(2)}) collective-permute-start(bf16[32,8320]{1,0:T(8,128)(2,1)} %collective-permute-done.5.refs_0_), channel_id=1, source_target_pairs={{0,4},{1,5},{2,6},{3,7},{4,8},{5,9},{6,10},{7,11},{8,12},{9,13},{1... | collective-permute-start | bytes 1597448 | tf_op jit(solution)/shard_map/ppermute | solution.py:683
  64.4 19.6 %collective-permute-start.11 = (bf16[32,8320]{1,0:T(8,128)(2,1)}, bf16[32,8320]{1,0:T(8,128)(2,1)}, u32[]{:S(2)}, u32[]{:S(2)}) collective-permute-start(bf16[32,8320]{1,0:T(8,128)(2,1)} %collective-permute-done.9.refs_0_), channel_id=1, source_target_pairs={{0,1},{1,0},{2,3},{3,2},{4,5},{5,4},{6,7},{7,6},{8,9},{9,8},{10,11... | collective-permute-start | bytes 1597448 | tf_op jit(solution)/shard_map/ppermute | solution.py:683
  67.4 16.5 %collective-permute-start.12 = (bf16[16,8320]{1,0:T(8,128)(2,1)S(1)}, bf16[16,8320]{1,0:T(8,128)(2,1)S(1)}, u32[]{:S(2)}, u32[]{:S(2)}) collective-permute-start(bf16[16,8320]{1,0:T(8,128)(2,1)S(1)} %slice.57), channel_id=1, source_target_pairs={{0,2},{1,3},{2,0},{3,1},{4,6},{5,7},{6,4},{7,5},{8,10},{9,11},{10,... | collective-permute-start | bytes 798728 | tf_op jit(solution)/shard_map/ppermute | solution.py:683
  68.7 15.3 %collective-permute-start.13 = (bf16[16,8320]{1,0:T(8,128)(2,1)S(1)}, bf16[16,8320]{1,0:T(8,128)(2,1)}, u32[]{:S(2)}, u32[]{:S(2)}) collective-permute-start(bf16[16,8320]{1,0:T(8,128)(2,1)S(1)} %slice.58), channel_id=1, source_target_pairs={{0,4},{1,5},{2,6},{3,7},{4,8},{5,9},{6,10},{7,11},{8,12},{9,13},{1... | collective-permute-start | bytes 798728 | tf_op jit(solution)/shard_map/ppermute | solution.py:683
  69.8 12.9 %collective-permute-start.15 = (bf16[256,128]{1,0:T(8,128)(2,1)S(1)}, bf16[256,128]{1,0:T(8,128)(2,1)S(1)}, u32[]{:S(2)}, u32[]{:S(2)}) collective-permute-start(bf16[256,128]{1,0:T(8,128)(2,1)S(1)} %maximum_select_fusion), channel_id=1, source_target_pairs={{0,0},{1,1},{2,4},{3,5},{4,8},{5,9},{6,12},{7,13},{8,2},{9,3},{10,... | collective-permute-start | bytes 196616 | tf_op jit(solution)/shard_map/ppermute | solution.py:683
  70.5 12.9 %collective-permute-start.16 = (bf16[256,128]{1,0:T(8,128)(2,1)S(1)}, bf16[256,128]{1,0:T(8,128)(2,1)S(1)}, u32[]{:S(2)}, u32[]{:S(2)}) collective-permute-start(bf16[256,128]{1,0:T(8,128)(2,1)S(1)} %maximum_select_fusion), channel_id=1, source_target_pairs={{0,2},{1,3},{2,6},{3,7},{4,10},{5,11},{6,14},{7,15},{8,0},{9,1},{1... | collective-permute-start | bytes 196616 | tf_op jit(solution)/shard_map/ppermute | solution.py:683
  131.6 41.2 %collective-permute-start.23 = (bf16[64,4096]{1,0:T(8,128)(2,1)S(1)}, bf16[64,4096]{1,0:T(8,128)(2,1)S(1)}, u32[]{:S(2)}, u32[]{:S(2)}) collective-permute-start(bf16[64,4096]{1,0:T(8,128)(2,1)S(1)} %get-tuple-element.170), channel_id=1, source_target_pairs={{0,1},{1,0},{2,3},{3,2},{4,5},{5,4},{6,7},{7,6},{8,9},{9,8},{10,11... | collective-permute-start | bytes 1572872 | tf_op jit(solution)/shard_map/ppermute | solution.py:683
  132.2 25.9 %collective-permute-start.27 = (bf16[64,4096]{1,0:T(8,128)(2,1)S(1)}, bf16[64,4096]{1,0:T(8,128)(2,1)S(1)}, u32[]{:S(2)}, u32[]{:S(2)}) collective-permute-start(bf16[64,4096]{1,0:T(8,128)(2,1)S(1)} %get-tuple-element.174), channel_id=1, source_target_pairs={{0,1},{1,0},{2,3},{3,2},{4,5},{5,4},{6,7},{7,6},{8,9},{9,8},{10,11... | collective-permute-start | bytes 1572872 | tf_op jit(solution)/shard_map/ppermute | solution.py:683
  137.3 33.1 %collective-permute-start.41 = (bf16[32,4096]{1,0:T(8,128)(2,1)S(1)}, bf16[32,4096]{1,0:T(8,128)(2,1)S(1)}, u32[]{:S(2)}, u32[]{:S(2)}) collective-permute-start(bf16[32,4096]{1,0:T(8,128)(2,1)S(1)} %add_convert_fusion.3), channel_id=1, source_target_pairs={{0,2},{1,3},{2,0},{3,1},{4,6},{5,7},{6,4},{7,5},{8,10},{9,11},{10,... | collective-permute-start | bytes 786440 | tf_op jit(solution)/shard_map/ppermute | solution.py:683
  138.7 13.3 %collective-permute-start.43 = (bf16[32,4096]{1,0:T(8,128)(2,1)S(1)}, bf16[32,4096]{1,0:T(8,128)(2,1)S(1)}, u32[]{:S(2)}, u32[]{:S(2)}) collective-permute-start(bf16[32,4096]{1,0:T(8,128)(2,1)S(1)} %add_convert_fusion.2), channel_id=1, source_target_pairs={{0,2},{1,3},{2,0},{3,1},{4,6},{5,7},{6,4},{7,5},{8,10},{9,11},{10,... | collective-permute-start | bytes 786440 | tf_op jit(solution)/shard_map/ppermute | solution.py:683
  139.6 18.1 %collective-permute-start.32 = (bf16[32,4096]{1,0:T(8,128)(2,1)S(1)}, bf16[32,4096]{1,0:T(8,128)(2,1)S(1)}, u32[]{:S(2)}, u32[]{:S(2)}) collective-permute-start(bf16[32,4096]{1,0:T(8,128)(2,1)S(1)} %add_convert_fusion.8), channel_id=1, source_target_pairs={{0,2},{1,3},{2,0},{3,1},{4,6},{5,7},{6,4},{7,5},{8,10},{9,11},{10,... | collective-permute-start | bytes 786440 | tf_op jit(solution)/shard_map/ppermute | solution.py:683
  152.1 19.0 %collective-permute-start.30 = (bf16[32,4096]{1,0:T(8,128)(2,1)S(1)}, bf16[32,4096]{1,0:T(8,128)(2,1)S(1)}, u32[]{:S(2)}, u32[]{:S(2)}) collective-permute-start(bf16[32,4096]{1,0:T(8,128)(2,1)S(1)} %add_convert_fusion.9), channel_id=1, source_target_pairs={{0,2},{1,3},{2,0},{3,1},{4,6},{5,7},{6,4},{7,5},{8,10},{9,11},{10,... | collective-permute-start | bytes 786440 | tf_op jit(solution)/shard_map/ppermute | solution.py:683
  158.1 14.4 %collective-permute-start.44 = (bf16[32,4096]{1,0:T(8,128)(2,1)S(1)}, bf16[32,4096]{1,0:T(8,128)(2,1)S(1)}, u32[]{:S(2)}, u32[]{:S(2)}) collective-permute-start(bf16[32,4096]{1,0:T(8,128)(2,1)S(1)} %get-tuple-element.211), channel_id=1, source_target_pairs={{0,4},{1,5},{2,6},{3,7},{4,8},{5,9},{6,10},{7,11},{8,12},{9,13},{1... | collective-permute-start | bytes 786440 | tf_op jit(solution)/shard_map/ppermute | solution.py:683
  169.0 17.8 %collective-permute-start.37 = (bf16[32,4096]{1,0:T(8,128)(2,1)S(1)}, bf16[32,4096]{1,0:T(8,128)(2,1)S(1)}, u32[]{:S(2)}, u32[]{:S(2)}) collective-permute-start(bf16[32,4096]{1,0:T(8,128)(2,1)S(1)} %add_convert_fusion.5), channel_id=1, source_target_pairs={{0,2},{1,3},{2,0},{3,1},{4,6},{5,7},{6,4},{7,5},{8,10},{9,11},{10,... | collective-permute-start | bytes 786440 | tf_op jit(solution)/shard_map/ppermute | solution.py:683
  170.4 13.2 %collective-permute-start.39 = (bf16[32,4096]{1,0:T(8,128)(2,1)S(1)}, bf16[32,4096]{1,0:T(8,128)(2,1)S(1)}, u32[]{:S(2)}, u32[]{:S(2)}) collective-permute-start(bf16[32,4096]{1,0:T(8,128)(2,1)S(1)} %add_convert_fusion.4), channel_id=1, source_target_pairs={{0,2},{1,3},{2,0},{3,1},{4,6},{5,7},{6,4},{7,5},{8,10},{9,11},{10,... | collective-permute-start | bytes 786440 | tf_op jit(solution)/shard_map/ppermute | solution.py:683
  171.1 15.3 %collective-permute-start.28 = (bf16[32,4096]{1,0:T(8,128)(2,1)S(1)}, bf16[32,4096]{1,0:T(8,128)(2,1)S(1)}, u32[]{:S(2)}, u32[]{:S(2)}) collective-permute-start(bf16[32,4096]{1,0:T(8,128)(2,1)S(1)} %add_convert_fusion.10), channel_id=1, source_target_pairs={{0,2},{1,3},{2,0},{3,1},{4,6},{5,7},{6,4},{7,5},{8,10},{9,11},{10,... | collective-permute-start | bytes 786440 | tf_op jit(solution)/shard_map/ppermute | solution.py:683
  172.7 13.6 %collective-permute-start.34 = (bf16[32,4096]{1,0:T(8,128)(2,1)S(1)}, bf16[32,4096]{1,0:T(8,128)(2,1)S(1)}, u32[]{:S(2)}, u32[]{:S(2)}) collective-permute-start(bf16[32,4096]{1,0:T(8,128)(2,1)S(1)} %get-tuple-element.208), channel_id=1, source_target_pairs={{0,4},{1,5},{2,6},{3,7},{4,8},{5,9},{6,10},{7,11},{8,12},{9,13},{1... | collective-permute-start | bytes 786440 | tf_op jit(solution)/shard_map/ppermute | solution.py:683
  172.8 13.6 %collective-permute-start.45 = (bf16[32,4096]{1,0:T(8,128)(2,1)S(1)}, bf16[32,4096]{1,0:T(8,128)(2,1)S(1)}, u32[]{:S(2)}, u32[]{:S(2)}) collective-permute-start(bf16[32,4096]{1,0:T(8,128)(2,1)S(1)} %get-tuple-element.209), channel_id=1, source_target_pairs={{0,4},{1,5},{2,6},{3,7},{4,8},{5,9},{6,10},{7,11},{8,12},{9,13},{1... | collective-permute-start | bytes 786440 | tf_op jit(solution)/shard_map/ppermute | solution.py:683
  (65 other events, 588.4 us)

commit v3 on v2

--- a/solution.py
+++ b/solution.py
@@ -205,8 +205,7 @@
 
 
 PLANE = 4
-VMEM_LIMIT = 16 * 1024 * 1024
-WEIGHT_LIMIT = 28 * 1024 * 1024
+VMEM_LIMIT = 9 * 1024 * 1024
 NEG = -1e30
 
 
@@ -232,8 +231,15 @@
     )
 
 
-def norm_kernel(spot_ref, *refs, pieces):
-    gain_ref, small_ref, normed_ref, bc_ref, dt_ref = refs[sum(pieces) :]
+def norm_kernel(spot_ref, *refs, pieces, held):
+    gain_ref, small_ref, *rest = refs[sum(pieces) :]
+    weights, (normed_ref, bc_ref, dt_ref) = rest[:held], rest[held : held + 3]
+    copies = [
+        pltpu.make_async_copy(weight, rest[held + 3 + i], rest[-1].at[i])
+        for i, weight in enumerate(weights)
+    ]
+    for copy in copies:
+        copy.start()
     width = gain_ref.shape[1]
     step = 1024
     taken = 0
@@ -261,89 +267,66 @@
     half = bc_ref.shape[1]
     bc_ref[...] = result[:, :half]
     dt_ref[...] = result[:, half:].astype(jnp.float32)
-
-
-def norm_plane(spots, blocks, gain, small):
+    for copy in copies:
+        copy.wait()
+
+
+def norm_plane(spots, blocks, gain, small, late, weights):
     rows, width = blocks[0][0].shape[0] * PLANE, gain.shape[1]
     flat = [near(part) for block in blocks for part in block]
     return pl.pallas_call(
-        functools.partial(norm_kernel, pieces=tuple(len(block) for block in blocks)),
+        functools.partial(
+            norm_kernel, pieces=tuple(len(block) for block in blocks), held=len(weights)
+        ),
         out_shape=(
-            jax.ShapeDtypeStruct((rows, width), jnp.bfloat16),
+            (pltpu.VMEM if late else jax.ShapeDtypeStruct)((rows, width), jnp.bfloat16),
             jax.ShapeDtypeStruct((rows, small.shape[0] - 128), jnp.bfloat16),
             jax.ShapeDtypeStruct((rows, 128), jnp.float32),
+            *[pltpu.VMEM(weight.shape, weight.dtype) for weight in weights],
         ),
-        in_specs=[smem()] + [vmem()] * (len(flat) + 2),
-        out_specs=(vmem(), vmem(), vmem()),
+        in_specs=[smem()]
+        + [vmem()] * (len(flat) + 2)
+        + [pl.BlockSpec(memory_space=pltpu.MemorySpace.HBM)] * len(weights),
+        out_specs=(vmem(),) * (3 + len(weights)),
+        scratch_shapes=[pltpu.SemaphoreType.DMA((len(weights),))] if weights else [],
         compiler_params=pltpu.CompilerParams(vmem_limit_bytes=VMEM_LIMIT),
         cost_estimate=pl.CostEstimate(
             flops=1 << 31, bytes_accessed=6 << 20, transcendentals=0
         ),
         name="norm_plane",
-    )(spots, *flat, near(gain), near(small))
-
-
-def flow(sources, held, sems, ahead):
-    copies = [
-        pltpu.make_async_copy(source, held.at[i], sems.at[i]) for i, source in enumerate(sources)
-    ]
-    for copy in copies[:ahead]:
-        copy.start()
-
-    def take(i):
-        copies[i].wait()
-        if i + ahead < len(copies):
-            copies[i + ahead].start()
-
-    return take
+    )(spots, *flat, near(gain), near(small), *[far(weight) for weight in weights])
 
 
 def project_kernel(*refs, planes):
-    normed, (wx_ref, wz_ref) = refs[:planes], refs[planes : planes + 2]
-    outs, (left, held, sems) = refs[planes + 2 : -3], refs[-3:]
-    tile = held.shape[1]
-    count = wx_ref.shape[0] // tile
-    take = flow(
-        [ref.at[pl.ds(i * tile, tile)] for ref in (wx_ref, wz_ref) for i in range(count)], held, sems, 3
-    )
+    normed, weights = refs[:planes], refs[planes : planes + 2]
+    outs, left = refs[planes + 2 : -1], refs[-1]
+    tile = 256
     rows = normed[0].shape[0]
     for index, ref in enumerate(normed):
         left[index * rows : (index + 1) * rows, :] = ref[...]
-    for i in range(0, 2 * count, 2):
-        take(i)
-        take(i + 1)
-        weight = jnp.concatenate([held[i], held[i + 1]], axis=0)
-        result = dot_nt(left[...], weight).astype(jnp.bfloat16)
-        col = i % count * tile
-        for index in range(planes):
-            outs[2 * index + i // count][:, col : col + 2 * tile] = result[
-                index * rows : (index + 1) * rows
-            ]
+    for which, weight in enumerate(weights):
+        for col in range(0, weight.shape[0], tile):
+            result = dot_nt(left[...], weight[col : col + tile, :]).astype(jnp.bfloat16)
+            for index in range(planes):
+                outs[2 * index + which][:, col : col + tile] = result[index * rows : (index + 1) * rows]
 
 
 def project_planes(normed, in_x, in_z):
     rows, width = normed[0].shape
     cols = in_x.shape[0]
-    tile = 128
-    pieces = 2 * cols // tile
     count = len(normed)
-    far_space = pl.BlockSpec(memory_space=pltpu.MemorySpace.HBM)
     outs = pl.pallas_call(
         functools.partial(project_kernel, planes=count),
         out_shape=(jax.ShapeDtypeStruct((rows, cols), jnp.bfloat16),) * (2 * count),
-        in_specs=[vmem()] * count + [far_space, far_space],
+        in_specs=[vmem()] * (count + 2),
         out_specs=(vmem(),) * (2 * count),
-        scratch_shapes=[
-            pltpu.VMEM((count * rows, width), jnp.bfloat16),
-            pltpu.VMEM((pieces, tile, width), jnp.bfloat16),
-            pltpu.SemaphoreType.DMA((pieces,)),
-        ],
-        compiler_params=pltpu.CompilerParams(vmem_limit_bytes=WEIGHT_LIMIT),
+        scratch_shapes=[pltpu.VMEM((count * rows, width), jnp.bfloat16)],
+        compiler_params=pltpu.CompilerParams(vmem_limit_bytes=VMEM_LIMIT),
         cost_estimate=pl.CostEstimate(
-            flops=6 << 30, bytes_accessed=16 << 20, transcendentals=0
+            flops=4 << 30, bytes_accessed=4 << 20, transcendentals=0
         ),
         name="project_planes",
-    )(*[near(value) for value in normed], far(in_x), far(in_z))
+    )(*[near(value) for value in normed], near(in_x), near(in_z))
     return outs[0::2], outs[1::2]
 
 
@@ -359,16 +342,17 @@
 ):
     xs, zs, dts = refs[:planes], refs[planes : 2 * planes], refs[2 * planes : 3 * planes]
     refs = refs[3 * planes :]
-    early, late = refs[:2], refs[2:4]
-    (taps_x, taps_bc, masks, bias, marks, keep, head_rows, gain_ref) = refs[4:12]
-    gated_ref, square_ref = refs[12:14]
-    x_all, z_all, dt_all, bc_all = refs[14:]
+    far_pieces = refs[:2]
+    (taps_x, taps_bc, masks, bias, marks, keep, head_rows, gain_ref) = refs[2:10]
+    weight_ref, gated_ref, square_ref, held_ref = refs[10:14]
+    x_all, z_all, dt_all, bc_all, sem = refs[14:]
+    held_copy = pltpu.make_async_copy(weight_ref, held_ref, sem)
+    held_copy.start()
     z_pos, spot = spot_ref[0], spot_ref[1]
     rows = xs[0].shape[0]
     chans = xs[0].shape[1]
     highest_ = lax.Precision.HIGHEST
     upper = spot >= 2
-    ahead = early[0].shape[0] // rows
     x_all[0:8, :] = jnp.zeros((8, chans), jnp.float32)
     bc_all[0:8, :] = jnp.zeros((8, 2 * STATE), jnp.float32)
     for s in range(planes):
@@ -376,9 +360,9 @@
         x_all[pl.ds(at + 8, rows), :] = xs[s][...].astype(jnp.float32)
         z_all[pl.ds(at, rows), :] = zs[s][...]
         dt_all[pl.ds(at, rows), :] = dts[s][...]
-        part = early if s < ahead else late
-        first = (s if s < ahead else s - ahead) * rows
-        one, two = [ref[first : first + rows, :].astype(jnp.float32) for ref in part]
+        one, two = [
+            ref[s * rows : (s + 1) * rows, :].astype(jnp.float32) for ref in far_pieces
+        ]
         for chip, left, value in (
             (z_pos, 0, jnp.where(upper, two, one)),
             (z_pos + GROUPS, STATE, jnp.where(upper, one, two)),
@@ -461,9 +445,36 @@
                 keys, end_x, (((0,), (0,)), ((), ())), preferred_element_type=jnp.float32
             )
             state = spread[3 * rows : 3 * rows + 1] * state + fresh
-
-
-def scan_all(spots, xs, zs, dts, early, late, consts, heads):
+    held_copy.wait()
+
+
+def pair_kernel(spots, *refs):
+    *pieces, out_ref = refs
+    count = len(pieces) // 2
+    rows, cols = pieces[0].shape
+    first = lax.rem(spots[1], 2) == 0
+    for i in range(count):
+        own, other = pieces[i][...].astype(jnp.float32), pieces[count + i][...].astype(jnp.float32)
+        span = slice(i * rows, (i + 1) * rows)
+        out_ref[span, :] = jnp.concatenate(
+            [jnp.where(first, own, other), jnp.where(first, other, own)], axis=1
+        ).astype(jnp.bfloat16)
+
+
+def pair_pieces(spots, own, other):
+    rows, cols = own[0].shape
+    return pl.pallas_call(
+        pair_kernel,
+        out_shape=jax.ShapeDtypeStruct((len(own) * rows, 2 * cols), jnp.bfloat16),
+        in_specs=[smem()] + [vmem()] * (2 * len(own)),
+        out_specs=vmem(),
+        compiler_params=pltpu.CompilerParams(vmem_limit_bytes=VMEM_LIMIT),
+        cost_estimate=pl.CostEstimate(flops=1 << 20, bytes_accessed=1 << 20, transcendentals=0),
+        name="pair_pieces",
+    )(spots, *[near(value) for value in (*own, *other)])
+
+
+def scan_all(spots, xs, zs, dts, far_pieces, consts, weight, heads):
     planes = len(xs)
     rows, chans = xs[0].shape
     return pl.pallas_call(
@@ -471,65 +482,63 @@
         out_shape=(
             jax.ShapeDtypeStruct((planes * rows, chans), jnp.bfloat16),
             jax.ShapeDtypeStruct((8, rows), jnp.float32),
+            pltpu.VMEM(weight.shape, weight.dtype),
         ),
-        in_specs=[smem()] + [vmem()] * (3 * planes + 4 + len(consts)),
-        out_specs=(vmem(), vmem()),
+        in_specs=[smem()]
+        + [vmem()] * (3 * planes + 2 + len(consts))
+        + [pl.BlockSpec(memory_space=pltpu.MemorySpace.HBM)],
+        out_specs=(vmem(), vmem(), vmem()),
         scratch_shapes=[
             pltpu.VMEM((planes * rows + 8, chans), jnp.float32),
             pltpu.VMEM((planes * rows, chans), jnp.bfloat16),
             pltpu.VMEM((planes * rows, 128), jnp.float32),
             pltpu.VMEM((planes * rows + 8, 2 * STATE), jnp.float32),
+            pltpu.SemaphoreType.DMA,
         ],
         compiler_params=pltpu.CompilerParams(vmem_limit_bytes=VMEM_LIMIT),
         cost_estimate=pl.CostEstimate(flops=1 << 30, bytes_accessed=8 << 20, transcendentals=0),
         name="scan_all",
-    )(spots, *[near(v) for v in (*xs, *zs, *dts, *early, *late, *consts)])
-
-
-def out_kernel(spots, gated_ref, weight_ref, *refs, planes, first):
-    outs, (held, sems) = refs[:-2], refs[-2:]
-    tile = held.shape[2]
-    take = flow(
-        [weight_ref.at[:, pl.ds(first + i * tile, tile)] for i in range(held.shape[0])], held, sems, 3
-    )
+    )(spots, *[near(v) for v in (*xs, *zs, *dts, *far_pieces, *consts)], far(weight))
+
+
+def out_kernel(spots, gated_ref, weight_ref, *outs, planes, steps):
     rows = gated_ref.shape[0] // planes // PLANE
     level, side = lax.div(spots[1], 2), lax.rem(spots[1], 2)
     parts = []
-    for at_side in (1 - side, side):
-        for step in range(planes):
-            plane = lax.rem(spots[0] - 1 - step + planes, planes)
+    for step in steps:
+        plane = lax.rem(spots[0] - 1 - step + planes, planes)
+        for at_side in (1 - side, side):
             for at_level in (1 - level, level):
                 at = pl.multiple_of(((plane * 2 + at_level) * 2 + at_side) * rows, rows)
                 parts.append(gated_ref[pl.ds(at, rows), :])
     left = jnp.concatenate(parts, axis=0)
-    for i in range(held.shape[0]):
-        take(i)
-        result = jnp.dot(left, held[i], preferred_element_type=jnp.float32).astype(jnp.bfloat16)
+    tile = 1024
+    for col in range(0, weight_ref.shape[1], tile):
+        result = jnp.dot(
+            left, weight_ref[:, col : col + tile], preferred_element_type=jnp.float32
+        ).astype(jnp.bfloat16)
         at = 0
         for out in outs:
-            out[:, i * tile : (i + 1) * tile] = result[at : at + out.shape[0]]
+            out[:, col : col + tile] = result[at : at + out.shape[0]]
             at += out.shape[0]
 
 
-def out_part(spots, gated, weight, planes, first, width):
-    chans = weight.shape[0]
+def out_part(spots, gated, weight, planes, steps):
+    width = weight.shape[1]
     rows = gated.shape[0] // planes // PLANE
-    tile = 1024
-    shapes = [2 * rows] * planes + [rows] * (2 * planes)
+    shapes = [2 * rows, rows, rows] * len(steps)
     outs = pl.pallas_call(
-        functools.partial(out_kernel, planes=planes, first=first),
+        functools.partial(out_kernel, planes=planes, steps=steps),
         out_shape=tuple(jax.ShapeDtypeStruct((high, width), jnp.bfloat16) for high in shapes),
-        in_specs=[smem(), vmem(), pl.BlockSpec(memory_space=pltpu.MemorySpace.HBM)],
+        in_specs=[smem(), vmem(), vmem()],
         out_specs=(vmem(),) * len(shapes),
-        scratch_shapes=[
-            pltpu.VMEM((width // tile, chans, tile), jnp.bfloat16),
-            pltpu.SemaphoreType.DMA((width // tile,)),
-        ],
         compiler_params=pltpu.CompilerParams(vmem_limit_bytes=VMEM_LIMIT),
-        cost_estimate=pl.CostEstimate(flops=3 << 30, bytes_accessed=8 << 20, transcendentals=0),
+        cost_estimate=pl.CostEstimate(
+            flops=len(steps) << 30, bytes_accessed=len(steps) << 21, transcendentals=0
+        ),
         name="out_part",
-    )(spots, near(gated), far(weight))
-    return outs[:planes], outs[planes::2], outs[planes + 1 :: 2]
+    )(spots, near(gated), near(weight))
+    return [outs[i : i + 3] for i in range(0, len(outs), 3)]
 
 
 def pick_kernel(spots, *refs, pieces, step, planes, chained):
@@ -696,13 +705,11 @@
     straight, crossed = [[own]], []
     straight_core, crossed_core = [], []
     results = []
-    early = picked = None
+    picked = None
+    peers = []
     spec = (segment_ids, conv_x, conv_bc, dt_bias, decay_rate, skip, norm_gain)
 
-    def exchange(piece):
-        other = permute(piece, over_core)
-        own_first = jnp.concatenate([piece, other], axis=1)
-        both = jnp.where(me % 2 == 0, own_first, jnp.concatenate([other, piece], axis=1))
+    def send_far(both):
         result = []
         for turn in range(2):
             pairs = []
@@ -719,8 +726,8 @@
     def blocks_of(step):
         return [straight[step], straight_core[step], crossed[step], crossed_core[step]]
 
-    def compute(step):
-        return norm_plane(spots, blocks_of(step), gain_row, small)
+    def compute(step, *weights):
+        return norm_plane(spots, blocks_of(step), gain_row, small, step >= 2, weights)
 
     def pick(step, earlier):
         return pick_plane(spots, blocks_of(step), earlier, count * CAP, width, step, planes)
@@ -749,16 +756,15 @@
             extra["spec"] = (spec, destination)
         else:
             extra["result"] = compute(step - 1)
-            picked = pick(step - 1, picked)
+            if step < 3:
+                picked = pick(step - 1, picked)
         if step == 1:
             extra["consts"] = scan_constants(*spec, z_pos, planes)
             extra["place"] = own_slots(own_dest)
         if step == 2:
             extra["first"] = project_planes([results[0][0], extra["result"][0]], in_x, in_z)
-        if last:
-            extra["early"] = exchange(
-                jnp.concatenate([result[1] for result in results[:2]], axis=0)
-            )
+        if step >= 2:
+            extra["peer"] = permute(results[step - 2][1], over_core)
         group, extra, picked = lax.optimization_barrier((group, extra, picked))
         straight_core.append(group[0])
         crossed.append(group[1])
@@ -772,52 +778,47 @@
             consts, place = extra["consts"], extra["place"]
         if step == 2:
             first = extra["first"]
-        if last:
-            early = extra["early"]
+        if step >= 2:
+            peers.append(extra["peer"])
     crossed_core.append(over(crossed[-1], over_core))
-    results.append(compute(planes - 1))
+    *result, near_x, near_z = compute(planes - 1, in_x, in_z)
+    results.append(result)
 
     normed, pieces, dts = zip(*results)
-    late = exchange(jnp.concatenate(pieces[2:], axis=0))
-    second = project_planes(normed[2:], in_x, in_z)
+    peers += over(pieces[2:], over_core)
+    both = pair_pieces(spots, pieces, peers)
+    both, normed = lax.optimization_barrier((both, normed[2:]))
+    far_pieces = send_far(both)
+    second = project_planes(normed, near_x, near_z)
     xs, zs = [first[i] + second[i] for i in range(2)]
-    gated, squares = scan_all(spots, xs, zs, dts, early, late, consts, heads)
+    gated, squares, held_out = scan_all(spots, xs, zs, dts, far_pieces, consts, out_weight, heads)
 
     squares = squares + permute(squares, over_core)
     squares = squares + permute(squares, over_y)
     scale = lax.rsqrt(squares[:planes].reshape(-1) / (INNER // GROUPS) + 1e-05)
 
-    parts = 2
-    part = width // parts
     mine = [
         lax.dynamic_slice_in_dim(scale, ((z_pos - 1 - step) % planes * PLANE + spot) * rows, rows)[:, None]
         for step in range(planes)
     ]
-    kept, got_y = [], []
-    for index in range(parts):
-        away, send, keep = out_part(spots, gated, out_weight, planes, index * part, part)
-        got = over(away, over_core)
-        send = [
-            (send[step].astype(f32) + got[step][:rows].astype(f32)).astype(jnp.bfloat16)
-            for step in range(planes)
-        ]
-        kept.append([(keep[step], got[step][rows:]) for step in range(planes)])
-        got_y.append(over(send, over_y))
-    travelling = [None] * parts
-    totals = [None] * parts
+    outs = out_part(spots, gated, held_out, planes, (0,))
+    got = [permute(outs[0][0], over_core)]
+    outs += out_part(spots, gated, held_out, planes, tuple(range(1, planes)))
+    got += [permute(away, over_core) for away, _, _ in outs[1:]]
+    total = None
     for step in range(planes):
-        for index in range(parts):
-            low, high = kept[index][step]
-            total = low.astype(f32) + high.astype(f32)
-            total = (total + got_y[index][step].astype(f32)) * mine[step]
-            if step:
-                total = total + travelling[index].astype(f32)
-            if step + 1 < planes:
-                travelling[index] = permute(total.astype(jnp.bfloat16), ring)
-            totals[index] = total
-        if step == 0:
-            picked, travelling[0] = lax.optimization_barrier((pick(planes - 1, picked), travelling[0]))
-    layer_out = (hidden.astype(f32) + jnp.concatenate(totals, axis=1)).astype(jnp.bfloat16)
+        send = (outs[step][1].astype(f32) + got[step][:rows].astype(f32)).astype(jnp.bfloat16)
+        group = [permute(send, over_y)]
+        if step:
+            group.append(permute(total.astype(jnp.bfloat16), ring))
+        if step in (1, 2):
+            picked = pick(planes - 3 + step, picked)
+        group, got, picked, outs = lax.optimization_barrier((group, got, picked, outs))
+        total = outs[step][2].astype(f32) + got[step][rows:].astype(f32)
+        total = (total + group[0].astype(f32)) * mine[step]
+        if step:
+            total = total + group[1].astype(f32)
+    layer_out = (hidden.astype(f32) + total).astype(jnp.bfloat16)
 
     filled = jnp.dot(place, layer_out, preferred_element_type=f32).astype(jnp.bfloat16)
     received = lax.all_to_all(

time: 222 us -> 192 us (0.86); the launches traced: 218 us -> 191 us
  starting transfers between devices: 36 us -> 17.4 us
  Pallas kernels: 63.2 us -> 50.3 us
  local copies, waits for them, and re-layouts: 15.2 us -> 2.6 us
  waiting for transfers between devices: 75.5 us -> 83.9 us
  other arithmetic: 8.65 us -> 16 us
    ppermute x47 -> x36, starting transfers between devices: 36 us -> 17.4 us  [permute(): return lax.ppermute(value, 'tensor', pairs)]
    pallas_call x2, Pallas kernels: 23.4 us -> 9.17 us  [project_planes(): pl.pallas_call(functools.partial(project_kernel, planes=count), out_shape...]
    unnamed x86 -> x68, local copies, waits for them, and re-layouts: 11 us -> 0.93 us
    convert_element_type x12 -> x8, other arithmetic: 1.48 us -> 10.3 us  [the longest x4 4.67 us: on_device_planes(): (outs[step][1].astype(f32) + got[step][:rows].astype(f32)).astype(jnp.bfl...]
    ppermute x47 -> x36, waiting for transfers between devices: 75.5 us -> 83.9 us  [permute(): return lax.ppermute(value, 'tensor', pairs)]
    pallas_call x4, Pallas kernels: 14.9 us -> 18.8 us  [norm_plane(): pl.pallas_call(functools.partial(norm_kernel, pieces=tuple((len(block) fo...]
    pallas_call x2 -> x3, Pallas kernels: 9.36 us -> 8.51 us  [the longest x2 7.84 us: out_part(): pl.pallas_call(functools.partial(out_kernel, planes=planes, steps=steps),...]
  transfers between devices with their start and end apart: 47 -> 36, of which waited for: 18 -> 20; matrix products, arithmetic and copies ran while one was open for 4% -> 4% of each run, Pallas kernels for 24% -> 22%
where the time goes in v3:
time: 192 us; the launch traced here: 191 us
  waiting for transfers between devices  83.9 us (44%)
  Pallas kernels  50.3 us (26%)
  blocking collectives  19.3 us (10%)
  starting transfers between devices  17.4 us (9%)
  other arithmetic  16 us (8%)
  local copies, waits for them, and re-layouts  2.6 us (1%)
    ppermute x36, waiting for transfers between devices, permute(): return lax.ppermute(value, 'tensor', pairs)  83.9 us
    all_to_all x1, blocking collectives, on_device_planes(): lax.all_to_all(filled.reshape(count, CAP, width), 'tensor', split_axis=0,...  19.3 us
    pallas_call x4, Pallas kernels, norm_plane(): pl.pallas_call(functools.partial(norm_kernel, pieces=tuple((len(block) fo...  18.8 us
    ppermute x36, starting transfers between devices, permute(): return lax.ppermute(value, 'tensor', pairs)  17.4 us
    pallas_call x2, Pallas kernels, project_planes(): pl.pallas_call(functools.partial(project_kernel, planes=count), out_shape...  9.17 us
    pallas_call x2, Pallas kernels, out_part(): pl.pallas_call(functools.partial(out_kernel, planes=planes, steps=steps),...  7.84 us
    pallas_call x4, Pallas kernels, pick_plane(): pl.pallas_call(functools.partial(pick_kernel, pieces=tuple((len(block) fo...  7.16 us
    pallas_call x1, Pallas kernels, scan_all(): pl.pallas_call(functools.partial(scan_kernel, heads=heads, planes=planes)...  6.5 us
  transfers between devices with their start and end apart: 36, of which 20 were waited for; matrix products, arithmetic and copies ran while one was open for 4% of the time, Pallas kernels for 22%

profile of v3, /device:TPU:0, one launch (start us, length us, event | category | flops | bytes accessed | tf_op | source)
XLA Modules:
  0.0 191.2 jit_solution(11634141243532841651)
XLA Ops:
  3.8 2.5 %collective-permute-start.1 = (bf16[32,8320]{1,0:T(8,128)(2,1)}, bf16[32,8320]{1,0:T(8,128)(2,1)}, u32[]{:S(2)}, u32[]{:S(2)}) collective-permute-start(bf16[32,8320]{1,0:T(8,128)(2,1)} %pad_maximum_fusion.1.refs_0_), channel_id=1, source_target_pairs={{0,2},{1,3},{2,0},{3,1},{4,6},{5,7},{6,4},{7,5},{8,10},{9,11},{10,... | collective-permute-start | bytes 1597448 | tf_op jit(solution)/shard_map/ppermute | solution.py:692
  9.8 9.6 %collective-permute-done.1.refs_2_ = bf16[32,8320]{1,0:T(8,128)(2,1)} collective-permute-done((bf16[32,8320]{1,0:T(8,128)(2,1)}, bf16[32,8320]{1,0:T(8,128)(2,1)}, u32[]{:S(2)}, u32[]{:S(2)}) %collective-permute-start.1) | collective-permute-done | bytes 532512 | tf_op jit(solution)/shard_map/ppermute | solution.py:692
  19.4 3.4 %collective-permute-done.2.refs_0_ = bf16[32,8320]{1,0:T(8,128)(2,1)} collective-permute-done((bf16[32,8320]{1,0:T(8,128)(2,1)}, bf16[32,8320]{1,0:T(8,128)(2,1)}, u32[]{:S(2)}, u32[]{:S(2)}) %collective-permute-start.2) | collective-permute-done | bytes 532512 | tf_op jit(solution)/shard_map/ppermute | solution.py:692
  25.8 2.3 %pick_plane.4.refs_4_ = bf16[32,8192]{1,0:T(8,128)(2,1)S(1)} custom-call(s32[2]{0:T(128)S(1)} %pad_add_fusion.spot_ref.spots, bf16[32,8320]{1,0:T(8,128)(2,1)} %pad_maximum_fusion.1.refs_0_, bf16[32,8320]{1,0:T(8,128)(2,1)} %collective-permute-done.refs_1_, bf16[32,8320]{1,0:T(8,128)(2,1)} %collective-permute-done.1.refs_2_, ...), custom_call_target="tpu_custom_call" | custom-call | flops 1073741824 | bytes 3145728 | tf_op jit(solution)/shard_map/pick_plane/pallas_call | solution.py:574
  28.1 4.5 %norm_plane.4 = (bf16[128,8192]{1,0:T(8,128)(2,1)S(1)}, bf16[128,64]{1,0:T(8,128)(2,1)S(1)}, f32[128,128]{1,0:T(8,128)S(1)}) custom-call(s32[2]{0:T(128)S(1)} %pad_add_fusion.spot_ref.spots, bf16[32,8320]{1,0:T(8,128)(2,1)} %pad_maximum_fusion.1.refs_0_, bf16[32,8320]{1,0:T(8,128)(2,1)} %collective-permute-done.refs_1_, ...), custom_call_target="tpu_custom_call" | custom-call | flops 2147483648 | bytes 6291456 | tf_op jit(solution)/shard_map/norm_plane/pallas_call | solution.py:277
  32.6 5.0 %collective-permute-done.4.refs_2_ = bf16[32,8320]{1,0:T(8,128)(2,1)} collective-permute-done((bf16[32,8320]{1,0:T(8,128)(2,1)}, bf16[32,8320]{1,0:T(8,128)(2,1)}, u32[]{:S(2)}, u32[]{:S(2)}) %collective-permute-start.4) | collective-permute-done | bytes 532512 | tf_op jit(solution)/shard_map/ppermute | solution.py:692
  41.8 3.7 %norm_plane.5 = (bf16[128,8192]{1,0:T(8,128)(2,1)S(1)}, bf16[128,64]{1,0:T(8,128)(2,1)S(1)}, f32[128,128]{1,0:T(8,128)S(1)}) custom-call(s32[2]{0:T(128)S(1)} %pad_add_fusion.spot_ref.spots, bf16[32,8320]{1,0:T(8,128)(2,1)} %collective-permute-done.2.refs_0_, bf16[32,8320]{1,0:T(8,128)(2,1)} %collective-permute-done.3.refs_1_, ...), custom_call_target="tpu_custom_call" | custom-call | flops 2147483648 | bytes 6291456 | tf_op jit(solution)/shard_map/norm_plane/pallas_call | solution.py:277
  45.5 4.5 %project_planes.2 = (bf16[128,512]{1,0:T(8,128)(2,1)S(1)}, bf16[128,512]{1,0:T(8,128)(2,1)S(1)}, bf16[128,512]{1,0:T(8,128)(2,1)S(1)}, bf16[128,512]{1,0:T(8,128)(2,1)S(1)}) custom-call(bf16[128,8192]{1,0:T(8,128)(2,1)S(1)} %get-tuple-element.148.refs_0_, bf16[128,8192]{1,0:T(8,128)(2,1)S(1)} %get-tuple-element.151.refs_1_, bf16[512,8192]{1,0:T(8,128)(2,1)S(1)} %bitcast.20, ...), custom_call_target="tpu_custom_call" | custom-call | flops 4294967296 | bytes 4194304 | tf_op jit(solution)/shard_map/project_planes/pallas_call | solution.py:318
  54.4 3.0 %collective-permute-done.9.refs_0_ = bf16[32,8320]{1,0:T(8,128)(2,1)S(1)} collective-permute-done((bf16[32,8320]{1,0:T(8,128)(2,1)}, bf16[32,8320]{1,0:T(8,128)(2,1)S(1)}, u32[]{:S(2)}, u32[]{:S(2)}) %collective-permute-start.9) | collective-permute-done | bytes 532512 | tf_op jit(solution)/shard_map/ppermute | solution.py:692
  59.3 3.5 %norm_plane.6 = (bf16[128,8192]{1,0:T(8,128)(2,1)S(1)}, bf16[128,64]{1,0:T(8,128)(2,1)S(1)}, f32[128,128]{1,0:T(8,128)S(1)}) custom-call(s32[2]{0:T(128)S(1)} %pad_add_fusion.spot_ref.spots, bf16[32,8320]{1,0:T(8,128)(2,1)} %collective-permute-done.5.refs_0_, bf16[32,8320]{1,0:T(8,128)(2,1)S(1)} %collective-permute-done.7.refs_1_, ...), custom_call_target="tpu_custom_call" | custom-call | flops 2147483648 | bytes 6291456 | tf_op jit(solution)/shard_map/norm_plane/pallas_call | solution.py:277
  62.9 3.5 %collective-permute-done.13.refs_2_ = bf16[16,8320]{1,0:T(8,128)(2,1)S(1)} collective-permute-done((bf16[16,8320]{1,0:T(8,128)(2,1)S(1)}, bf16[16,8320]{1,0:T(8,128)(2,1)S(1)}, u32[]{:S(2)}, u32[]{:S(2)}) %collective-permute-start.13) | collective-permute-done | bytes 266272 | tf_op jit(solution)/shard_map/ppermute | solution.py:692
  66.3 2.0 %collective-permute-done.14.refs_3_ = bf16[16,8320]{1,0:T(8,128)(2,1)S(1)} collective-permute-done((bf16[16,8320]{1,0:T(8,128)(2,1)S(1)}, bf16[16,8320]{1,0:T(8,128)(2,1)S(1)}, u32[]{:S(2)}, u32[]{:S(2)}) %collective-permute-start.14) | collective-permute-done | bytes 266272 | tf_op jit(solution)/shard_map/ppermute | solution.py:692
  70.4 7.1 %norm_plane.7 = (bf16[128,8192]{1,0:T(8,128)(2,1)S(1)}, bf16[128,64]{1,0:T(8,128)(2,1)S(1)}, f32[128,128]{1,0:T(8,128)S(1)}, bf16[512,8192]{1,0:T(8,128)(2,1)S(1)}, bf16[512,8192]{1,0:T(8,128)(2,1)S(1)}) custom-call(s32[2]{0:T(128)S(1)} %pad_add_fusion.spot_ref.spots, bf16[32,8320]{1,0:T(8,128)(2,1)S(1)} %collective-permute-done.9.refs_0_, ...), custom_call_target="tpu_custom_call" | custom-call | flops 2147483648 | bytes 6291456 | tf_op jit(solution)/shard_map/norm_plane/pallas_call | solution.py:277
  80.1 2.8 %collective-permute-start.22 = (bf16[512,128]{1,0:T(8,128)(2,1)S(1)}, bf16[512,128]{1,0:T(8,128)(2,1)S(1)}, u32[]{:S(2)}, u32[]{:S(2)}) collective-permute-start(bf16[512,128]{1,0:T(8,128)(2,1)S(1)} %pair_pieces.1), channel_id=1, source_target_pairs={{0,2},{1,3},{2,6},{3,7},{4,10},{5,11},{6,14},{7,15},{8,0},{9,1},{1... | collective-permute-start | bytes 393224 | tf_op jit(solution)/shard_map/ppermute | solution.py:692
  82.9 4.6 %project_planes.3 = (bf16[128,512]{1,0:T(8,128)(2,1)S(1)}, bf16[128,512]{1,0:T(8,128)(2,1)S(1)}, bf16[128,512]{1,0:T(8,128)(2,1)S(1)}, bf16[128,512]{1,0:T(8,128)(2,1)S(1)}) custom-call(bf16[128,8192]{1,0:T(8,128)(2,1)S(1)} %get-tuple-element.179.refs_0_, bf16[128,8192]{1,0:T(8,128)(2,1)S(1)} %get-tuple-element.180.refs_1_, ...), custom_call_target="tpu_custom_call" | custom-call | flops 4294967296 | bytes 4194304 | tf_op jit(solution)/shard_map/project_planes/pallas_call | solution.py:318
  87.6 4.0 %collective-permute-done.22.refs_13_ = bf16[512,128]{1,0:T(8,128)(2,1)S(1)} collective-permute-done((bf16[512,128]{1,0:T(8,128)(2,1)S(1)}, bf16[512,128]{1,0:T(8,128)(2,1)S(1)}, u32[]{:S(2)}, u32[]{:S(2)}) %collective-permute-start.22) | collective-permute-done | bytes 131104 | tf_op jit(solution)/shard_map/ppermute | solution.py:692
  91.6 6.5 %scan_all.1 = (bf16[512,512]{1,0:T(8,128)(2,1)S(1)}, f32[8,128]{1,0:T(8,128)S(1)}, bf16[512,8192]{1,0:T(8,128)(2,1)S(1)}) custom-call(s32[2]{0:T(128)S(1)} %pad_add_fusion.spot_ref.spots, bf16[128,512]{1,0:T(8,128)(2,1)S(1)} %get-tuple-element.160.refs_0_, bf16[128,512]{1,0:T(8,128)(2,1)S(1)} %get-tuple-element.161.refs_1_, ...), custom_call_target="tpu_custom_call" | custom-call | flops 1073741824 | bytes 8388608 | tf_op jit(solution)/shard_map/scan_all/pallas_call | solution.py:480
  100.2 5.9 %out_part.3 = (bf16[64,8192]{1,0:T(8,128)(2,1)}, bf16[32,8192]{1,0:T(8,128)(2,1)S(1)}, bf16[32,8192]{1,0:T(8,128)(2,1)S(1)}, bf16[64,8192]{1,0:T(8,128)(2,1)}, b...) custom-call(s32[2]{0:T(128)S(1)} %pad_add_fusion.spot_ref.spots, ...), custom_call_target="tpu_custom_call" | custom-call | flops 3221225472 | bytes 6291456 | tf_op jit(solution)/shard_map/out_part/pallas_call | solution.py:530
  108.1 2.2 %collective-permute-done.29 = f32[8,128]{1,0:T(8,128)S(1)} collective-permute-done((f32[8,128]{1,0:T(8,128)S(1)}, f32[8,128]{1,0:T(8,128)S(1)}, u32[]{:S(2)}, u32[]{:S(2)}) %collective-permute-start.29) | collective-permute-done | bytes 4128 | tf_op jit(solution)/shard_map/ppermute | solution.py:692
  111.6 10.7 %collective-permute-done.30 = f32[8,128]{1,0:T(8,128)S(1)} collective-permute-done((f32[8,128]{1,0:T(8,128)S(1)}, f32[8,128]{1,0:T(8,128)S(1)}, u32[]{:S(2)}, u32[]{:S(2)}) %collective-permute-start.30) | collective-permute-done | bytes 4128 | tf_op jit(solution)/shard_map/ppermute | solution.py:692
  127.5 11.3 %collective-permute-done.31 = bf16[32,8192]{1,0:T(8,128)(2,1)S(1)} collective-permute-done((bf16[32,8192]{1,0:T(8,128)(2,1)S(1)}, bf16[32,8192]{1,0:T(8,128)(2,1)S(1)}, u32[]{:S(2)}, u32[]{:S(2)}) %collective-permute-start.31) | collective-permute-done | bytes 524320 | tf_op jit(solution)/shard_map/ppermute | solution.py:692
  143.3 10.8 %collective-permute-done.33 = bf16[32,8192]{1,0:T(8,128)(2,1)S(1)} collective-permute-done((bf16[32,8192]{1,0:T(8,128)(2,1)S(1)}, bf16[32,8192]{1,0:T(8,128)(2,1)S(1)}, u32[]{:S(2)}, u32[]{:S(2)}) %collective-permute-start.33) | collective-permute-done | bytes 524320 | tf_op jit(solution)/shard_map/ppermute | solution.py:692
  157.8 10.8 %collective-permute-done.35 = bf16[32,8192]{1,0:T(8,128)(2,1)S(1)} collective-permute-done((bf16[32,8192]{1,0:T(8,128)(2,1)S(1)}, bf16[32,8192]{1,0:T(8,128)(2,1)S(1)}, u32[]{:S(2)}, u32[]{:S(2)}) %collective-permute-start.35) | collective-permute-done | bytes 524320 | tf_op jit(solution)/shard_map/ppermute | solution.py:692
  170.6 19.3 %all_to_all.5 = bf16[16,2,8192]{2,1,0:T(2,128)(2,1)S(1)} all-to-all(bf16[16,2,8192]{2,1,0:T(2,128)(2,1)S(1)} %reshape.38), channel_id=1, replica_groups=mesh['rep'=2,'dp'=1,'tensor'=16] {'tensor'}, dimensions={0} | all-to-all | bytes 1048576 | tf_op jit(solution)/shard_map/all_to_all | solution.py:824
  (172 shorter events, 46.3 us)
Async XLA Ops:
  3.8 15.6 %collective-permute-start.1 = (bf16[32,8320]{1,0:T(8,128)(2,1)}, bf16[32,8320]{1,0:T(8,128)(2,1)}, u32[]{:S(2)}, u32[]{:S(2)}) collective-permute-start(bf16[32,8320]{1,0:T(8,128)(2,1)} %pad_maximum_fusion.1.refs_0_), channel_id=1, source_target_pairs={{0,2},{1,3},{2,0},{3,1},{4,6},{5,7},{6,4},{7,5},{8,10},{9,11},{10,... | collective-permute-start | bytes 1597448 | tf_op jit(solution)/shard_map/ppermute | solution.py:692
  6.3 16.4 %collective-permute-start.2 = (bf16[32,8320]{1,0:T(8,128)(2,1)}, bf16[32,8320]{1,0:T(8,128)(2,1)}, u32[]{:S(2)}, u32[]{:S(2)}) collective-permute-start(bf16[32,8320]{1,0:T(8,128)(2,1)} %pad_maximum_fusion.1.refs_0_), channel_id=1, source_target_pairs={{0,4},{1,5},{2,6},{3,7},{4,8},{5,9},{6,10},{7,11},{8,12},{9,13},{1... | collective-permute-start | bytes 1597448 | tf_op jit(solution)/shard_map/ppermute | solution.py:692
  22.8 9.9 %collective-permute-start.3 = (bf16[32,8320]{1,0:T(8,128)(2,1)}, bf16[32,8320]{1,0:T(8,128)(2,1)}, u32[]{:S(2)}, u32[]{:S(2)}) collective-permute-start(bf16[32,8320]{1,0:T(8,128)(2,1)} %collective-permute-done.2.refs_0_), channel_id=1, source_target_pairs={{0,1},{1,0},{2,3},{3,2},{4,5},{5,4},{6,7},{7,6},{8,9},{9,8},{10,11... | collective-permute-start | bytes 1597448 | tf_op jit(solution)/shard_map/ppermute | solution.py:692
  22.8 14.8 %collective-permute-start.4 = (bf16[32,8320]{1,0:T(8,128)(2,1)}, bf16[32,8320]{1,0:T(8,128)(2,1)}, u32[]{:S(2)}, u32[]{:S(2)}) collective-permute-start(bf16[32,8320]{1,0:T(8,128)(2,1)} %collective-permute-done.2.refs_0_), channel_id=1, source_target_pairs={{0,2},{1,3},{2,0},{3,1},{4,6},{5,7},{6,4},{7,5},{8,10},{9,11},{10,... | collective-permute-start | bytes 1597448 | tf_op jit(solution)/shard_map/ppermute | solution.py:692
  23.3 16.3 %collective-permute-start.5 = (bf16[32,8320]{1,0:T(8,128)(2,1)}, bf16[32,8320]{1,0:T(8,128)(2,1)}, u32[]{:S(2)}, u32[]{:S(2)}) collective-permute-start(bf16[32,8320]{1,0:T(8,128)(2,1)} %collective-permute-done.2.refs_0_), channel_id=1, source_target_pairs={{0,4},{1,5},{2,6},{3,7},{4,8},{5,9},{6,10},{7,11},{8,12},{9,13},{1... | collective-permute-start | bytes 1597448 | tf_op jit(solution)/shard_map/ppermute | solution.py:692
  39.6 13.2 %collective-permute-start.7 = (bf16[32,8320]{1,0:T(8,128)(2,1)}, bf16[32,8320]{1,0:T(8,128)(2,1)S(1)}, u32[]{:S(2)}, u32[]{:S(2)}) collective-permute-start(bf16[32,8320]{1,0:T(8,128)(2,1)} %collective-permute-done.5.refs_0_), channel_id=1, source_target_pairs={{0,1},{1,0},{2,3},{3,2},{4,5},{5,4},{6,7},{7,6},{8,9},{9,8},{10,11... | collective-permute-start | bytes 1597448 | tf_op jit(solution)/shard_map/ppermute | solution.py:692
  40.1 14.2 %collective-permute-start.8 = (bf16[32,8320]{1,0:T(8,128)(2,1)}, bf16[32,8320]{1,0:T(8,128)(2,1)S(1)}, u32[]{:S(2)}, u32[]{:S(2)}) collective-permute-start(bf16[32,8320]{1,0:T(8,128)(2,1)} %collective-permute-done.5.refs_0_), channel_id=1, source_target_pairs={{0,2},{1,3},{2,0},{3,1},{4,6},{5,7},{6,4},{7,5},{8,10},{9,11},{10,... | collective-permute-start | bytes 1597448 | tf_op jit(solution)/shard_map/ppermute | solution.py:692
  41.6 15.7 %collective-permute-start.9 = (bf16[32,8320]{1,0:T(8,128)(2,1)}, bf16[32,8320]{1,0:T(8,128)(2,1)S(1)}, u32[]{:S(2)}, u32[]{:S(2)}) collective-permute-start(bf16[32,8320]{1,0:T(8,128)(2,1)} %collective-permute-done.5.refs_0_), channel_id=1, source_target_pairs={{0,4},{1,5},{2,6},{3,7},{4,8},{5,9},{6,10},{7,11},{8,12},{9,13},{1... | collective-permute-start | bytes 1597448 | tf_op jit(solution)/shard_map/ppermute | solution.py:692
  41.7 11.2 %collective-permute-start.11 = (bf16[128,64]{1,0:T(8,128)(2,1)S(1)}, bf16[128,64]{1,0:T(8,128)(2,1)S(1)}, u32[]{:S(2)}, u32[]{:S(2)}) collective-permute-start(bf16[128,64]{1,0:T(8,128)(2,1)S(1)} %get-tuple-element.156.refs_0_), channel_id=1, source_target_pairs={{0,1},{1,0},{2,3},{3,2},{4,5},{5,4},{6,7},{7,6},{8,9},{9,8},{10,11... | collective-permute-start | bytes 49160 | tf_op jit(solution)/shard_map/ppermute | solution.py:692
  57.4 11.0 %collective-permute-start.12 = (bf16[32,8320]{1,0:T(8,128)(2,1)S(1)}, bf16[32,8320]{1,0:T(8,128)(2,1)S(1)}, u32[]{:S(2)}, u32[]{:S(2)}) collective-permute-start(bf16[32,8320]{1,0:T(8,128)(2,1)S(1)} %collective-permute-done.9.refs_0_), channel_id=1, source_target_pairs={{0,1},{1,0},{2,3},{3,2},{4,5},{5,4},{6,7},{7,6},{8,9},{9,8},{10,11... | collective-permute-start | bytes 1597448 | tf_op jit(solution)/shard_map/ppermute | solution.py:692
  58.5 9.8 %collective-permute-start.14 = (bf16[16,8320]{1,0:T(8,128)(2,1)S(1)}, bf16[16,8320]{1,0:T(8,128)(2,1)S(1)}, u32[]{:S(2)}, u32[]{:S(2)}) collective-permute-start(bf16[16,8320]{1,0:T(8,128)(2,1)S(1)} %slice.34), channel_id=1, source_target_pairs={{0,4},{1,5},{2,6},{3,7},{4,8},{5,9},{6,10},{7,11},{8,12},{9,13},{1... | collective-permute-start | bytes 798728 | tf_op jit(solution)/shard_map/ppermute | solution.py:692
  68.9 8.8 %collective-permute-start.19 = (bf16[128,64]{1,0:T(8,128)(2,1)S(1)}, bf16[128,64]{1,0:T(8,128)(2,1)S(1)}, u32[]{:S(2)}, u32[]{:S(2)}) collective-permute-start(bf16[128,64]{1,0:T(8,128)(2,1)S(1)} %get-tuple-element.170.refs_2_), channel_id=1, source_target_pairs={{0,1},{1,0},{2,3},{3,2},{4,5},{5,4},{6,7},{7,6},{8,9},{9,8},{10,11... | collective-permute-start | bytes 49160 | tf_op jit(solution)/shard_map/ppermute | solution.py:692
  80.1 11.5 %collective-permute-start.22 = (bf16[512,128]{1,0:T(8,128)(2,1)S(1)}, bf16[512,128]{1,0:T(8,128)(2,1)S(1)}, u32[]{:S(2)}, u32[]{:S(2)}) collective-permute-start(bf16[512,128]{1,0:T(8,128)(2,1)S(1)} %pair_pieces.1), channel_id=1, source_target_pairs={{0,2},{1,3},{2,6},{3,7},{4,10},{5,11},{6,14},{7,15},{8,0},{9,1},{1... | collective-permute-start | bytes 393224 | tf_op jit(solution)/shard_map/ppermute | solution.py:692
  106.0 16.4 %collective-permute-start.25 = (bf16[64,8192]{1,0:T(8,128)(2,1)}, bf16[64,8192]{1,0:T(8,128)(2,1)}, u32[]{:S(2)}, u32[]{:S(2)}) collective-permute-start(bf16[64,8192]{1,0:T(8,128)(2,1)} %get-tuple-element.206), channel_id=1, source_target_pairs={{0,1},{1,0},{2,3},{3,2},{4,5},{5,4},{6,7},{7,6},{8,9},{9,8},{10,11... | collective-permute-start | bytes 3145736 | tf_op jit(solution)/shard_map/ppermute | solution.py:692
  106.5 15.8 %collective-permute-start.26 = (bf16[64,8192]{1,0:T(8,128)(2,1)}, bf16[64,8192]{1,0:T(8,128)(2,1)}, u32[]{:S(2)}, u32[]{:S(2)}) collective-permute-start(bf16[64,8192]{1,0:T(8,128)(2,1)} %get-tuple-element.207), channel_id=1, source_target_pairs={{0,1},{1,0},{2,3},{3,2},{4,5},{5,4},{6,7},{7,6},{8,9},{9,8},{10,11... | collective-permute-start | bytes 3145736 | tf_op jit(solution)/shard_map/ppermute | solution.py:692
  106.6 15.8 %collective-permute-start.27 = (bf16[64,8192]{1,0:T(8,128)(2,1)}, bf16[64,8192]{1,0:T(8,128)(2,1)}, u32[]{:S(2)}, u32[]{:S(2)}) collective-permute-start(bf16[64,8192]{1,0:T(8,128)(2,1)} %get-tuple-element.208), channel_id=1, source_target_pairs={{0,1},{1,0},{2,3},{3,2},{4,5},{5,4},{6,7},{7,6},{8,9},{9,8},{10,11... | collective-permute-start | bytes 3145736 | tf_op jit(solution)/shard_map/ppermute | solution.py:692
  108.1 14.3 %collective-permute-start.24 = (bf16[32,8192]{1,0:T(8,128)(2,1)}, bf16[32,8192]{1,0:T(8,128)(2,1)}, u32[]{:S(2)}, u32[]{:S(2)}) collective-permute-start(bf16[32,8192]{1,0:T(8,128)(2,1)} %add_convert_fusion.6), channel_id=1, source_target_pairs={{0,2},{1,3},{2,0},{3,1},{4,6},{5,7},{6,4},{7,5},{8,10},{9,11},{10,... | collective-permute-start | bytes 1572872 | tf_op jit(solution)/shard_map/ppermute | solution.py:692
  110.4 11.9 %collective-permute-start.30 = (f32[8,128]{1,0:T(8,128)S(1)}, f32[8,128]{1,0:T(8,128)S(1)}, u32[]{:S(2)}, u32[]{:S(2)}) collective-permute-start(f32[8,128]{1,0:T(8,128)S(1)} %add.143), channel_id=1, source_target_pairs={{0,2},{1,3},{2,0},{3,1},{4,6},{5,7},{6,4},{7,5},{8,10},{9,11},{10,... | collective-permute-start | bytes 12296 | tf_op jit(solution)/shard_map/ppermute | solution.py:692
  123.9 14.9 %collective-permute-start.31 = (bf16[32,8192]{1,0:T(8,128)(2,1)S(1)}, bf16[32,8192]{1,0:T(8,128)(2,1)S(1)}, u32[]{:S(2)}, u32[]{:S(2)}) collective-permute-start(bf16[32,8192]{1,0:T(8,128)(2,1)S(1)} %multiply_convert_fusion), channel_id=1, source_target_pairs={{0,4},{1,5},{2,6},{3,7},{4,8},{5,9},{6,10},{7,11},{8,12},{9,13},{1... | collective-permute-start | bytes 1572872 | tf_op jit(solution)/shard_map/ppermute | solution.py:692
  125.3 13.5 %collective-permute-start.28 = (bf16[32,8192]{1,0:T(8,128)(2,1)S(1)}, bf16[32,8192]{1,0:T(8,128)(2,1)S(1)}, u32[]{:S(2)}, u32[]{:S(2)}) collective-permute-start(bf16[32,8192]{1,0:T(8,128)(2,1)S(1)} %add_convert_fusion.5), channel_id=1, source_target_pairs={{0,2},{1,3},{2,0},{3,1},{4,6},{5,7},{6,4},{7,5},{8,10},{9,11},{10,... | collective-permute-start | bytes 1572872 | tf_op jit(solution)/shard_map/ppermute | solution.py:692
  140.2 14.0 %collective-permute-start.33 = (bf16[32,8192]{1,0:T(8,128)(2,1)S(1)}, bf16[32,8192]{1,0:T(8,128)(2,1)S(1)}, u32[]{:S(2)}, u32[]{:S(2)}) collective-permute-start(bf16[32,8192]{1,0:T(8,128)(2,1)S(1)} %add_convert_fusion.3), channel_id=1, source_target_pairs={{0,4},{1,5},{2,6},{3,7},{4,8},{5,9},{6,10},{7,11},{8,12},{9,13},{1... | collective-permute-start | bytes 1572872 | tf_op jit(solution)/shard_map/ppermute | solution.py:692
  141.4 12.7 %collective-permute-start.32 = (bf16[32,8192]{1,0:T(8,128)(2,1)S(1)}, bf16[32,8192]{1,0:T(8,128)(2,1)S(1)}, u32[]{:S(2)}, u32[]{:S(2)}) collective-permute-start(bf16[32,8192]{1,0:T(8,128)(2,1)S(1)} %add_convert_fusion.4), channel_id=1, source_target_pairs={{0,2},{1,3},{2,0},{3,1},{4,6},{5,7},{6,4},{7,5},{8,10},{9,11},{10,... | collective-permute-start | bytes 1572872 | tf_op jit(solution)/shard_map/ppermute | solution.py:692
  155.5 13.0 %collective-permute-start.35 = (bf16[32,8192]{1,0:T(8,128)(2,1)S(1)}, bf16[32,8192]{1,0:T(8,128)(2,1)S(1)}, u32[]{:S(2)}, u32[]{:S(2)}) collective-permute-start(bf16[32,8192]{1,0:T(8,128)(2,1)S(1)} %add_convert_fusion.1), channel_id=1, source_target_pairs={{0,4},{1,5},{2,6},{3,7},{4,8},{5,9},{6,10},{7,11},{8,12},{9,13},{1... | collective-permute-start | bytes 1572872 | tf_op jit(solution)/shard_map/ppermute | solution.py:692
  156.8 11.8 %collective-permute-start.34 = (bf16[32,8192]{1,0:T(8,128)(2,1)S(1)}, bf16[32,8192]{1,0:T(8,128)(2,1)S(1)}, u32[]{:S(2)}, u32[]{:S(2)}) collective-permute-start(bf16[32,8192]{1,0:T(8,128)(2,1)S(1)} %add_convert_fusion.2), channel_id=1, source_target_pairs={{0,2},{1,3},{2,0},{3,1},{4,6},{5,7},{6,4},{7,5},{8,10},{9,11},{10,... | collective-permute-start | bytes 1572872 | tf_op jit(solution)/shard_map/ppermute | solution.py:692
  (46 other events, 545.1 us)

commit v4 on v3

--- a/solution.py
+++ b/solution.py
@@ -512,26 +512,28 @@
                 at = pl.multiple_of(((plane * 2 + at_level) * 2 + at_side) * rows, rows)
                 parts.append(gated_ref[pl.ds(at, rows), :])
     left = jnp.concatenate(parts, axis=0)
-    tile = 1024
-    for col in range(0, weight_ref.shape[1], tile):
-        result = jnp.dot(
-            left, weight_ref[:, col : col + tile], preferred_element_type=jnp.float32
-        ).astype(jnp.bfloat16)
-        at = 0
-        for out in outs:
-            out[:, col : col + tile] = result[at : at + out.shape[0]]
-            at += out.shape[0]
+    tile = outs[0].shape[1]
+    col = pl.multiple_of(pl.program_id(0) * tile, tile)
+    result = jnp.dot(
+        left, weight_ref[:, pl.ds(col, tile)], preferred_element_type=jnp.float32
+    ).astype(jnp.bfloat16)
+    at = 0
+    for out in outs:
+        out[...] = result[at : at + out.shape[0]]
+        at += out.shape[0]
 
 
 def out_part(spots, gated, weight, planes, steps):
     width = weight.shape[1]
     rows = gated.shape[0] // planes // PLANE
     shapes = [2 * rows, rows, rows] * len(steps)
+    tile = 1024
     outs = pl.pallas_call(
         functools.partial(out_kernel, planes=planes, steps=steps),
-        out_shape=tuple(jax.ShapeDtypeStruct((high, width), jnp.bfloat16) for high in shapes),
+        grid=(width // tile,),
+        out_shape=tuple(pltpu.MemorySpace.HBM((high, width), jnp.bfloat16) for high in shapes),
         in_specs=[smem(), vmem(), vmem()],
-        out_specs=(vmem(),) * len(shapes),
+        out_specs=tuple(pl.BlockSpec((high, tile), lambda i: (0, i)) for high in shapes),
         compiler_params=pltpu.CompilerParams(vmem_limit_bytes=VMEM_LIMIT),
         cost_estimate=pl.CostEstimate(
             flops=len(steps) << 30, bytes_accessed=len(steps) << 21, transcendentals=0
@@ -755,9 +757,8 @@
         if step == 0:
             extra["spec"] = (spec, destination)
         else:
-            extra["result"] = compute(step - 1)
-            if step < 3:
-                picked = pick(step - 1, picked)
+            extra["result"] = compute(step - 1, *([in_x] if last else []))
+            picked = pick(step - 1, picked)
         if step == 1:
             extra["consts"] = scan_constants(*spec, z_pos, planes)
             extra["place"] = own_slots(own_dest)
@@ -771,7 +772,9 @@
         if not last:
             straight.append(group[2])
         if step:
-            results.append(extra["result"])
+            result = extra["result"]
+            results.append(result[:3])
+            near_x = result[3] if last else None
         else:
             spec, own_dest = extra["spec"]
         if step == 1:
@@ -781,7 +784,7 @@
         if step >= 2:
             peers.append(extra["peer"])
     crossed_core.append(over(crossed[-1], over_core))
-    *result, near_x, near_z = compute(planes - 1, in_x, in_z)
+    *result, near_z = compute(planes - 1, in_z)
     results.append(result)
 
     normed, pieces, dts = zip(*results)
@@ -790,6 +793,7 @@
     both, normed = lax.optimization_barrier((both, normed[2:]))
     far_pieces = send_far(both)
     second = project_planes(normed, near_x, near_z)
+    far_pieces, picked = lax.optimization_barrier((far_pieces, pick(planes - 1, picked)))
     xs, zs = [first[i] + second[i] for i in range(2)]
     gated, squares, held_out = scan_all(spots, xs, zs, dts, far_pieces, consts, out_weight, heads)
 
@@ -797,27 +801,41 @@
     squares = squares + permute(squares, over_y)
     scale = lax.rsqrt(squares[:planes].reshape(-1) / (INNER // GROUPS) + 1e-05)
 
-    mine = [
-        lax.dynamic_slice_in_dim(scale, ((z_pos - 1 - step) % planes * PLANE + spot) * rows, rows)[:, None]
-        for step in range(planes)
-    ]
-    outs = out_part(spots, gated, held_out, planes, (0,))
-    got = [permute(outs[0][0], over_core)]
-    outs += out_part(spots, gated, held_out, planes, tuple(range(1, planes)))
-    got += [permute(away, over_core) for away, _, _ in outs[1:]]
+    def scale_of(step, at_spot):
+        start = ((z_pos - 1 - step) % planes * PLANE + at_spot) * rows
+        return lax.dynamic_slice_in_dim(scale, start, rows)[:, None]
+
+    mine = [scale_of(step, spot) for step in range(planes)]
+    theirs = [scale_of(step, spot ^ 2) for step in range(planes)]
+    outs = out_part(spots, gated, held_out, planes, tuple(range(planes)))
+    got = [permute(away, over_core) for away, _, _ in outs]
+
+    def send_of(step):
+        return outs[step][1].astype(f32) + got[step][:rows].astype(f32)
+
+    send = send_of(0)
+    aside = permute((send[half:] * theirs[0][half:]).astype(jnp.bfloat16), ring)
+    send = send[:half].astype(jnp.bfloat16)
     total = None
     for step in range(planes):
-        send = (outs[step][1].astype(f32) + got[step][:rows].astype(f32)).astype(jnp.bfloat16)
         group = [permute(send, over_y)]
         if step:
             group.append(permute(total.astype(jnp.bfloat16), ring))
-        if step in (1, 2):
-            picked = pick(planes - 3 + step, picked)
-        group, got, picked, outs = lax.optimization_barrier((group, got, picked, outs))
+        else:
+            group.append(aside)
+        group = lax.optimization_barrier(group)
+        if step + 1 < planes:
+            send = send_of(step + 1) * theirs[step + 1]
+            if step == 0:
+                send = jnp.concatenate([send[:half], send[half:] + group[1].astype(f32)], axis=0)
+            send = send.astype(jnp.bfloat16)
         total = outs[step][2].astype(f32) + got[step][rows:].astype(f32)
-        total = (total + group[0].astype(f32)) * mine[step]
         if step:
-            total = total + group[1].astype(f32)
+            total = total * mine[step] + group[0].astype(f32) + group[1].astype(f32)
+        else:
+            total = (
+                jnp.concatenate([total[:half] + group[0].astype(f32), total[half:]], axis=0) * mine[0]
+            )
     layer_out = (hidden.astype(f32) + total).astype(jnp.bfloat16)
 
     filled = jnp.dot(place, layer_out, preferred_element_type=f32).astype(jnp.bfloat16)

time: 192 us -> 180 us (0.938)
  other arithmetic: 16 us -> 9.07 us
  blocking collectives: 19.3 us -> 17.1 us
  Pallas kernels: 50.3 us -> 48.3 us
    convert_element_type x4 -> x3, other arithmetic: 4.67 us -> 0.44 us  [the longest x2 0.34 us: on_device_planes(): send = send.astype(jnp.bfloat16)]
    convert_element_type x3, other arithmetic: 4.21 us -> 0.77 us  [on_device_planes(): group.append(permute(total.astype(jnp.bfloat16), ring))]
    all_to_all x1, blocking collectives: 19.3 us -> 17.1 us  [on_device_planes(): lax.all_to_all(filled.reshape(count, CAP, width), 'tensor', split_axis=0,...]
    ppermute x36 -> x37, waiting for transfers between devices: 83.9 us -> 83.5 us  [permute(): return lax.ppermute(value, 'tensor', pairs)]
    pallas_call x2 -> x1, Pallas kernels: 7.84 us -> 7.56 us  [out_part(): pl.pallas_call(functools.partial(out_kernel, planes=planes, steps=steps),...]
    ppermute x36 -> x37, starting transfers between devices: 17.4 us -> 17.6 us  [permute(): return lax.ppermute(value, 'tensor', pairs)]
  transfers between devices with their start and end apart: 36 -> 37, of which waited for: 20 -> 23; matrix products, arithmetic and copies ran while one was open for 4% -> 4% of each run, Pallas kernels for 22% -> 19%
where the time goes in v4:
time: 180 us; the launch traced here: 179 us
  waiting for transfers between devices  83.5 us (46%)
  Pallas kernels  48.3 us (27%)
  starting transfers between devices  17.6 us (10%)
  blocking collectives  17.1 us (10%)
  other arithmetic  9.07 us (5%)
  local copies, waits for them, and re-layouts  1.89 us (1%)
    ppermute x37, waiting for transfers between devices, permute(): return lax.ppermute(value, 'tensor', pairs)  83.5 us
    ppermute x37, starting transfers between devices, permute(): return lax.ppermute(value, 'tensor', pairs)  17.6 us
    pallas_call x4, Pallas kernels, norm_plane(): pl.pallas_call(functools.partial(norm_kernel, pieces=tuple((len(block) fo...  17.2 us
    all_to_all x1, blocking collectives, on_device_planes(): lax.all_to_all(filled.reshape(count, CAP, width), 'tensor', split_axis=0,...  17.1 us
    pallas_call x2, Pallas kernels, project_planes(): pl.pallas_call(functools.partial(project_kernel, planes=count), out_shape...  9.06 us
    pallas_call x1, Pallas kernels, out_part(): pl.pallas_call(functools.partial(out_kernel, planes=planes, steps=steps),...  7.56 us
    pallas_call x4, Pallas kernels, pick_plane(): pl.pallas_call(functools.partial(pick_kernel, pieces=tuple((len(block) fo...  7.14 us
    pallas_call x1, Pallas kernels, scan_all(): pl.pallas_call(functools.partial(scan_kernel, heads=heads, planes=planes)...  6.47 us
  transfers between devices with their start and end apart: 37, of which 23 were waited for; matrix products, arithmetic and copies ran while one was open for 4% of the time, Pallas kernels for 19%

profile of v4, /device:TPU:0, one launch (start us, length us, event | category | flops | bytes accessed | tf_op | source)
XLA Modules:
  0.0 179.0 jit_solution(16140407236114795705)
XLA Ops:
  3.8 2.5 %collective-permute-start.1 = (bf16[32,8320]{1,0:T(8,128)(2,1)}, bf16[32,8320]{1,0:T(8,128)(2,1)}, u32[]{:S(2)}, u32[]{:S(2)}) collective-permute-start(bf16[32,8320]{1,0:T(8,128)(2,1)} %pad_maximum_fusion.1.refs_0_), channel_id=1, source_target_pairs={{0,2},{1,3},{2,0},{3,1},{4,6},{5,7},{6,4},{7,5},{8,10},{9,11},{10,... | collective-permute-start | bytes 1597448 | tf_op jit(solution)/shard_map/ppermute | solution.py:694
  9.8 9.6 %collective-permute-done.1.refs_2_ = bf16[32,8320]{1,0:T(8,128)(2,1)} collective-permute-done((bf16[32,8320]{1,0:T(8,128)(2,1)}, bf16[32,8320]{1,0:T(8,128)(2,1)}, u32[]{:S(2)}, u32[]{:S(2)}) %collective-permute-start.1) | collective-permute-done | bytes 532512 | tf_op jit(solution)/shard_map/ppermute | solution.py:694
  19.4 3.4 %collective-permute-done.2.refs_0_ = bf16[32,8320]{1,0:T(8,128)(2,1)} collective-permute-done((bf16[32,8320]{1,0:T(8,128)(2,1)}, bf16[32,8320]{1,0:T(8,128)(2,1)}, u32[]{:S(2)}, u32[]{:S(2)}) %collective-permute-start.2) | collective-permute-done | bytes 532512 | tf_op jit(solution)/shard_map/ppermute | solution.py:694
  25.8 2.3 %pick_plane.4.refs_4_ = bf16[32,8192]{1,0:T(8,128)(2,1)S(1)} custom-call(s32[2]{0:T(128)S(1)} %pad_add_fusion.spot_ref.spots, bf16[32,8320]{1,0:T(8,128)(2,1)} %pad_maximum_fusion.1.refs_0_, bf16[32,8320]{1,0:T(8,128)(2,1)} %collective-permute-done.refs_1_, bf16[32,8320]{1,0:T(8,128)(2,1)} %collective-permute-done.1.refs_2_, ...), custom_call_target="tpu_custom_call" | custom-call | flops 1073741824 | bytes 3145728 | tf_op jit(solution)/shard_map/pick_plane/pallas_call | solution.py:576
  28.1 4.5 %norm_plane.4 = (bf16[128,8192]{1,0:T(8,128)(2,1)S(1)}, bf16[128,64]{1,0:T(8,128)(2,1)S(1)}, f32[128,128]{1,0:T(8,128)S(1)}) custom-call(s32[2]{0:T(128)S(1)} %pad_add_fusion.spot_ref.spots, bf16[32,8320]{1,0:T(8,128)(2,1)} %pad_maximum_fusion.1.refs_0_, bf16[32,8320]{1,0:T(8,128)(2,1)} %collective-permute-done.refs_1_, ...), custom_call_target="tpu_custom_call" | custom-call | flops 2147483648 | bytes 6291456 | tf_op jit(solution)/shard_map/norm_plane/pallas_call | solution.py:277
  32.6 5.0 %collective-permute-done.4.refs_2_ = bf16[32,8320]{1,0:T(8,128)(2,1)} collective-permute-done((bf16[32,8320]{1,0:T(8,128)(2,1)}, bf16[32,8320]{1,0:T(8,128)(2,1)}, u32[]{:S(2)}, u32[]{:S(2)}) %collective-permute-start.4) | collective-permute-done | bytes 532512 | tf_op jit(solution)/shard_map/ppermute | solution.py:694
  41.8 3.6 %norm_plane.5 = (bf16[128,8192]{1,0:T(8,128)(2,1)S(1)}, bf16[128,64]{1,0:T(8,128)(2,1)S(1)}, f32[128,128]{1,0:T(8,128)S(1)}) custom-call(s32[2]{0:T(128)S(1)} %pad_add_fusion.spot_ref.spots, bf16[32,8320]{1,0:T(8,128)(2,1)} %collective-permute-done.2.refs_0_, bf16[32,8320]{1,0:T(8,128)(2,1)} %collective-permute-done.3.refs_1_, ...), custom_call_target="tpu_custom_call" | custom-call | flops 2147483648 | bytes 6291456 | tf_op jit(solution)/shard_map/norm_plane/pallas_call | solution.py:277
  45.4 4.5 %project_planes.2 = (bf16[128,512]{1,0:T(8,128)(2,1)S(1)}, bf16[128,512]{1,0:T(8,128)(2,1)S(1)}, bf16[128,512]{1,0:T(8,128)(2,1)S(1)}, bf16[128,512]{1,0:T(8,128)(2,1)S(1)}) custom-call(bf16[128,8192]{1,0:T(8,128)(2,1)S(1)} %get-tuple-element.123.refs_0_, bf16[128,8192]{1,0:T(8,128)(2,1)S(1)} %get-tuple-element.126.refs_1_, bf16[512,8192]{1,0:T(8,128)(2,1)S(1)} %bitcast.20, ...), custom_call_target="tpu_custom_call" | custom-call | flops 4294967296 | bytes 4194304 | tf_op jit(solution)/shard_map/project_planes/pallas_call | solution.py:318
  52.0 2.4 %collective-permute-done.8.refs_2_ = bf16[32,8320]{1,0:T(8,128)(2,1)S(1)} collective-permute-done((bf16[32,8320]{1,0:T(8,128)(2,1)}, bf16[32,8320]{1,0:T(8,128)(2,1)S(1)}, u32[]{:S(2)}, u32[]{:S(2)}) %collective-permute-start.8) | collective-permute-done | bytes 532512 | tf_op jit(solution)/shard_map/ppermute | solution.py:694
  54.3 3.0 %collective-permute-done.9.refs_0_ = bf16[32,8320]{1,0:T(8,128)(2,1)S(1)} collective-permute-done((bf16[32,8320]{1,0:T(8,128)(2,1)}, bf16[32,8320]{1,0:T(8,128)(2,1)S(1)}, u32[]{:S(2)}, u32[]{:S(2)}) %collective-permute-start.9) | collective-permute-done | bytes 532512 | tf_op jit(solution)/shard_map/ppermute | solution.py:694
  59.3 4.4 %norm_plane.6 = (bf16[128,8192]{1,0:T(8,128)(2,1)S(1)}, bf16[128,64]{1,0:T(8,128)(2,1)S(1)}, f32[128,128]{1,0:T(8,128)S(1)}, bf16[512,8192]{1,0:T(8,128)(2,1)S(1)}) custom-call(s32[2]{0:T(128)S(1)} %pad_add_fusion.spot_ref.spots, bf16[32,8320]{1,0:T(8,128)(2,1)} %collective-permute-done.5.refs_0_, bf16[32,8320]{1,0:T(8,128)(2,1)S(1)} %collective-permute-done.7.refs_1_, ...), custom_call_target="tpu_custom_call" | custom-call | flops 2147483648 | bytes 6291456 | tf_op jit(solution)/shard_map/norm_plane/pallas_call | solution.py:277
  70.3 4.6 %norm_plane.7 = (bf16[128,8192]{1,0:T(8,128)(2,1)S(1)}, bf16[128,64]{1,0:T(8,128)(2,1)S(1)}, f32[128,128]{1,0:T(8,128)S(1)}, bf16[512,8192]{1,0:T(8,128)(2,1)S(1)}) custom-call(s32[2]{0:T(128)S(1)} %pad_add_fusion.spot_ref.spots, bf16[32,8320]{1,0:T(8,128)(2,1)S(1)} %collective-permute-done.9.refs_0_, bf16[32,8320]{1,0:T(8,128)(2,1)S(1)} %collective-permute-done.12.refs_1_, ...), custom_call_target="tpu_custom_call" | custom-call | flops 2147483648 | bytes 6291456 | tf_op jit(solution)/shard_map/norm_plane/pallas_call | solution.py:277
  77.7 2.8 %collective-permute-start.22 = (bf16[512,128]{1,0:T(8,128)(2,1)S(1)}, bf16[512,128]{1,0:T(8,128)(2,1)S(1)}, u32[]{:S(2)}, u32[]{:S(2)}) collective-permute-start(bf16[512,128]{1,0:T(8,128)(2,1)S(1)} %pair_pieces.1), channel_id=1, source_target_pairs={{0,2},{1,3},{2,6},{3,7},{4,10},{5,11},{6,14},{7,15},{8,0},{9,1},{1... | collective-permute-start | bytes 393224 | tf_op jit(solution)/shard_map/ppermute | solution.py:694
  80.5 4.5 %project_planes.3 = (bf16[128,512]{1,0:T(8,128)(2,1)S(1)}, bf16[128,512]{1,0:T(8,128)(2,1)S(1)}, bf16[128,512]{1,0:T(8,128)(2,1)S(1)}, bf16[128,512]{1,0:T(8,128)(2,1)S(1)}) custom-call(bf16[128,8192]{1,0:T(8,128)(2,1)S(1)} %get-tuple-element.155.refs_0_, bf16[128,8192]{1,0:T(8,128)(2,1)S(1)} %get-tuple-element.156.refs_1_, ...), custom_call_target="tpu_custom_call" | custom-call | flops 4294967296 | bytes 4194304 | tf_op jit(solution)/shard_map/project_planes/pallas_call | solution.py:318
  85.1 4.3 %collective-permute-done.22.refs_13_ = bf16[512,128]{1,0:T(8,128)(2,1)S(1)} collective-permute-done((bf16[512,128]{1,0:T(8,128)(2,1)S(1)}, bf16[512,128]{1,0:T(8,128)(2,1)S(1)}, u32[]{:S(2)}, u32[]{:S(2)}) %collective-permute-start.22) | collective-permute-done | bytes 131104 | tf_op jit(solution)/shard_map/ppermute | solution.py:694
  89.4 6.5 %scan_all.1 = (bf16[512,512]{1,0:T(8,128)(2,1)S(1)}, f32[8,128]{1,0:T(8,128)S(1)}, bf16[512,8192]{1,0:T(8,128)(2,1)S(1)}) custom-call(s32[2]{0:T(128)S(1)} %pad_add_fusion.spot_ref.spots, bf16[128,512]{1,0:T(8,128)(2,1)S(1)} %get-tuple-element.135.refs_0_, bf16[128,512]{1,0:T(8,128)(2,1)S(1)} %get-tuple-element.136.refs_1_, ...), custom_call_target="tpu_custom_call" | custom-call | flops 1073741824 | bytes 8388608 | tf_op jit(solution)/shard_map/scan_all/pallas_call | solution.py:480
  95.8 7.6 %out_part.1 = (bf16[64,8192]{1,0:T(8,128)(2,1)}, bf16[32,8192]{1,0:T(8,128)(2,1)}, bf16[32,8192]{1,0:T(8,128)(2,1)}, bf16[64,8192]{1,0:T(8,128)(2,1)}, bf16[32,8...) custom-call(s32[2]{0:T(128)S(1)} %pad_add_fusion.spot_ref.spots, ...), custom_call_target="tpu_custom_call" | custom-call | flops 4294967296 | bytes 8388608 | tf_op jit(solution)/shard_map/out_part/pallas_call | solution.py:531
  106.7 2.7 %collective-permute-done.25 = f32[8,128]{1,0:T(8,128)S(1)} collective-permute-done((f32[8,128]{1,0:T(8,128)S(1)}, f32[8,128]{1,0:T(8,128)S(1)}, u32[]{:S(2)}, u32[]{:S(2)}) %collective-permute-start.25) | collective-permute-done | bytes 4128 | tf_op jit(solution)/shard_map/ppermute | solution.py:694
  112.0 8.4 %collective-permute-done.32 = bf16[16,8192]{1,0:T(8,128)(2,1)S(1)} collective-permute-done((bf16[16,8192]{1,0:T(8,128)(2,1)S(1)}, bf16[16,8192]{1,0:T(8,128)(2,1)S(1)}, u32[]{:S(2)}, u32[]{:S(2)}) %collective-permute-start.32) | collective-permute-done | bytes 262176 | tf_op jit(solution)/shard_map/ppermute | solution.py:694
  123.4 11.5 %collective-permute-done.34 = bf16[32,8192]{1,0:T(8,128)(2,1)S(1)} collective-permute-done((bf16[32,8192]{1,0:T(8,128)(2,1)S(1)}, bf16[32,8192]{1,0:T(8,128)(2,1)S(1)}, u32[]{:S(2)}, u32[]{:S(2)}) %collective-permute-start.34) | collective-permute-done | bytes 524320 | tf_op jit(solution)/shard_map/ppermute | solution.py:694
  136.9 10.3 %collective-permute-done.28 = bf16[32,8192]{1,0:T(8,128)(2,1)S(1)} collective-permute-done((bf16[32,8192]{1,0:T(8,128)(2,1)S(1)}, bf16[32,8192]{1,0:T(8,128)(2,1)S(1)}, u32[]{:S(2)}, u32[]{:S(2)}) %collective-permute-start.28) | collective-permute-done | bytes 524320 | tf_op jit(solution)/shard_map/ppermute | solution.py:694
  148.6 7.1 %collective-permute-done.26 = bf16[32,8192]{1,0:T(8,128)(2,1)S(1)} collective-permute-done((bf16[32,8192]{1,0:T(8,128)(2,1)S(1)}, bf16[32,8192]{1,0:T(8,128)(2,1)S(1)}, u32[]{:S(2)}, u32[]{:S(2)}) %collective-permute-start.26) | collective-permute-done | bytes 524320 | tf_op jit(solution)/shard_map/ppermute | solution.py:694
  155.7 3.9 %collective-permute-done.36 = bf16[32,8192]{1,0:T(8,128)(2,1)S(1)} collective-permute-done((bf16[32,8192]{1,0:T(8,128)(2,1)S(1)}, bf16[32,8192]{1,0:T(8,128)(2,1)S(1)}, u32[]{:S(2)}, u32[]{:S(2)}) %collective-permute-start.36) | collective-permute-done | bytes 524320 | tf_op jit(solution)/shard_map/ppermute | solution.py:694
  160.6 17.1 %all_to_all.5 = bf16[16,2,8192]{2,1,0:T(2,128)(2,1)S(1)} all-to-all(bf16[16,2,8192]{2,1,0:T(2,128)(2,1)S(1)} %reshape.43), channel_id=1, replica_groups=mesh['rep'=2,'dp'=1,'tensor'=16] {'tensor'}, dimensions={0} | all-to-all | bytes 1048576 | tf_op jit(solution)/shard_map/all_to_all | solution.py:842
  (150 shorter events, 41.2 us)
Async XLA Ops:
  3.8 15.6 %collective-permute-start.1 = (bf16[32,8320]{1,0:T(8,128)(2,1)}, bf16[32,8320]{1,0:T(8,128)(2,1)}, u32[]{:S(2)}, u32[]{:S(2)}) collective-permute-start(bf16[32,8320]{1,0:T(8,128)(2,1)} %pad_maximum_fusion.1.refs_0_), channel_id=1, source_target_pairs={{0,2},{1,3},{2,0},{3,1},{4,6},{5,7},{6,4},{7,5},{8,10},{9,11},{10,... | collective-permute-start | bytes 1597448 | tf_op jit(solution)/shard_map/ppermute | solution.py:694
  6.3 16.4 %collective-permute-start.2 = (bf16[32,8320]{1,0:T(8,128)(2,1)}, bf16[32,8320]{1,0:T(8,128)(2,1)}, u32[]{:S(2)}, u32[]{:S(2)}) collective-permute-start(bf16[32,8320]{1,0:T(8,128)(2,1)} %pad_maximum_fusion.1.refs_0_), channel_id=1, source_target_pairs={{0,4},{1,5},{2,6},{3,7},{4,8},{5,9},{6,10},{7,11},{8,12},{9,13},{1... | collective-permute-start | bytes 1597448 | tf_op jit(solution)/shard_map/ppermute | solution.py:694
  22.8 9.8 %collective-permute-start.3 = (bf16[32,8320]{1,0:T(8,128)(2,1)}, bf16[32,8320]{1,0:T(8,128)(2,1)}, u32[]{:S(2)}, u32[]{:S(2)}) collective-permute-start(bf16[32,8320]{1,0:T(8,128)(2,1)} %collective-permute-done.2.refs_0_), channel_id=1, source_target_pairs={{0,1},{1,0},{2,3},{3,2},{4,5},{5,4},{6,7},{7,6},{8,9},{9,8},{10,11... | collective-permute-start | bytes 1597448 | tf_op jit(solution)/shard_map/ppermute | solution.py:694
  22.8 14.8 %collective-permute-start.4 = (bf16[32,8320]{1,0:T(8,128)(2,1)}, bf16[32,8320]{1,0:T(8,128)(2,1)}, u32[]{:S(2)}, u32[]{:S(2)}) collective-permute-start(bf16[32,8320]{1,0:T(8,128)(2,1)} %collective-permute-done.2.refs_0_), channel_id=1, source_target_pairs={{0,2},{1,3},{2,0},{3,1},{4,6},{5,7},{6,4},{7,5},{8,10},{9,11},{10,... | collective-permute-start | bytes 1597448 | tf_op jit(solution)/shard_map/ppermute | solution.py:694
  23.3 16.3 %collective-permute-start.5 = (bf16[32,8320]{1,0:T(8,128)(2,1)}, bf16[32,8320]{1,0:T(8,128)(2,1)}, u32[]{:S(2)}, u32[]{:S(2)}) collective-permute-start(bf16[32,8320]{1,0:T(8,128)(2,1)} %collective-permute-done.2.refs_0_), channel_id=1, source_target_pairs={{0,4},{1,5},{2,6},{3,7},{4,8},{5,9},{6,10},{7,11},{8,12},{9,13},{1... | collective-permute-start | bytes 1597448 | tf_op jit(solution)/shard_map/ppermute | solution.py:694
  39.6 12.3 %collective-permute-start.7 = (bf16[32,8320]{1,0:T(8,128)(2,1)}, bf16[32,8320]{1,0:T(8,128)(2,1)S(1)}, u32[]{:S(2)}, u32[]{:S(2)}) collective-permute-start(bf16[32,8320]{1,0:T(8,128)(2,1)} %collective-permute-done.5.refs_0_), channel_id=1, source_target_pairs={{0,1},{1,0},{2,3},{3,2},{4,5},{5,4},{6,7},{7,6},{8,9},{9,8},{10,11... | collective-permute-start | bytes 1597448 | tf_op jit(solution)/shard_map/ppermute | solution.py:694
  40.1 14.2 %collective-permute-start.8 = (bf16[32,8320]{1,0:T(8,128)(2,1)}, bf16[32,8320]{1,0:T(8,128)(2,1)S(1)}, u32[]{:S(2)}, u32[]{:S(2)}) collective-permute-start(bf16[32,8320]{1,0:T(8,128)(2,1)} %collective-permute-done.5.refs_0_), channel_id=1, source_target_pairs={{0,2},{1,3},{2,0},{3,1},{4,6},{5,7},{6,4},{7,5},{8,10},{9,11},{10,... | collective-permute-start | bytes 1597448 | tf_op jit(solution)/shard_map/ppermute | solution.py:694
  41.6 15.7 %collective-permute-start.9 = (bf16[32,8320]{1,0:T(8,128)(2,1)}, bf16[32,8320]{1,0:T(8,128)(2,1)S(1)}, u32[]{:S(2)}, u32[]{:S(2)}) collective-permute-start(bf16[32,8320]{1,0:T(8,128)(2,1)} %collective-permute-done.5.refs_0_), channel_id=1, source_target_pairs={{0,4},{1,5},{2,6},{3,7},{4,8},{5,9},{6,10},{7,11},{8,12},{9,13},{1... | collective-permute-start | bytes 1597448 | tf_op jit(solution)/shard_map/ppermute | solution.py:694
  41.7 10.3 %collective-permute-start.11 = (bf16[128,64]{1,0:T(8,128)(2,1)S(1)}, bf16[128,64]{1,0:T(8,128)(2,1)S(1)}, u32[]{:S(2)}, u32[]{:S(2)}) collective-permute-start(bf16[128,64]{1,0:T(8,128)(2,1)S(1)} %get-tuple-element.131.refs_0_), channel_id=1, source_target_pairs={{0,1},{1,0},{2,3},{3,2},{4,5},{5,4},{6,7},{7,6},{8,9},{9,8},{10,11... | collective-permute-start | bytes 49160 | tf_op jit(solution)/shard_map/ppermute | solution.py:694
  57.4 11.0 %collective-permute-start.12 = (bf16[32,8320]{1,0:T(8,128)(2,1)S(1)}, bf16[32,8320]{1,0:T(8,128)(2,1)S(1)}, u32[]{:S(2)}, u32[]{:S(2)}) collective-permute-start(bf16[32,8320]{1,0:T(8,128)(2,1)S(1)} %collective-permute-done.9.refs_0_), channel_id=1, source_target_pairs={{0,1},{1,0},{2,3},{3,2},{4,5},{5,4},{6,7},{7,6},{8,9},{9,8},{10,11... | collective-permute-start | bytes 1597448 | tf_op jit(solution)/shard_map/ppermute | solution.py:694
  57.9 8.4 %collective-permute-start.13 = (bf16[16,8320]{1,0:T(8,128)(2,1)S(1)}, bf16[16,8320]{1,0:T(8,128)(2,1)S(1)}, u32[]{:S(2)}, u32[]{:S(2)}) collective-permute-start(bf16[16,8320]{1,0:T(8,128)(2,1)S(1)} %slice.57), channel_id=1, source_target_pairs={{0,2},{1,3},{2,0},{3,1},{4,6},{5,7},{6,4},{7,5},{8,10},{9,11},{10,... | collective-permute-start | bytes 798728 | tf_op jit(solution)/shard_map/ppermute | solution.py:694
  58.5 9.8 %collective-permute-start.14 = (bf16[16,8320]{1,0:T(8,128)(2,1)S(1)}, bf16[16,8320]{1,0:T(8,128)(2,1)S(1)}, u32[]{:S(2)}, u32[]{:S(2)}) collective-permute-start(bf16[16,8320]{1,0:T(8,128)(2,1)S(1)} %slice.58), channel_id=1, source_target_pairs={{0,4},{1,5},{2,6},{3,7},{4,8},{5,9},{6,10},{7,11},{8,12},{9,13},{1... | collective-permute-start | bytes 798728 | tf_op jit(solution)/shard_map/ppermute | solution.py:694
  77.0 8.0 %collective-permute-start.21 = (bf16[512,128]{1,0:T(8,128)(2,1)S(1)}, bf16[512,128]{1,0:T(8,128)(2,1)S(1)}, u32[]{:S(2)}, u32[]{:S(2)}) collective-permute-start(bf16[512,128]{1,0:T(8,128)(2,1)S(1)} %pair_pieces.1), channel_id=1, source_target_pairs={{0,0},{1,1},{2,4},{3,5},{4,8},{5,9},{6,12},{7,13},{8,2},{9,3},{10,... | collective-permute-start | bytes 393224 | tf_op jit(solution)/shard_map/ppermute | solution.py:694
  77.7 11.7 %collective-permute-start.22 = (bf16[512,128]{1,0:T(8,128)(2,1)S(1)}, bf16[512,128]{1,0:T(8,128)(2,1)S(1)}, u32[]{:S(2)}, u32[]{:S(2)}) collective-permute-start(bf16[512,128]{1,0:T(8,128)(2,1)S(1)} %pair_pieces.1), channel_id=1, source_target_pairs={{0,2},{1,3},{2,6},{3,7},{4,10},{5,11},{6,14},{7,15},{8,0},{9,1},{1... | collective-permute-start | bytes 393224 | tf_op jit(solution)/shard_map/ppermute | solution.py:694
  106.2 15.3 %collective-permute-start.27 = (bf16[64,8192]{1,0:T(8,128)(2,1)}, bf16[64,8192]{1,0:T(8,128)(2,1)S(1)}, u32[]{:S(2)}, u32[]{:S(2)}) collective-permute-start(bf16[64,8192]{1,0:T(8,128)(2,1)} %get-tuple-element.188), channel_id=1, source_target_pairs={{0,1},{1,0},{2,3},{3,2},{4,5},{5,4},{6,7},{7,6},{8,9},{9,8},{10,11... | collective-permute-start | bytes 3145736 | tf_op jit(solution)/shard_map/ppermute | solution.py:694
  106.3 30.1 %collective-permute-start.23 = (bf16[64,8192]{1,0:T(8,128)(2,1)}, bf16[64,8192]{1,0:T(8,128)(2,1)S(1)}, u32[]{:S(2)}, u32[]{:S(2)}) collective-permute-start(bf16[64,8192]{1,0:T(8,128)(2,1)} %get-tuple-element.184), channel_id=1, source_target_pairs={{0,1},{1,0},{2,3},{3,2},{4,5},{5,4},{6,7},{7,6},{8,9},{9,8},{10,11... | collective-permute-start | bytes 3145736 | tf_op jit(solution)/shard_map/ppermute | solution.py:694
  111.1 9.3 %collective-permute-start.32 = (bf16[16,8192]{1,0:T(8,128)(2,1)S(1)}, bf16[16,8192]{1,0:T(8,128)(2,1)S(1)}, u32[]{:S(2)}, u32[]{:S(2)}) collective-permute-start(bf16[16,8192]{1,0:T(8,128)(2,1)S(1)} %fusion.1), channel_id=1, source_target_pairs={{0,4},{1,5},{2,6},{3,7},{4,8},{5,9},{6,10},{7,11},{8,12},{9,13},{1... | collective-permute-start | bytes 786440 | tf_op jit(solution)/shard_map/ppermute | solution.py:694
  111.2 9.2 %collective-permute-start.31 = (bf16[16,8192]{1,0:T(8,128)(2,1)S(1)}, bf16[16,8192]{1,0:T(8,128)(2,1)S(1)}, u32[]{:S(2)}, u32[]{:S(2)}) collective-permute-start(bf16[16,8192]{1,0:T(8,128)(2,1)S(1)} %slice.107), channel_id=1, source_target_pairs={{0,2},{1,3},{2,0},{3,1},{4,6},{5,7},{6,4},{7,5},{8,10},{9,11},{10,... | collective-permute-start | bytes 786440 | tf_op jit(solution)/shard_map/ppermute | solution.py:694
  120.7 14.2 %collective-permute-start.34 = (bf16[32,8192]{1,0:T(8,128)(2,1)S(1)}, bf16[32,8192]{1,0:T(8,128)(2,1)S(1)}, u32[]{:S(2)}, u32[]{:S(2)}) collective-permute-start(bf16[32,8192]{1,0:T(8,128)(2,1)S(1)} %fusion), channel_id=1, source_target_pairs={{0,4},{1,5},{2,6},{3,7},{4,8},{5,9},{6,10},{7,11},{8,12},{9,13},{1... | collective-permute-start | bytes 1572872 | tf_op jit(solution)/shard_map/ppermute | solution.py:694
  121.1 14.9 %collective-permute-start.33 = (bf16[32,8192]{1,0:T(8,128)(2,1)S(1)}, bf16[32,8192]{1,0:T(8,128)(2,1)S(1)}, u32[]{:S(2)}, u32[]{:S(2)}) collective-permute-start(bf16[32,8192]{1,0:T(8,128)(2,1)S(1)} %pad_maximum_fusion.2), channel_id=1, source_target_pairs={{0,2},{1,3},{2,0},{3,1},{4,6},{5,7},{6,4},{7,5},{8,10},{9,11},{10,... | collective-permute-start | bytes 1572872 | tf_op jit(solution)/shard_map/ppermute | solution.py:694
  121.6 25.6 %collective-permute-start.28 = (bf16[32,8192]{1,0:T(8,128)(2,1)S(1)}, bf16[32,8192]{1,0:T(8,128)(2,1)S(1)}, u32[]{:S(2)}, u32[]{:S(2)}) collective-permute-start(bf16[32,8192]{1,0:T(8,128)(2,1)S(1)} %multiply_convert_fusion), channel_id=1, source_target_pairs={{0,2},{1,3},{2,0},{3,1},{4,6},{5,7},{6,4},{7,5},{8,10},{9,11},{10,... | collective-permute-start | bytes 1572872 | tf_op jit(solution)/shard_map/ppermute | solution.py:694
  136.3 11.9 %collective-permute-start.35 = (bf16[32,8192]{1,0:T(8,128)(2,1)S(1)}, bf16[32,8192]{1,0:T(8,128)(2,1)S(1)}, u32[]{:S(2)}, u32[]{:S(2)}) collective-permute-start(bf16[32,8192]{1,0:T(8,128)(2,1)S(1)} %add_convert_fusion.2), channel_id=1, source_target_pairs={{0,4},{1,5},{2,6},{3,7},{4,8},{5,9},{6,10},{7,11},{8,12},{9,13},{1... | collective-permute-start | bytes 1572872 | tf_op jit(solution)/shard_map/ppermute | solution.py:694
  136.6 19.1 %collective-permute-start.26 = (bf16[32,8192]{1,0:T(8,128)(2,1)S(1)}, bf16[32,8192]{1,0:T(8,128)(2,1)S(1)}, u32[]{:S(2)}, u32[]{:S(2)}) collective-permute-start(bf16[32,8192]{1,0:T(8,128)(2,1)S(1)} %multiply_convert_fusion.1), channel_id=1, source_target_pairs={{0,2},{1,3},{2,0},{3,1},{4,6},{5,7},{6,4},{7,5},{8,10},{9,11},{10,... | collective-permute-start | bytes 1572872 | tf_op jit(solution)/shard_map/ppermute | solution.py:694
  148.6 11.0 %collective-permute-start.36 = (bf16[32,8192]{1,0:T(8,128)(2,1)S(1)}, bf16[32,8192]{1,0:T(8,128)(2,1)S(1)}, u32[]{:S(2)}, u32[]{:S(2)}) collective-permute-start(bf16[32,8192]{1,0:T(8,128)(2,1)S(1)} %add_convert_fusion.1), channel_id=1, source_target_pairs={{0,4},{1,5},{2,6},{3,7},{4,8},{5,9},{6,10},{7,11},{8,12},{9,13},{1... | collective-permute-start | bytes 1572872 | tf_op jit(solution)/shard_map/ppermute | solution.py:694
  (32 other events, 411.2 us)

commit v5 on v4

--- a/solution.py
+++ b/solution.py
@@ -272,7 +272,7 @@
 
 
 def norm_plane(spots, blocks, gain, small, late, weights):
-    rows, width = blocks[0][0].shape[0] * PLANE, gain.shape[1]
+    rows, width = sum(part.shape[0] for part in blocks[0]) * PLANE, gain.shape[1]
     flat = [near(part) for block in blocks for part in block]
     return pl.pallas_call(
         functools.partial(
@@ -700,11 +700,15 @@
     gain_row = pre_gain[None, :]
     spots = jnp.stack([z_pos, spot]).astype(jnp.int32)
 
-    own = jnp.concatenate(
-        [hidden, jnp.broadcast_to(destination.astype(jnp.bfloat16), (rows, 128))], axis=1
-    )
     half = rows // 2
-    straight, crossed = [[own]], []
+    own = [
+        jnp.concatenate(
+            [hidden[at : at + half], jnp.broadcast_to(destination[at : at + half].astype(jnp.bfloat16), (half, 128))],
+            axis=1,
+        )
+        for at in (0, half)
+    ]
+    straight, crossed = [own], []
     straight_core, crossed_core = [], []
     results = []
     picked = None
@@ -743,14 +747,6 @@
 
     for step in range(planes):
         last = step + 1 == planes
-        group = [over(straight[step], over_core)]
-        if last:
-            group.append(
-                [permute(straight[step][0][:half], over_y), permute(crossed[step - 1][0][half:], ring)]
-            )
-        else:
-            group.append(over(straight[step], over_y))
-            group.append(over(straight[step], ring))
         if step:
             crossed_core.append(over(crossed[step - 1], over_core))
         extra = {}
@@ -766,11 +762,22 @@
             extra["first"] = project_planes([results[0][0], extra["result"][0]], in_x, in_z)
         if step >= 2:
             extra["peer"] = permute(results[step - 2][1], over_core)
-        group, extra, picked = lax.optimization_barrier((group, extra, picked))
-        straight_core.append(group[0])
-        crossed.append(group[1])
+        moved = []
+        for index, piece in enumerate(straight[step]):
+            if last:
+                group = [permute(crossed[step - 1][1], ring) if index else permute(piece, over_y)]
+            else:
+                group = [permute(piece, over_y), permute(piece, ring)]
+            group.append(permute(piece, over_core))
+            if index:
+                group, extra, picked = lax.optimization_barrier((group, extra, picked))
+            else:
+                group = lax.optimization_barrier(group)
+            moved.append(group)
+        straight_core.append([group[-1] for group in moved])
+        crossed.append([group[0] for group in moved])
         if not last:
-            straight.append(group[2])
+            straight.append([group[1] for group in moved])
         if step:
             result = extra["result"]
             results.append(result[:3])

time: 180 us -> 176 us (0.978)
  waiting for transfers between devices: 83.5 us -> 66.2 us
  starting transfers between devices: 17.6 us -> 29.1 us
  local copies, waits for them, and re-layouts: 1.89 us -> 5.75 us
    ppermute x37 -> x50, waiting for transfers between devices: 83.5 us -> 66.2 us  [permute(): return lax.ppermute(value, 'tensor', pairs)]
    ppermute x37 -> x50, starting transfers between devices: 17.6 us -> 29.1 us  [permute(): return lax.ppermute(value, 'tensor', pairs)]
    unnamed x38 -> x48, local copies, waits for them, and re-layouts: 0.08 us -> 2.71 us
  transfers between devices with their start and end apart: 37 -> 50, of which waited for: 23 -> 19; matrix products, arithmetic and copies ran while one was open for 4% -> 4% of each run, Pallas kernels for 19% -> 19%
where the time goes in v5:
time: 176 us; the launch traced here: 175 us
  waiting for transfers between devices  66.2 us (38%)
  Pallas kernels  47.4 us (27%)
  starting transfers between devices  29.1 us (17%)
  blocking collectives  17.1 us (10%)
  other arithmetic  7.93 us (5%)
  local copies, waits for them, and re-layouts  5.75 us (3%)
    ppermute x50, waiting for transfers between devices, permute(): return lax.ppermute(value, 'tensor', pairs)  66.2 us
    ppermute x50, starting transfers between devices, permute(): return lax.ppermute(value, 'tensor', pairs)  29.1 us
    all_to_all x1, blocking collectives, on_device_planes(): lax.all_to_all(filled.reshape(count, CAP, width), 'tensor', split_axis=0,...  17.1 us
    pallas_call x4, Pallas kernels, norm_plane(): pl.pallas_call(functools.partial(norm_kernel, pieces=tuple((len(block) fo...  16.9 us
    pallas_call x2, Pallas kernels, project_planes(): pl.pallas_call(functools.partial(project_kernel, planes=count), out_shape...  9.31 us
    pallas_call x1, Pallas kernels, out_part(): pl.pallas_call(functools.partial(out_kernel, planes=planes, steps=steps),...  7.57 us
    pallas_call x1, Pallas kernels, scan_all(): pl.pallas_call(functools.partial(scan_kernel, heads=heads, planes=planes)...  6.46 us
    pallas_call x4, Pallas kernels, pick_plane(): pl.pallas_call(functools.partial(pick_kernel, pieces=tuple((len(block) fo...  6.32 us
  transfers between devices with their start and end apart: 50, of which 19 were waited for; matrix products, arithmetic and copies ran while one was open for 4% of the time, Pallas kernels for 19%

profile of v5, /device:TPU:0, one launch (start us, length us, event | category | flops | bytes accessed | tf_op | source)
XLA Modules:
  0.0 175.1 jit_solution(8026705924175575476)
XLA Ops:
  2.7 3.0 %collective-permute-start = (bf16[16,8320]{1,0:T(8,128)(2,1)S(1)}, bf16[16,8320]{1,0:T(8,128)(2,1)S(1)}, u32[]{:S(2)}, u32[]{:S(2)}) collective-permute-start(bf16[16,8320]{1,0:T(8,128)(2,1)S(1)} %pad_maximum_fusion.2.refs_1_), channel_id=1, source_target_pairs={{0,2},{1,3},{2,0},{3,1},{4,6},{5,7},{6,4},{7,5},{8,10},{9,11},{10,... | collective-permute-start | bytes 798728 | tf_op jit(solution)/shard_map/ppermute | solution.py:694
  10.3 2.5 %collective-permute-done.refs_5_ = bf16[16,8320]{1,0:T(8,128)(2,1)S(1)} collective-permute-done((bf16[16,8320]{1,0:T(8,128)(2,1)S(1)}, bf16[16,8320]{1,0:T(8,128)(2,1)S(1)}, u32[]{:S(2)}, u32[]{:S(2)}) %collective-permute-start) | collective-permute-done | bytes 266272 | tf_op jit(solution)/shard_map/ppermute | solution.py:694
  19.2 2.0 %collective-permute-done.7.refs_0_ = bf16[16,8320]{1,0:T(8,128)(2,1)} collective-permute-done((bf16[16,8320]{1,0:T(8,128)(2,1)}, bf16[16,8320]{1,0:T(8,128)(2,1)}, u32[]{:S(2)}, u32[]{:S(2)}) %collective-permute-start.7) | collective-permute-done | bytes 266272 | tf_op jit(solution)/shard_map/ppermute | solution.py:694
  26.9 2.1 %pick_plane.4.refs_8_ = bf16[32,8192]{1,0:T(8,128)(2,1)S(1)} custom-call(s32[2]{0:T(128)S(1)} %pad_add_fusion.spot_ref.spots, bf16[16,8320]{1,0:T(8,128)(2,1)} %pad_maximum_fusion.3.refs_0_, bf16[16,8320]{1,0:T(8,128)(2,1)S(1)} %copy-done.1, bf16[16,8320]{1,0:T(8,128)(2,1)} %collective-permute-done.8.refs_2_, ...), custom_call_target="tpu_custom_call" | custom-call | flops 1073741824 | bytes 3145728 | tf_op jit(solution)/shard_map/pick_plane/pallas_call | solution.py:576
  29.1 3.8 %norm_plane.4 = (bf16[128,8192]{1,0:T(8,128)(2,1)S(1)}, bf16[128,64]{1,0:T(8,128)(2,1)S(1)}, f32[128,128]{1,0:T(8,128)S(1)}) custom-call(s32[2]{0:T(128)S(1)} %pad_add_fusion.spot_ref.spots, bf16[16,8320]{1,0:T(8,128)(2,1)} %pad_maximum_fusion.3.refs_0_, bf16[16,8320]{1,0:T(8,128)(2,1)S(1)} %copy-done.1, bf16[16,8320]{1,0:T(8,128)(2,1)} %collective-permute-done.8.refs_2_, ...), custom_call_target="tpu_custom_call" | custom-call | flops 2147483648 | bytes 6291456 | tf_op jit(solution)/shard_map/norm_plane/pallas_call | solution.py:277
  35.4 2.0 %collective-permute-start.12 = (bf16[16,8320]{1,0:T(8,128)(2,1)S(1)}, bf16[16,8320]{1,0:T(8,128)(2,1)S(1)}, u32[]{:S(2)}, u32[]{:S(2)}) collective-permute-start(bf16[16,8320]{1,0:T(8,128)(2,1)S(1)} %collective-permute-done.4.refs_1_), channel_id=1, source_target_pairs={{0,4},{1,5},{2,6},{3,7},{4,8},{5,9},{6,10},{7,11},{8,12},{9,13},{1... | collective-permute-start | bytes 798728 | tf_op jit(solution)/shard_map/ppermute | solution.py:694
  38.0 3.5 %norm_plane.5 = (bf16[128,8192]{1,0:T(8,128)(2,1)S(1)}, bf16[128,64]{1,0:T(8,128)(2,1)S(1)}, f32[128,128]{1,0:T(8,128)S(1)}) custom-call(s32[2]{0:T(128)S(1)} %pad_add_fusion.spot_ref.spots, bf16[16,8320]{1,0:T(8,128)(2,1)} %collective-permute-done.7.refs_0_, bf16[16,8320]{1,0:T(8,128)(2,1)} %collective-permute-done.1.refs_1_, ...), custom_call_target="tpu_custom_call" | custom-call | flops 2147483648 | bytes 6291456 | tf_op jit(solution)/shard_map/norm_plane/pallas_call | solution.py:277
  45.1 4.5 %project_planes.2 = (bf16[128,512]{1,0:T(8,128)(2,1)S(1)}, bf16[128,512]{1,0:T(8,128)(2,1)S(1)}, bf16[128,512]{1,0:T(8,128)(2,1)S(1)}, bf16[128,512]{1,0:T(8,128)(2,1)S(1)}) custom-call(bf16[128,8192]{1,0:T(8,128)(2,1)S(1)} %get-tuple-element.135.refs_0_, bf16[128,8192]{1,0:T(8,128)(2,1)S(1)} %get-tuple-element.141.refs_1_, bf16[512,8192]{1,0:T(8,128)(2,1)S(1)} %bitcast.22, ...), custom_call_target="tpu_custom_call" | custom-call | flops 4294967296 | bytes 4194304 | tf_op jit(solution)/shard_map/project_planes/pallas_call | solution.py:318
  50.2 3.3 %collective-permute-done.24.refs_0_ = bf16[16,8320]{1,0:T(8,128)(2,1)S(1)} collective-permute-done((bf16[16,8320]{1,0:T(8,128)(2,1)S(1)}, bf16[16,8320]{1,0:T(8,128)(2,1)S(1)}, u32[]{:S(2)}, u32[]{:S(2)}) %collective-permute-start.24) | collective-permute-done | bytes 266272 | tf_op jit(solution)/shard_map/ppermute | solution.py:694
  56.0 4.8 %norm_plane.6 = (bf16[128,8192]{1,0:T(8,128)(2,1)S(1)}, bf16[128,64]{1,0:T(8,128)(2,1)S(1)}, f32[128,128]{1,0:T(8,128)S(1)}, bf16[512,8192]{1,0:T(8,128)(2,1)S(1)}) custom-call(s32[2]{0:T(128)S(1)} %pad_add_fusion.spot_ref.spots, bf16[16,8320]{1,0:T(8,128)(2,1)S(1)} %collective-permute-done.15.refs_0_, bf16[16,8320]{1,0:T(8,128)(2,1)S(1)} %collective-permute-done.4.refs_1_, ...), custom_call_target="tpu_custom_call" | custom-call | flops 2147483648 | bytes 6291456 | tf_op jit(solution)/shard_map/norm_plane/pallas_call | solution.py:277
  62.0 2.1 %collective-permute-done.20.refs_5_ = bf16[16,8320]{1,0:T(8,128)(2,1)S(1)} collective-permute-done((bf16[16,8320]{1,0:T(8,128)(2,1)S(1)}, bf16[16,8320]{1,0:T(8,128)(2,1)S(1)}, u32[]{:S(2)}, u32[]{:S(2)}) %collective-permute-start.20) | collective-permute-done | bytes 266272 | tf_op jit(solution)/shard_map/ppermute | solution.py:694
  66.0 4.8 %norm_plane.7 = (bf16[128,8192]{1,0:T(8,128)(2,1)S(1)}, bf16[128,64]{1,0:T(8,128)(2,1)S(1)}, f32[128,128]{1,0:T(8,128)S(1)}, bf16[512,8192]{1,0:T(8,128)(2,1)S(1)}) custom-call(s32[2]{0:T(128)S(1)} %pad_add_fusion.spot_ref.spots, bf16[16,8320]{1,0:T(8,128)(2,1)S(1)} %collective-permute-done.24.refs_0_, bf16[16,8320]{1,0:T(8,128)(2,1)S(1)} %collective-permute-done.12.refs_1_, ...), custom_call_target="tpu_custom_call" | custom-call | flops 2147483648 | bytes 6291456 | tf_op jit(solution)/shard_map/norm_plane/pallas_call | solution.py:277
  73.6 3.1 %collective-permute-start.35 = (bf16[512,128]{1,0:T(8,128)(2,1)S(1)}, bf16[512,128]{1,0:T(8,128)(2,1)S(1)}, u32[]{:S(2)}, u32[]{:S(2)}) collective-permute-start(bf16[512,128]{1,0:T(8,128)(2,1)S(1)} %pair_pieces.1), channel_id=1, source_target_pairs={{0,2},{1,3},{2,6},{3,7},{4,10},{5,11},{6,14},{7,15},{8,0},{9,1},{1... | collective-permute-start | bytes 393224 | tf_op jit(solution)/shard_map/ppermute | solution.py:694
  76.6 4.8 %project_planes.3 = (bf16[128,512]{1,0:T(8,128)(2,1)S(1)}, bf16[128,512]{1,0:T(8,128)(2,1)S(1)}, bf16[128,512]{1,0:T(8,128)(2,1)S(1)}, bf16[128,512]{1,0:T(8,128)(2,1)S(1)}) custom-call(bf16[128,8192]{1,0:T(8,128)(2,1)S(1)} %get-tuple-element.175.refs_0_, bf16[128,8192]{1,0:T(8,128)(2,1)S(1)} %get-tuple-element.176.refs_1_, ...), custom_call_target="tpu_custom_call" | custom-call | flops 4294967296 | bytes 4194304 | tf_op jit(solution)/shard_map/project_planes/pallas_call | solution.py:318
  81.4 4.1 %collective-permute-done.35.refs_13_ = bf16[512,128]{1,0:T(8,128)(2,1)S(1)} collective-permute-done((bf16[512,128]{1,0:T(8,128)(2,1)S(1)}, bf16[512,128]{1,0:T(8,128)(2,1)S(1)}, u32[]{:S(2)}, u32[]{:S(2)}) %collective-permute-start.35) | collective-permute-done | bytes 131104 | tf_op jit(solution)/shard_map/ppermute | solution.py:694
  85.5 6.5 %scan_all.1 = (bf16[512,512]{1,0:T(8,128)(2,1)S(1)}, f32[8,128]{1,0:T(8,128)S(1)}, bf16[512,8192]{1,0:T(8,128)(2,1)S(1)}) custom-call(s32[2]{0:T(128)S(1)} %pad_add_fusion.spot_ref.spots, bf16[128,512]{1,0:T(8,128)(2,1)S(1)} %get-tuple-element.150.refs_0_, bf16[128,512]{1,0:T(8,128)(2,1)S(1)} %get-tuple-element.151.refs_1_, ...), custom_call_target="tpu_custom_call" | custom-call | flops 1073741824 | bytes 8388608 | tf_op jit(solution)/shard_map/scan_all/pallas_call | solution.py:480
  92.0 7.6 %out_part.1 = (bf16[64,8192]{1,0:T(8,128)(2,1)}, bf16[32,8192]{1,0:T(8,128)(2,1)}, bf16[32,8192]{1,0:T(8,128)(2,1)}, bf16[64,8192]{1,0:T(8,128)(2,1)}, bf16[32,8...) custom-call(s32[2]{0:T(128)S(1)} %pad_add_fusion.spot_ref.spots, ...), custom_call_target="tpu_custom_call" | custom-call | flops 4294967296 | bytes 8388608 | tf_op jit(solution)/shard_map/out_part/pallas_call | solution.py:531
  102.8 2.7 %collective-permute-done.38 = f32[8,128]{1,0:T(8,128)S(1)} collective-permute-done((f32[8,128]{1,0:T(8,128)S(1)}, f32[8,128]{1,0:T(8,128)S(1)}, u32[]{:S(2)}, u32[]{:S(2)}) %collective-permute-start.38) | collective-permute-done | bytes 4128 | tf_op jit(solution)/shard_map/ppermute | solution.py:694
  107.7 8.8 %collective-permute-done.45 = bf16[16,8192]{1,0:T(8,128)(2,1)S(1)} collective-permute-done((bf16[16,8192]{1,0:T(8,128)(2,1)S(1)}, bf16[16,8192]{1,0:T(8,128)(2,1)S(1)}, u32[]{:S(2)}, u32[]{:S(2)}) %collective-permute-start.45) | collective-permute-done | bytes 262176 | tf_op jit(solution)/shard_map/ppermute | solution.py:694
  119.5 11.4 %collective-permute-done.47 = bf16[32,8192]{1,0:T(8,128)(2,1)S(1)} collective-permute-done((bf16[32,8192]{1,0:T(8,128)(2,1)S(1)}, bf16[32,8192]{1,0:T(8,128)(2,1)S(1)}, u32[]{:S(2)}, u32[]{:S(2)}) %collective-permute-start.47) | collective-permute-done | bytes 524320 | tf_op jit(solution)/shard_map/ppermute | solution.py:694
  133.7 9.6 %collective-permute-done.41 = bf16[32,8192]{1,0:T(8,128)(2,1)S(1)} collective-permute-done((bf16[32,8192]{1,0:T(8,128)(2,1)S(1)}, bf16[32,8192]{1,0:T(8,128)(2,1)S(1)}, u32[]{:S(2)}, u32[]{:S(2)}) %collective-permute-start.41) | collective-permute-done | bytes 524320 | tf_op jit(solution)/shard_map/ppermute | solution.py:694
  144.8 7.1 %collective-permute-done.39 = bf16[32,8192]{1,0:T(8,128)(2,1)S(1)} collective-permute-done((bf16[32,8192]{1,0:T(8,128)(2,1)S(1)}, bf16[32,8192]{1,0:T(8,128)(2,1)S(1)}, u32[]{:S(2)}, u32[]{:S(2)}) %collective-permute-start.39) | collective-permute-done | bytes 524320 | tf_op jit(solution)/shard_map/ppermute | solution.py:694
  151.9 3.9 %collective-permute-done.49 = bf16[32,8192]{1,0:T(8,128)(2,1)S(1)} collective-permute-done((bf16[32,8192]{1,0:T(8,128)(2,1)S(1)}, bf16[32,8192]{1,0:T(8,128)(2,1)S(1)}, u32[]{:S(2)}, u32[]{:S(2)}) %collective-permute-start.49) | collective-permute-done | bytes 524320 | tf_op jit(solution)/shard_map/ppermute | solution.py:694
  156.8 17.1 %all_to_all.5 = bf16[16,2,8192]{2,1,0:T(2,128)(2,1)S(1)} all-to-all(bf16[16,2,8192]{2,1,0:T(2,128)(2,1)S(1)} %reshape.43), channel_id=1, replica_groups=mesh['rep'=2,'dp'=1,'tensor'=16] {'tensor'}, dimensions={0} | all-to-all | bytes 1048576 | tf_op jit(solution)/shard_map/all_to_all | solution.py:849
  (189 shorter events, 48.6 us)
Async XLA Ops:
  2.7 10.1 %collective-permute-start = (bf16[16,8320]{1,0:T(8,128)(2,1)S(1)}, bf16[16,8320]{1,0:T(8,128)(2,1)S(1)}, u32[]{:S(2)}, u32[]{:S(2)}) collective-permute-start(bf16[16,8320]{1,0:T(8,128)(2,1)S(1)} %pad_maximum_fusion.2.refs_1_), channel_id=1, source_target_pairs={{0,2},{1,3},{2,0},{3,1},{4,6},{5,7},{6,4},{7,5},{8,10},{9,11},{10,... | collective-permute-start | bytes 798728 | tf_op jit(solution)/shard_map/ppermute | solution.py:694
  5.7 11.2 %collective-permute-start.1 = (bf16[16,8320]{1,0:T(8,128)(2,1)S(1)}, bf16[16,8320]{1,0:T(8,128)(2,1)}, u32[]{:S(2)}, u32[]{:S(2)}) collective-permute-start(bf16[16,8320]{1,0:T(8,128)(2,1)S(1)} %pad_maximum_fusion.2.refs_1_), channel_id=1, source_target_pairs={{0,4},{1,5},{2,6},{3,7},{4,8},{5,9},{6,10},{7,11},{8,12},{9,13},{1... | collective-permute-start | bytes 798728 | tf_op jit(solution)/shard_map/ppermute | solution.py:694
  8.1 11.1 %collective-permute-start.6 = (bf16[16,8320]{1,0:T(8,128)(2,1)}, bf16[16,8320]{1,0:T(8,128)(2,1)}, u32[]{:S(2)}, u32[]{:S(2)}) collective-permute-start(bf16[16,8320]{1,0:T(8,128)(2,1)} %pad_maximum_fusion.3.refs_0_), channel_id=1, source_target_pairs={{0,2},{1,3},{2,0},{3,1},{4,6},{5,7},{6,4},{7,5},{8,10},{9,11},{10,... | collective-permute-start | bytes 798728 | tf_op jit(solution)/shard_map/ppermute | solution.py:694
  8.6 12.6 %collective-permute-start.7 = (bf16[16,8320]{1,0:T(8,128)(2,1)}, bf16[16,8320]{1,0:T(8,128)(2,1)}, u32[]{:S(2)}, u32[]{:S(2)}) collective-permute-start(bf16[16,8320]{1,0:T(8,128)(2,1)} %pad_maximum_fusion.3.refs_0_), channel_id=1, source_target_pairs={{0,4},{1,5},{2,6},{3,7},{4,8},{5,9},{6,10},{7,11},{8,12},{9,13},{1... | collective-permute-start | bytes 798728 | tf_op jit(solution)/shard_map/ppermute | solution.py:694
  17.6 15.3 %collective-permute-start.4 = (bf16[16,8320]{1,0:T(8,128)(2,1)}, bf16[16,8320]{1,0:T(8,128)(2,1)S(1)}, u32[]{:S(2)}, u32[]{:S(2)}) collective-permute-start(bf16[16,8320]{1,0:T(8,128)(2,1)} %collective-permute-done.1.refs_1_), channel_id=1, source_target_pairs={{0,4},{1,5},{2,6},{3,7},{4,8},{5,9},{6,10},{7,11},{8,12},{9,13},{1... | collective-permute-start | bytes 798728 | tf_op jit(solution)/shard_map/ppermute | solution.py:694
  19.2 13.7 %collective-permute-start.5 = (bf16[16,8320]{1,0:T(8,128)(2,1)}, bf16[16,8320]{1,0:T(8,128)(2,1)}, u32[]{:S(2)}, u32[]{:S(2)}) collective-permute-start(bf16[16,8320]{1,0:T(8,128)(2,1)} %collective-permute-done.1.refs_1_), channel_id=1, source_target_pairs={{0,1},{1,0},{2,3},{3,2},{4,5},{5,4},{6,7},{7,6},{8,9},{9,8},{10,11... | collective-permute-start | bytes 798728 | tf_op jit(solution)/shard_map/ppermute | solution.py:694
  23.3 10.2 %collective-permute-start.14 = (bf16[16,8320]{1,0:T(8,128)(2,1)}, bf16[16,8320]{1,0:T(8,128)(2,1)S(1)}, u32[]{:S(2)}, u32[]{:S(2)}) collective-permute-start(bf16[16,8320]{1,0:T(8,128)(2,1)} %collective-permute-done.7.refs_0_), channel_id=1, source_target_pairs={{0,2},{1,3},{2,0},{3,1},{4,6},{5,7},{6,4},{7,5},{8,10},{9,11},{10,... | collective-permute-start | bytes 798728 | tf_op jit(solution)/shard_map/ppermute | solution.py:694
  23.9 10.1 %collective-permute-start.15 = (bf16[16,8320]{1,0:T(8,128)(2,1)}, bf16[16,8320]{1,0:T(8,128)(2,1)S(1)}, u32[]{:S(2)}, u32[]{:S(2)}) collective-permute-start(bf16[16,8320]{1,0:T(8,128)(2,1)} %collective-permute-done.7.refs_0_), channel_id=1, source_target_pairs={{0,4},{1,5},{2,6},{3,7},{4,8},{5,9},{6,10},{7,11},{8,12},{9,13},{1... | collective-permute-start | bytes 798728 | tf_op jit(solution)/shard_map/ppermute | solution.py:694
  34.0 11.1 %collective-permute-start.11 = (bf16[16,8320]{1,0:T(8,128)(2,1)S(1)}, bf16[16,8320]{1,0:T(8,128)(2,1)S(1)}, u32[]{:S(2)}, u32[]{:S(2)}) collective-permute-start(bf16[16,8320]{1,0:T(8,128)(2,1)S(1)} %collective-permute-done.4.refs_1_), channel_id=1, source_target_pairs={{0,2},{1,3},{2,0},{3,1},{4,6},{5,7},{6,4},{7,5},{8,10},{9,11},{10,... | collective-permute-start | bytes 798728 | tf_op jit(solution)/shard_map/ppermute | solution.py:694
  35.4 14.2 %collective-permute-start.12 = (bf16[16,8320]{1,0:T(8,128)(2,1)S(1)}, bf16[16,8320]{1,0:T(8,128)(2,1)S(1)}, u32[]{:S(2)}, u32[]{:S(2)}) collective-permute-start(bf16[16,8320]{1,0:T(8,128)(2,1)S(1)} %collective-permute-done.4.refs_1_), channel_id=1, source_target_pairs={{0,4},{1,5},{2,6},{3,7},{4,8},{5,9},{6,10},{7,11},{8,12},{9,13},{1... | collective-permute-start | bytes 798728 | tf_op jit(solution)/shard_map/ppermute | solution.py:694
  37.4 12.3 %collective-permute-start.13 = (bf16[16,8320]{1,0:T(8,128)(2,1)S(1)}, bf16[16,8320]{1,0:T(8,128)(2,1)S(1)}, u32[]{:S(2)}, u32[]{:S(2)}) collective-permute-start(bf16[16,8320]{1,0:T(8,128)(2,1)S(1)} %collective-permute-done.4.refs_1_), channel_id=1, source_target_pairs={{0,1},{1,0},{2,3},{3,2},{4,5},{5,4},{6,7},{7,6},{8,9},{9,8},{10,11... | collective-permute-start | bytes 798728 | tf_op jit(solution)/shard_map/ppermute | solution.py:694
  37.9 12.3 %collective-permute-start.23 = (bf16[16,8320]{1,0:T(8,128)(2,1)S(1)}, bf16[16,8320]{1,0:T(8,128)(2,1)S(1)}, u32[]{:S(2)}, u32[]{:S(2)}) collective-permute-start(bf16[16,8320]{1,0:T(8,128)(2,1)S(1)} %collective-permute-done.15.refs_0_), channel_id=1, source_target_pairs={{0,2},{1,3},{2,0},{3,1},{4,6},{5,7},{6,4},{7,5},{8,10},{9,11},{10,... | collective-permute-start | bytes 798728 | tf_op jit(solution)/shard_map/ppermute | solution.py:694
  43.4 10.1 %collective-permute-start.24 = (bf16[16,8320]{1,0:T(8,128)(2,1)S(1)}, bf16[16,8320]{1,0:T(8,128)(2,1)S(1)}, u32[]{:S(2)}, u32[]{:S(2)}) collective-permute-start(bf16[16,8320]{1,0:T(8,128)(2,1)S(1)} %collective-permute-done.15.refs_0_), channel_id=1, source_target_pairs={{0,4},{1,5},{2,6},{3,7},{4,8},{5,9},{6,10},{7,11},{8,12},{9,13},{1... | collective-permute-start | bytes 798728 | tf_op jit(solution)/shard_map/ppermute | solution.py:694
  53.5 10.6 %collective-permute-start.20 = (bf16[16,8320]{1,0:T(8,128)(2,1)S(1)}, bf16[16,8320]{1,0:T(8,128)(2,1)S(1)}, u32[]{:S(2)}, u32[]{:S(2)}) collective-permute-start(bf16[16,8320]{1,0:T(8,128)(2,1)S(1)} %collective-permute-done.11.refs_5_), channel_id=1, source_target_pairs={{0,4},{1,5},{2,6},{3,7},{4,8},{5,9},{6,10},{7,11},{8,12},{9,13},{1... | collective-permute-start | bytes 798728 | tf_op jit(solution)/shard_map/ppermute | solution.py:694
  53.5 10.6 %collective-permute-start.28 = (bf16[16,8320]{1,0:T(8,128)(2,1)S(1)}, bf16[16,8320]{1,0:T(8,128)(2,1)S(1)}, u32[]{:S(2)}, u32[]{:S(2)}) collective-permute-start(bf16[16,8320]{1,0:T(8,128)(2,1)S(1)} %collective-permute-done.24.refs_0_), channel_id=1, source_target_pairs={{0,2},{1,3},{2,0},{3,1},{4,6},{5,7},{6,4},{7,5},{8,10},{9,11},{10,... | collective-permute-start | bytes 798728 | tf_op jit(solution)/shard_map/ppermute | solution.py:694
  73.6 11.9 %collective-permute-start.35 = (bf16[512,128]{1,0:T(8,128)(2,1)S(1)}, bf16[512,128]{1,0:T(8,128)(2,1)S(1)}, u32[]{:S(2)}, u32[]{:S(2)}) collective-permute-start(bf16[512,128]{1,0:T(8,128)(2,1)S(1)} %pair_pieces.1), channel_id=1, source_target_pairs={{0,2},{1,3},{2,6},{3,7},{4,10},{5,11},{6,14},{7,15},{8,0},{9,1},{1... | collective-permute-start | bytes 393224 | tf_op jit(solution)/shard_map/ppermute | solution.py:694
  102.3 15.3 %collective-permute-start.40 = (bf16[64,8192]{1,0:T(8,128)(2,1)}, bf16[64,8192]{1,0:T(8,128)(2,1)S(1)}, u32[]{:S(2)}, u32[]{:S(2)}) collective-permute-start(bf16[64,8192]{1,0:T(8,128)(2,1)} %get-tuple-element.208), channel_id=1, source_target_pairs={{0,1},{1,0},{2,3},{3,2},{4,5},{5,4},{6,7},{7,6},{8,9},{9,8},{10,11... | collective-permute-start | bytes 3145736 | tf_op jit(solution)/shard_map/ppermute | solution.py:694
  102.4 30.1 %collective-permute-start.36 = (bf16[64,8192]{1,0:T(8,128)(2,1)}, bf16[64,8192]{1,0:T(8,128)(2,1)S(1)}, u32[]{:S(2)}, u32[]{:S(2)}) collective-permute-start(bf16[64,8192]{1,0:T(8,128)(2,1)} %get-tuple-element.204), channel_id=1, source_target_pairs={{0,1},{1,0},{2,3},{3,2},{4,5},{5,4},{6,7},{7,6},{8,9},{9,8},{10,11... | collective-permute-start | bytes 3145736 | tf_op jit(solution)/shard_map/ppermute | solution.py:694
  116.8 14.2 %collective-permute-start.47 = (bf16[32,8192]{1,0:T(8,128)(2,1)S(1)}, bf16[32,8192]{1,0:T(8,128)(2,1)S(1)}, u32[]{:S(2)}, u32[]{:S(2)}) collective-permute-start(bf16[32,8192]{1,0:T(8,128)(2,1)S(1)} %fusion), channel_id=1, source_target_pairs={{0,4},{1,5},{2,6},{3,7},{4,8},{5,9},{6,10},{7,11},{8,12},{9,13},{1... | collective-permute-start | bytes 1572872 | tf_op jit(solution)/shard_map/ppermute | solution.py:694
  117.2 14.9 %collective-permute-start.46 = (bf16[32,8192]{1,0:T(8,128)(2,1)S(1)}, bf16[32,8192]{1,0:T(8,128)(2,1)S(1)}, u32[]{:S(2)}, u32[]{:S(2)}) collective-permute-start(bf16[32,8192]{1,0:T(8,128)(2,1)S(1)} %pad_maximum_fusion.1), channel_id=1, source_target_pairs={{0,2},{1,3},{2,0},{3,1},{4,6},{5,7},{6,4},{7,5},{8,10},{9,11},{10,... | collective-permute-start | bytes 1572872 | tf_op jit(solution)/shard_map/ppermute | solution.py:694
  117.7 25.6 %collective-permute-start.41 = (bf16[32,8192]{1,0:T(8,128)(2,1)S(1)}, bf16[32,8192]{1,0:T(8,128)(2,1)S(1)}, u32[]{:S(2)}, u32[]{:S(2)}) collective-permute-start(bf16[32,8192]{1,0:T(8,128)(2,1)S(1)} %multiply_convert_fusion), channel_id=1, source_target_pairs={{0,2},{1,3},{2,0},{3,1},{4,6},{5,7},{6,4},{7,5},{8,10},{9,11},{10,... | collective-permute-start | bytes 1572872 | tf_op jit(solution)/shard_map/ppermute | solution.py:694
  132.5 11.9 %collective-permute-start.48 = (bf16[32,8192]{1,0:T(8,128)(2,1)S(1)}, bf16[32,8192]{1,0:T(8,128)(2,1)S(1)}, u32[]{:S(2)}, u32[]{:S(2)}) collective-permute-start(bf16[32,8192]{1,0:T(8,128)(2,1)S(1)} %add_convert_fusion.2), channel_id=1, source_target_pairs={{0,4},{1,5},{2,6},{3,7},{4,8},{5,9},{6,10},{7,11},{8,12},{9,13},{1... | collective-permute-start | bytes 1572872 | tf_op jit(solution)/shard_map/ppermute | solution.py:694
  132.7 19.1 %collective-permute-start.39 = (bf16[32,8192]{1,0:T(8,128)(2,1)S(1)}, bf16[32,8192]{1,0:T(8,128)(2,1)S(1)}, u32[]{:S(2)}, u32[]{:S(2)}) collective-permute-start(bf16[32,8192]{1,0:T(8,128)(2,1)S(1)} %multiply_convert_fusion.1), channel_id=1, source_target_pairs={{0,2},{1,3},{2,0},{3,1},{4,6},{5,7},{6,4},{7,5},{8,10},{9,11},{10,... | collective-permute-start | bytes 1572872 | tf_op jit(solution)/shard_map/ppermute | solution.py:694
  144.7 11.0 %collective-permute-start.49 = (bf16[32,8192]{1,0:T(8,128)(2,1)S(1)}, bf16[32,8192]{1,0:T(8,128)(2,1)S(1)}, u32[]{:S(2)}, u32[]{:S(2)}) collective-permute-start(bf16[32,8192]{1,0:T(8,128)(2,1)S(1)} %add_convert_fusion.1), channel_id=1, source_target_pairs={{0,4},{1,5},{2,6},{3,7},{4,8},{5,9},{6,10},{7,11},{8,12},{9,13},{1... | collective-permute-start | bytes 1572872 | tf_op jit(solution)/shard_map/ppermute | solution.py:694
  (50 other events, 536.3 us)

commit v6 on v5

--- a/solution.py
+++ b/solution.py
@@ -797,7 +797,7 @@
     normed, pieces, dts = zip(*results)
     peers += over(pieces[2:], over_core)
     both = pair_pieces(spots, pieces, peers)
-    both, normed = lax.optimization_barrier((both, normed[2:]))
+    both, normed, picked = lax.optimization_barrier((both, normed[2:], picked))
     far_pieces = send_far(both)
     second = project_planes(normed, near_x, near_z)
     far_pieces, picked = lax.optimization_barrier((far_pieces, pick(planes - 1, picked)))

time: 176 us -> 175 us (level)
  transfers between devices with their start and end apart: 50 -> 50, of which waited for: 19 -> 20; matrix products, arithmetic and copies ran while one was open for 4% -> 4% of each run, Pallas kernels for 19% -> 19%
where the time goes in v6:
time: 175 us
  waiting for transfers between devices  65.9 us (38%)
  Pallas kernels  47.2 us (27%)
  starting transfers between devices  29.3 us (17%)
  blocking collectives  17.1 us (10%)
  other arithmetic  7.93 us (5%)
  local copies, waits for them, and re-layouts  5.75 us (3%)
    ppermute x50, waiting for transfers between devices, permute(): return lax.ppermute(value, 'tensor', pairs)  65.9 us
    ppermute x50, starting transfers between devices, permute(): return lax.ppermute(value, 'tensor', pairs)  29.3 us
    all_to_all x1, blocking collectives, on_device_planes(): lax.all_to_all(filled.reshape(count, CAP, width), 'tensor', split_axis=0,...  17.1 us
    pallas_call x4, Pallas kernels, norm_plane(): pl.pallas_call(functools.partial(norm_kernel, pieces=tuple((len(block) fo...  16.9 us
    pallas_call x2, Pallas kernels, project_planes(): pl.pallas_call(functools.partial(project_kernel, planes=count), out_shape...  9.06 us
    pallas_call x1, Pallas kernels, out_part(): pl.pallas_call(functools.partial(out_kernel, planes=planes, steps=steps),...  7.55 us
    pallas_call x1, Pallas kernels, scan_all(): pl.pallas_call(functools.partial(scan_kernel, heads=heads, planes=planes)...  6.46 us
    pallas_call x4, Pallas kernels, pick_plane(): pl.pallas_call(functools.partial(pick_kernel, pieces=tuple((len(block) fo...  6.31 us
  transfers between devices with their start and end apart: 50, of which 20 were waited for; matrix products, arithmetic and copies ran while one was open for 4% of the time, Pallas kernels for 19%

profile of v6, /device:TPU:0, one launch (start us, length us, event | category | flops | bytes accessed | tf_op | source)
XLA Modules:
  0.0 174.8 jit_solution(10102474649894520208)
XLA Ops:
  2.7 3.0 %collective-permute-start = (bf16[16,8320]{1,0:T(8,128)(2,1)S(1)}, bf16[16,8320]{1,0:T(8,128)(2,1)S(1)}, u32[]{:S(2)}, u32[]{:S(2)}) collective-permute-start(bf16[16,8320]{1,0:T(8,128)(2,1)S(1)} %pad_maximum_fusion.2.refs_1_), channel_id=1, source_target_pairs={{0,2},{1,3},{2,0},{3,1},{4,6},{5,7},{6,4},{7,5},{8,10},{9,11},{10,... | collective-permute-start | bytes 798728 | tf_op jit(solution)/shard_map/ppermute | solution.py:694
  10.3 2.5 %collective-permute-done.refs_5_ = bf16[16,8320]{1,0:T(8,128)(2,1)S(1)} collective-permute-done((bf16[16,8320]{1,0:T(8,128)(2,1)S(1)}, bf16[16,8320]{1,0:T(8,128)(2,1)S(1)}, u32[]{:S(2)}, u32[]{:S(2)}) %collective-permute-start) | collective-permute-done | bytes 266272 | tf_op jit(solution)/shard_map/ppermute | solution.py:694
  19.2 2.0 %collective-permute-done.7.refs_0_ = bf16[16,8320]{1,0:T(8,128)(2,1)} collective-permute-done((bf16[16,8320]{1,0:T(8,128)(2,1)}, bf16[16,8320]{1,0:T(8,128)(2,1)}, u32[]{:S(2)}, u32[]{:S(2)}) %collective-permute-start.7) | collective-permute-done | bytes 266272 | tf_op jit(solution)/shard_map/ppermute | solution.py:694
  26.9 2.1 %pick_plane.4.refs_8_ = bf16[32,8192]{1,0:T(8,128)(2,1)S(1)} custom-call(s32[2]{0:T(128)S(1)} %pad_add_fusion.spot_ref.spots, bf16[16,8320]{1,0:T(8,128)(2,1)} %pad_maximum_fusion.3.refs_0_, bf16[16,8320]{1,0:T(8,128)(2,1)S(1)} %copy-done.1, bf16[16,8320]{1,0:T(8,128)(2,1)} %collective-permute-done.8.refs_2_, ...), custom_call_target="tpu_custom_call" | custom-call | flops 1073741824 | bytes 3145728 | tf_op jit(solution)/shard_map/pick_plane/pallas_call | solution.py:576
  29.1 3.8 %norm_plane.4 = (bf16[128,8192]{1,0:T(8,128)(2,1)S(1)}, bf16[128,64]{1,0:T(8,128)(2,1)S(1)}, f32[128,128]{1,0:T(8,128)S(1)}) custom-call(s32[2]{0:T(128)S(1)} %pad_add_fusion.spot_ref.spots, bf16[16,8320]{1,0:T(8,128)(2,1)} %pad_maximum_fusion.3.refs_0_, bf16[16,8320]{1,0:T(8,128)(2,1)S(1)} %copy-done.1, bf16[16,8320]{1,0:T(8,128)(2,1)} %collective-permute-done.8.refs_2_, ...), custom_call_target="tpu_custom_call" | custom-call | flops 2147483648 | bytes 6291456 | tf_op jit(solution)/shard_map/norm_plane/pallas_call | solution.py:277
  35.5 1.9 %collective-permute-start.12 = (bf16[16,8320]{1,0:T(8,128)(2,1)S(1)}, bf16[16,8320]{1,0:T(8,128)(2,1)S(1)}, u32[]{:S(2)}, u32[]{:S(2)}) collective-permute-start(bf16[16,8320]{1,0:T(8,128)(2,1)S(1)} %collective-permute-done.4.refs_1_), channel_id=1, source_target_pairs={{0,4},{1,5},{2,6},{3,7},{4,8},{5,9},{6,10},{7,11},{8,12},{9,13},{1... | collective-permute-start | bytes 798728 | tf_op jit(solution)/shard_map/ppermute | solution.py:694
  38.0 3.6 %norm_plane.5 = (bf16[128,8192]{1,0:T(8,128)(2,1)S(1)}, bf16[128,64]{1,0:T(8,128)(2,1)S(1)}, f32[128,128]{1,0:T(8,128)S(1)}) custom-call(s32[2]{0:T(128)S(1)} %pad_add_fusion.spot_ref.spots, bf16[16,8320]{1,0:T(8,128)(2,1)} %collective-permute-done.7.refs_0_, bf16[16,8320]{1,0:T(8,128)(2,1)} %collective-permute-done.1.refs_1_, ...), custom_call_target="tpu_custom_call" | custom-call | flops 2147483648 | bytes 6291456 | tf_op jit(solution)/shard_map/norm_plane/pallas_call | solution.py:277
  45.1 4.5 %project_planes.2 = (bf16[128,512]{1,0:T(8,128)(2,1)S(1)}, bf16[128,512]{1,0:T(8,128)(2,1)S(1)}, bf16[128,512]{1,0:T(8,128)(2,1)S(1)}, bf16[128,512]{1,0:T(8,128)(2,1)S(1)}) custom-call(bf16[128,8192]{1,0:T(8,128)(2,1)S(1)} %get-tuple-element.136.refs_0_, bf16[128,8192]{1,0:T(8,128)(2,1)S(1)} %get-tuple-element.142.refs_1_, bf16[512,8192]{1,0:T(8,128)(2,1)S(1)} %bitcast.22, ...), custom_call_target="tpu_custom_call" | custom-call | flops 4294967296 | bytes 4194304 | tf_op jit(solution)/shard_map/project_planes/pallas_call | solution.py:318
  50.2 3.3 %collective-permute-done.24.refs_0_ = bf16[16,8320]{1,0:T(8,128)(2,1)S(1)} collective-permute-done((bf16[16,8320]{1,0:T(8,128)(2,1)S(1)}, bf16[16,8320]{1,0:T(8,128)(2,1)S(1)}, u32[]{:S(2)}, u32[]{:S(2)}) %collective-permute-start.24) | collective-permute-done | bytes 266272 | tf_op jit(solution)/shard_map/ppermute | solution.py:694
  56.0 4.8 %norm_plane.6 = (bf16[128,8192]{1,0:T(8,128)(2,1)S(1)}, bf16[128,64]{1,0:T(8,128)(2,1)S(1)}, f32[128,128]{1,0:T(8,128)S(1)}, bf16[512,8192]{1,0:T(8,128)(2,1)S(1)}) custom-call(s32[2]{0:T(128)S(1)} %pad_add_fusion.spot_ref.spots, bf16[16,8320]{1,0:T(8,128)(2,1)S(1)} %collective-permute-done.15.refs_0_, bf16[16,8320]{1,0:T(8,128)(2,1)S(1)} %collective-permute-done.4.refs_1_, ...), custom_call_target="tpu_custom_call" | custom-call | flops 2147483648 | bytes 6291456 | tf_op jit(solution)/shard_map/norm_plane/pallas_call | solution.py:277
  62.0 2.2 %collective-permute-done.20.refs_5_ = bf16[16,8320]{1,0:T(8,128)(2,1)S(1)} collective-permute-done((bf16[16,8320]{1,0:T(8,128)(2,1)S(1)}, bf16[16,8320]{1,0:T(8,128)(2,1)S(1)}, u32[]{:S(2)}, u32[]{:S(2)}) %collective-permute-start.20) | collective-permute-done | bytes 266272 | tf_op jit(solution)/shard_map/ppermute | solution.py:694
  66.1 4.8 %norm_plane.7 = (bf16[128,8192]{1,0:T(8,128)(2,1)S(1)}, bf16[128,64]{1,0:T(8,128)(2,1)S(1)}, f32[128,128]{1,0:T(8,128)S(1)}, bf16[512,8192]{1,0:T(8,128)(2,1)S(1)}) custom-call(s32[2]{0:T(128)S(1)} %pad_add_fusion.spot_ref.spots, bf16[16,8320]{1,0:T(8,128)(2,1)S(1)} %collective-permute-done.24.refs_0_, bf16[16,8320]{1,0:T(8,128)(2,1)S(1)} %collective-permute-done.12.refs_1_, ...), custom_call_target="tpu_custom_call" | custom-call | flops 2147483648 | bytes 6291456 | tf_op jit(solution)/shard_map/norm_plane/pallas_call | solution.py:277
  73.5 3.0 %collective-permute-start.35 = (bf16[512,128]{1,0:T(8,128)(2,1)S(1)}, bf16[512,128]{1,0:T(8,128)(2,1)S(1)}, u32[]{:S(2)}, u32[]{:S(2)}) collective-permute-start(bf16[512,128]{1,0:T(8,128)(2,1)S(1)} %pair_pieces.1), channel_id=1, source_target_pairs={{0,2},{1,3},{2,6},{3,7},{4,10},{5,11},{6,14},{7,15},{8,0},{9,1},{1... | collective-permute-start | bytes 393224 | tf_op jit(solution)/shard_map/ppermute | solution.py:694
  76.5 4.5 %project_planes.3 = (bf16[128,512]{1,0:T(8,128)(2,1)S(1)}, bf16[128,512]{1,0:T(8,128)(2,1)S(1)}, bf16[128,512]{1,0:T(8,128)(2,1)S(1)}, bf16[128,512]{1,0:T(8,128)(2,1)S(1)}) custom-call(bf16[128,8192]{1,0:T(8,128)(2,1)S(1)} %get-tuple-element.177.refs_0_, bf16[128,8192]{1,0:T(8,128)(2,1)S(1)} %get-tuple-element.178.refs_1_, ...), custom_call_target="tpu_custom_call" | custom-call | flops 4294967296 | bytes 4194304 | tf_op jit(solution)/shard_map/project_planes/pallas_call | solution.py:318
  82.2 3.0 %collective-permute-done.35.refs_13_ = bf16[512,128]{1,0:T(8,128)(2,1)S(1)} collective-permute-done((bf16[512,128]{1,0:T(8,128)(2,1)S(1)}, bf16[512,128]{1,0:T(8,128)(2,1)S(1)}, u32[]{:S(2)}, u32[]{:S(2)}) %collective-permute-start.35) | collective-permute-done | bytes 131104 | tf_op jit(solution)/shard_map/ppermute | solution.py:694
  85.2 6.5 %scan_all.1 = (bf16[512,512]{1,0:T(8,128)(2,1)S(1)}, f32[8,128]{1,0:T(8,128)S(1)}, bf16[512,8192]{1,0:T(8,128)(2,1)S(1)}) custom-call(s32[2]{0:T(128)S(1)} %pad_add_fusion.spot_ref.spots, bf16[128,512]{1,0:T(8,128)(2,1)S(1)} %get-tuple-element.151.refs_0_, bf16[128,512]{1,0:T(8,128)(2,1)S(1)} %get-tuple-element.152.refs_1_, ...), custom_call_target="tpu_custom_call" | custom-call | flops 1073741824 | bytes 8388608 | tf_op jit(solution)/shard_map/scan_all/pallas_call | solution.py:480
  91.7 7.5 %out_part.1 = (bf16[64,8192]{1,0:T(8,128)(2,1)}, bf16[32,8192]{1,0:T(8,128)(2,1)}, bf16[32,8192]{1,0:T(8,128)(2,1)}, bf16[64,8192]{1,0:T(8,128)(2,1)}, bf16[32,8...) custom-call(s32[2]{0:T(128)S(1)} %pad_add_fusion.spot_ref.spots, ...), custom_call_target="tpu_custom_call" | custom-call | flops 4294967296 | bytes 8388608 | tf_op jit(solution)/shard_map/out_part/pallas_call | solution.py:531
  102.5 2.7 %collective-permute-done.38 = f32[8,128]{1,0:T(8,128)S(1)} collective-permute-done((f32[8,128]{1,0:T(8,128)S(1)}, f32[8,128]{1,0:T(8,128)S(1)}, u32[]{:S(2)}, u32[]{:S(2)}) %collective-permute-start.38) | collective-permute-done | bytes 4128 | tf_op jit(solution)/shard_map/ppermute | solution.py:694
  107.5 8.8 %collective-permute-done.45 = bf16[16,8192]{1,0:T(8,128)(2,1)S(1)} collective-permute-done((bf16[16,8192]{1,0:T(8,128)(2,1)S(1)}, bf16[16,8192]{1,0:T(8,128)(2,1)S(1)}, u32[]{:S(2)}, u32[]{:S(2)}) %collective-permute-start.45) | collective-permute-done | bytes 262176 | tf_op jit(solution)/shard_map/ppermute | solution.py:694
  119.2 11.4 %collective-permute-done.47 = bf16[32,8192]{1,0:T(8,128)(2,1)S(1)} collective-permute-done((bf16[32,8192]{1,0:T(8,128)(2,1)S(1)}, bf16[32,8192]{1,0:T(8,128)(2,1)S(1)}, u32[]{:S(2)}, u32[]{:S(2)}) %collective-permute-start.47) | collective-permute-done | bytes 524320 | tf_op jit(solution)/shard_map/ppermute | solution.py:694
  133.6 9.4 %collective-permute-done.41 = bf16[32,8192]{1,0:T(8,128)(2,1)S(1)} collective-permute-done((bf16[32,8192]{1,0:T(8,128)(2,1)S(1)}, bf16[32,8192]{1,0:T(8,128)(2,1)S(1)}, u32[]{:S(2)}, u32[]{:S(2)}) %collective-permute-start.41) | collective-permute-done | bytes 524320 | tf_op jit(solution)/shard_map/ppermute | solution.py:694
  144.4 7.1 %collective-permute-done.39 = bf16[32,8192]{1,0:T(8,128)(2,1)S(1)} collective-permute-done((bf16[32,8192]{1,0:T(8,128)(2,1)S(1)}, bf16[32,8192]{1,0:T(8,128)(2,1)S(1)}, u32[]{:S(2)}, u32[]{:S(2)}) %collective-permute-start.39) | collective-permute-done | bytes 524320 | tf_op jit(solution)/shard_map/ppermute | solution.py:694
  151.5 3.9 %collective-permute-done.49 = bf16[32,8192]{1,0:T(8,128)(2,1)S(1)} collective-permute-done((bf16[32,8192]{1,0:T(8,128)(2,1)S(1)}, bf16[32,8192]{1,0:T(8,128)(2,1)S(1)}, u32[]{:S(2)}, u32[]{:S(2)}) %collective-permute-start.49) | collective-permute-done | bytes 524320 | tf_op jit(solution)/shard_map/ppermute | solution.py:694
  156.4 17.1 %all_to_all.5 = bf16[16,2,8192]{2,1,0:T(2,128)(2,1)S(1)} all-to-all(bf16[16,2,8192]{2,1,0:T(2,128)(2,1)S(1)} %reshape.43), channel_id=1, replica_groups=mesh['rep'=2,'dp'=1,'tensor'=16] {'tensor'}, dimensions={0} | all-to-all | bytes 1048576 | tf_op jit(solution)/shard_map/all_to_all | solution.py:849
  (189 shorter events, 50.0 us)
Async XLA Ops:
  2.7 10.1 %collective-permute-start = (bf16[16,8320]{1,0:T(8,128)(2,1)S(1)}, bf16[16,8320]{1,0:T(8,128)(2,1)S(1)}, u32[]{:S(2)}, u32[]{:S(2)}) collective-permute-start(bf16[16,8320]{1,0:T(8,128)(2,1)S(1)} %pad_maximum_fusion.2.refs_1_), channel_id=1, source_target_pairs={{0,2},{1,3},{2,0},{3,1},{4,6},{5,7},{6,4},{7,5},{8,10},{9,11},{10,... | collective-permute-start | bytes 798728 | tf_op jit(solution)/shard_map/ppermute | solution.py:694
  5.7 11.2 %collective-permute-start.1 = (bf16[16,8320]{1,0:T(8,128)(2,1)S(1)}, bf16[16,8320]{1,0:T(8,128)(2,1)}, u32[]{:S(2)}, u32[]{:S(2)}) collective-permute-start(bf16[16,8320]{1,0:T(8,128)(2,1)S(1)} %pad_maximum_fusion.2.refs_1_), channel_id=1, source_target_pairs={{0,4},{1,5},{2,6},{3,7},{4,8},{5,9},{6,10},{7,11},{8,12},{9,13},{1... | collective-permute-start | bytes 798728 | tf_op jit(solution)/shard_map/ppermute | solution.py:694
  8.1 11.1 %collective-permute-start.6 = (bf16[16,8320]{1,0:T(8,128)(2,1)}, bf16[16,8320]{1,0:T(8,128)(2,1)}, u32[]{:S(2)}, u32[]{:S(2)}) collective-permute-start(bf16[16,8320]{1,0:T(8,128)(2,1)} %pad_maximum_fusion.3.refs_0_), channel_id=1, source_target_pairs={{0,2},{1,3},{2,0},{3,1},{4,6},{5,7},{6,4},{7,5},{8,10},{9,11},{10,... | collective-permute-start | bytes 798728 | tf_op jit(solution)/shard_map/ppermute | solution.py:694
  8.6 12.6 %collective-permute-start.7 = (bf16[16,8320]{1,0:T(8,128)(2,1)}, bf16[16,8320]{1,0:T(8,128)(2,1)}, u32[]{:S(2)}, u32[]{:S(2)}) collective-permute-start(bf16[16,8320]{1,0:T(8,128)(2,1)} %pad_maximum_fusion.3.refs_0_), channel_id=1, source_target_pairs={{0,4},{1,5},{2,6},{3,7},{4,8},{5,9},{6,10},{7,11},{8,12},{9,13},{1... | collective-permute-start | bytes 798728 | tf_op jit(solution)/shard_map/ppermute | solution.py:694
  17.6 15.2 %collective-permute-start.4 = (bf16[16,8320]{1,0:T(8,128)(2,1)}, bf16[16,8320]{1,0:T(8,128)(2,1)S(1)}, u32[]{:S(2)}, u32[]{:S(2)}) collective-permute-start(bf16[16,8320]{1,0:T(8,128)(2,1)} %collective-permute-done.1.refs_1_), channel_id=1, source_target_pairs={{0,4},{1,5},{2,6},{3,7},{4,8},{5,9},{6,10},{7,11},{8,12},{9,13},{1... | collective-permute-start | bytes 798728 | tf_op jit(solution)/shard_map/ppermute | solution.py:694
  19.2 13.7 %collective-permute-start.5 = (bf16[16,8320]{1,0:T(8,128)(2,1)}, bf16[16,8320]{1,0:T(8,128)(2,1)}, u32[]{:S(2)}, u32[]{:S(2)}) collective-permute-start(bf16[16,8320]{1,0:T(8,128)(2,1)} %collective-permute-done.1.refs_1_), channel_id=1, source_target_pairs={{0,1},{1,0},{2,3},{3,2},{4,5},{5,4},{6,7},{7,6},{8,9},{9,8},{10,11... | collective-permute-start | bytes 798728 | tf_op jit(solution)/shard_map/ppermute | solution.py:694
  23.3 10.2 %collective-permute-start.14 = (bf16[16,8320]{1,0:T(8,128)(2,1)}, bf16[16,8320]{1,0:T(8,128)(2,1)S(1)}, u32[]{:S(2)}, u32[]{:S(2)}) collective-permute-start(bf16[16,8320]{1,0:T(8,128)(2,1)} %collective-permute-done.7.refs_0_), channel_id=1, source_target_pairs={{0,2},{1,3},{2,0},{3,1},{4,6},{5,7},{6,4},{7,5},{8,10},{9,11},{10,... | collective-permute-start | bytes 798728 | tf_op jit(solution)/shard_map/ppermute | solution.py:694
  23.9 10.1 %collective-permute-start.15 = (bf16[16,8320]{1,0:T(8,128)(2,1)}, bf16[16,8320]{1,0:T(8,128)(2,1)S(1)}, u32[]{:S(2)}, u32[]{:S(2)}) collective-permute-start(bf16[16,8320]{1,0:T(8,128)(2,1)} %collective-permute-done.7.refs_0_), channel_id=1, source_target_pairs={{0,4},{1,5},{2,6},{3,7},{4,8},{5,9},{6,10},{7,11},{8,12},{9,13},{1... | collective-permute-start | bytes 798728 | tf_op jit(solution)/shard_map/ppermute | solution.py:694
  34.0 11.1 %collective-permute-start.11 = (bf16[16,8320]{1,0:T(8,128)(2,1)S(1)}, bf16[16,8320]{1,0:T(8,128)(2,1)S(1)}, u32[]{:S(2)}, u32[]{:S(2)}) collective-permute-start(bf16[16,8320]{1,0:T(8,128)(2,1)S(1)} %collective-permute-done.4.refs_1_), channel_id=1, source_target_pairs={{0,2},{1,3},{2,0},{3,1},{4,6},{5,7},{6,4},{7,5},{8,10},{9,11},{10,... | collective-permute-start | bytes 798728 | tf_op jit(solution)/shard_map/ppermute | solution.py:694
  35.5 14.2 %collective-permute-start.12 = (bf16[16,8320]{1,0:T(8,128)(2,1)S(1)}, bf16[16,8320]{1,0:T(8,128)(2,1)S(1)}, u32[]{:S(2)}, u32[]{:S(2)}) collective-permute-start(bf16[16,8320]{1,0:T(8,128)(2,1)S(1)} %collective-permute-done.4.refs_1_), channel_id=1, source_target_pairs={{0,4},{1,5},{2,6},{3,7},{4,8},{5,9},{6,10},{7,11},{8,12},{9,13},{1... | collective-permute-start | bytes 798728 | tf_op jit(solution)/shard_map/ppermute | solution.py:694
  37.4 12.3 %collective-permute-start.13 = (bf16[16,8320]{1,0:T(8,128)(2,1)S(1)}, bf16[16,8320]{1,0:T(8,128)(2,1)S(1)}, u32[]{:S(2)}, u32[]{:S(2)}) collective-permute-start(bf16[16,8320]{1,0:T(8,128)(2,1)S(1)} %collective-permute-done.4.refs_1_), channel_id=1, source_target_pairs={{0,1},{1,0},{2,3},{3,2},{4,5},{5,4},{6,7},{7,6},{8,9},{9,8},{10,11... | collective-permute-start | bytes 798728 | tf_op jit(solution)/shard_map/ppermute | solution.py:694
  37.9 12.3 %collective-permute-start.23 = (bf16[16,8320]{1,0:T(8,128)(2,1)S(1)}, bf16[16,8320]{1,0:T(8,128)(2,1)S(1)}, u32[]{:S(2)}, u32[]{:S(2)}) collective-permute-start(bf16[16,8320]{1,0:T(8,128)(2,1)S(1)} %collective-permute-done.15.refs_0_), channel_id=1, source_target_pairs={{0,2},{1,3},{2,0},{3,1},{4,6},{5,7},{6,4},{7,5},{8,10},{9,11},{10,... | collective-permute-start | bytes 798728 | tf_op jit(solution)/shard_map/ppermute | solution.py:694
  43.5 10.1 %collective-permute-start.24 = (bf16[16,8320]{1,0:T(8,128)(2,1)S(1)}, bf16[16,8320]{1,0:T(8,128)(2,1)S(1)}, u32[]{:S(2)}, u32[]{:S(2)}) collective-permute-start(bf16[16,8320]{1,0:T(8,128)(2,1)S(1)} %collective-permute-done.15.refs_0_), channel_id=1, source_target_pairs={{0,4},{1,5},{2,6},{3,7},{4,8},{5,9},{6,10},{7,11},{8,12},{9,13},{1... | collective-permute-start | bytes 798728 | tf_op jit(solution)/shard_map/ppermute | solution.py:694
  53.5 10.6 %collective-permute-start.20 = (bf16[16,8320]{1,0:T(8,128)(2,1)S(1)}, bf16[16,8320]{1,0:T(8,128)(2,1)S(1)}, u32[]{:S(2)}, u32[]{:S(2)}) collective-permute-start(bf16[16,8320]{1,0:T(8,128)(2,1)S(1)} %collective-permute-done.11.refs_5_), channel_id=1, source_target_pairs={{0,4},{1,5},{2,6},{3,7},{4,8},{5,9},{6,10},{7,11},{8,12},{9,13},{1... | collective-permute-start | bytes 798728 | tf_op jit(solution)/shard_map/ppermute | solution.py:694
  53.5 10.6 %collective-permute-start.28 = (bf16[16,8320]{1,0:T(8,128)(2,1)S(1)}, bf16[16,8320]{1,0:T(8,128)(2,1)S(1)}, u32[]{:S(2)}, u32[]{:S(2)}) collective-permute-start(bf16[16,8320]{1,0:T(8,128)(2,1)S(1)} %collective-permute-done.24.refs_0_), channel_id=1, source_target_pairs={{0,2},{1,3},{2,0},{3,1},{4,6},{5,7},{6,4},{7,5},{8,10},{9,11},{10,... | collective-permute-start | bytes 798728 | tf_op jit(solution)/shard_map/ppermute | solution.py:694
  73.5 11.7 %collective-permute-start.35 = (bf16[512,128]{1,0:T(8,128)(2,1)S(1)}, bf16[512,128]{1,0:T(8,128)(2,1)S(1)}, u32[]{:S(2)}, u32[]{:S(2)}) collective-permute-start(bf16[512,128]{1,0:T(8,128)(2,1)S(1)} %pair_pieces.1), channel_id=1, source_target_pairs={{0,2},{1,3},{2,6},{3,7},{4,10},{5,11},{6,14},{7,15},{8,0},{9,1},{1... | collective-permute-start | bytes 393224 | tf_op jit(solution)/shard_map/ppermute | solution.py:694
  102.0 15.3 %collective-permute-start.40 = (bf16[64,8192]{1,0:T(8,128)(2,1)}, bf16[64,8192]{1,0:T(8,128)(2,1)S(1)}, u32[]{:S(2)}, u32[]{:S(2)}) collective-permute-start(bf16[64,8192]{1,0:T(8,128)(2,1)} %get-tuple-element.210), channel_id=1, source_target_pairs={{0,1},{1,0},{2,3},{3,2},{4,5},{5,4},{6,7},{7,6},{8,9},{9,8},{10,11... | collective-permute-start | bytes 3145736 | tf_op jit(solution)/shard_map/ppermute | solution.py:694
  102.1 30.1 %collective-permute-start.36 = (bf16[64,8192]{1,0:T(8,128)(2,1)}, bf16[64,8192]{1,0:T(8,128)(2,1)S(1)}, u32[]{:S(2)}, u32[]{:S(2)}) collective-permute-start(bf16[64,8192]{1,0:T(8,128)(2,1)} %get-tuple-element.206), channel_id=1, source_target_pairs={{0,1},{1,0},{2,3},{3,2},{4,5},{5,4},{6,7},{7,6},{8,9},{9,8},{10,11... | collective-permute-start | bytes 3145736 | tf_op jit(solution)/shard_map/ppermute | solution.py:694
  116.5 14.2 %collective-permute-start.47 = (bf16[32,8192]{1,0:T(8,128)(2,1)S(1)}, bf16[32,8192]{1,0:T(8,128)(2,1)S(1)}, u32[]{:S(2)}, u32[]{:S(2)}) collective-permute-start(bf16[32,8192]{1,0:T(8,128)(2,1)S(1)} %fusion), channel_id=1, source_target_pairs={{0,4},{1,5},{2,6},{3,7},{4,8},{5,9},{6,10},{7,11},{8,12},{9,13},{1... | collective-permute-start | bytes 1572872 | tf_op jit(solution)/shard_map/ppermute | solution.py:694
  116.9 14.9 %collective-permute-start.46 = (bf16[32,8192]{1,0:T(8,128)(2,1)S(1)}, bf16[32,8192]{1,0:T(8,128)(2,1)S(1)}, u32[]{:S(2)}, u32[]{:S(2)}) collective-permute-start(bf16[32,8192]{1,0:T(8,128)(2,1)S(1)} %pad_maximum_fusion.1), channel_id=1, source_target_pairs={{0,2},{1,3},{2,0},{3,1},{4,6},{5,7},{6,4},{7,5},{8,10},{9,11},{10,... | collective-permute-start | bytes 1572872 | tf_op jit(solution)/shard_map/ppermute | solution.py:694
  117.4 25.6 %collective-permute-start.41 = (bf16[32,8192]{1,0:T(8,128)(2,1)S(1)}, bf16[32,8192]{1,0:T(8,128)(2,1)S(1)}, u32[]{:S(2)}, u32[]{:S(2)}) collective-permute-start(bf16[32,8192]{1,0:T(8,128)(2,1)S(1)} %multiply_convert_fusion), channel_id=1, source_target_pairs={{0,2},{1,3},{2,0},{3,1},{4,6},{5,7},{6,4},{7,5},{8,10},{9,11},{10,... | collective-permute-start | bytes 1572872 | tf_op jit(solution)/shard_map/ppermute | solution.py:694
  132.1 11.9 %collective-permute-start.48 = (bf16[32,8192]{1,0:T(8,128)(2,1)S(1)}, bf16[32,8192]{1,0:T(8,128)(2,1)S(1)}, u32[]{:S(2)}, u32[]{:S(2)}) collective-permute-start(bf16[32,8192]{1,0:T(8,128)(2,1)S(1)} %add_convert_fusion.2), channel_id=1, source_target_pairs={{0,4},{1,5},{2,6},{3,7},{4,8},{5,9},{6,10},{7,11},{8,12},{9,13},{1... | collective-permute-start | bytes 1572872 | tf_op jit(solution)/shard_map/ppermute | solution.py:694
  132.4 19.1 %collective-permute-start.39 = (bf16[32,8192]{1,0:T(8,128)(2,1)S(1)}, bf16[32,8192]{1,0:T(8,128)(2,1)S(1)}, u32[]{:S(2)}, u32[]{:S(2)}) collective-permute-start(bf16[32,8192]{1,0:T(8,128)(2,1)S(1)} %multiply_convert_fusion.1), channel_id=1, source_target_pairs={{0,2},{1,3},{2,0},{3,1},{4,6},{5,7},{6,4},{7,5},{8,10},{9,11},{10,... | collective-permute-start | bytes 1572872 | tf_op jit(solution)/shard_map/ppermute | solution.py:694
  144.3 11.0 %collective-permute-start.49 = (bf16[32,8192]{1,0:T(8,128)(2,1)S(1)}, bf16[32,8192]{1,0:T(8,128)(2,1)S(1)}, u32[]{:S(2)}, u32[]{:S(2)}) collective-permute-start(bf16[32,8192]{1,0:T(8,128)(2,1)S(1)} %add_convert_fusion.1), channel_id=1, source_target_pairs={{0,4},{1,5},{2,6},{3,7},{4,8},{5,9},{6,10},{7,11},{8,12},{9,13},{1... | collective-permute-start | bytes 1572872 | tf_op jit(solution)/shard_map/ppermute | solution.py:694
  (50 other events, 536.1 us)
